TPU v7x, 128 devices: a whole 4x4x4 slice. The times are simulated.
128 devices in a mesh: row: 16 (over z, y_hi, core), col: 8 (over y_lo, x).
Axes of the slice: x: 4, y: 4 (y_hi: 2, y_lo: 2; y = y_hi * 2 + y_lo), z: 4, core: 2. Of those that a mesh axis runs over, the one named last changes fastest.
Arguments:
- row_query: bfloat16 [512, 256, 768], P('row', 'col'), may hold values from -6 to 6
- row_key: bfloat16 [512, 256, 768], P('row', 'col'), may hold values from -6 to 6
- row_value: bfloat16 [512, 256, 768], P('row', 'col'), may hold values from -6 to 6
- row_out_grad: bfloat16 [512, 256, 768], P('row', 'col'), may hold values from -6 to 6
- col_query: bfloat16 [512, 256, 768], P('row', 'col'), may hold values from -6 to 6
- col_key: bfloat16 [512, 256, 768], P('row', 'col'), may hold values from -6 to 6
- col_value: bfloat16 [512, 256, 768], P('row', 'col'), may hold values from -6 to 6
- col_out_grad: bfloat16 [512, 256, 768], P('row', 'col'), may hold values from -6 to 6
Outputs:
- row_query_grad: bfloat16 [512, 256, 768], P('row', 'col')
- row_key_grad: bfloat16 [512, 256, 768], P('row', 'col')
- row_value_grad: bfloat16 [512, 256, 768], P('row', 'col')
- col_query_grad: bfloat16 [512, 256, 768], P('row', 'col')
- col_key_grad: bfloat16 [512, 256, 768], P('row', 'col')
- col_value_grad: bfloat16 [512, 256, 768], P('row', 'col')
All inputs are finite; a program needn't handle non-finite values.
Results may differ from a plain program's by a relative error of at most 0.0086.
Values may be sent and summed in bfloat16 or wider, within the bound.
No kernel may reach another device: no remote copies, remote signals or barrier semaphores. Data moves between devices by JAX's collectives and lax.ppermute only.
A program may use at most 128 MiB of HBM per device.

v0:
```python
import math

import jax
import jax.numpy as jnp
from jax import lax
from jax.sharding import PartitionSpec as P

H = 12
HD = 64


def attention_softmax(logits, dprobs, factor):
    weights = jax.nn.softmax(logits * factor, axis=-1)
    slopes = weights * (dprobs - jnp.sum(weights * dprobs, axis=-1, keepdims=True))
    return (weights, slopes)


def to_heads(tensor):
    return tensor.reshape(tensor.shape[0], tensor.shape[1], H, HD)


def column_backward(queries, key_rows, value_rows, grad_rows):
    total_rows, columns, features = queries.shape
    head_block = math.gcd(H, max(1, 128 // HD))
    span_width = head_block * HD
    factor = 1.0 / math.sqrt(HD)
    zeros_grad = jnp.zeros((total_rows, columns, features), jnp.bfloat16)

    def head_step(block_index, buffers):
        offset = block_index * span_width

        def take_block(tensor):
            return lax.dynamic_slice_in_dim(tensor, offset, span_width, 2).reshape(
                total_rows, columns, head_block, HD
            )

        query_block = take_block(queries)
        key_block = take_block(key_rows)
        value_block = take_block(value_rows)
        grad_block = take_block(grad_rows)
        logits = jnp.einsum(
            "rchd,schd->chrs", query_block, key_block, preferred_element_type=jnp.float32
        )
        dprobs = jnp.einsum(
            "rchd,schd->chrs", grad_block, value_block, preferred_element_type=jnp.float32
        )
        weights, slopes = attention_softmax(logits, dprobs, factor)
        weights_low = weights.astype(jnp.bfloat16)
        slopes_low = slopes.astype(jnp.bfloat16)
        query_grad = (
            factor
            * jnp.einsum(
                "chrs,schd->rchd", slopes_low, key_block, preferred_element_type=jnp.float32
            )
        ).astype(jnp.bfloat16)
        key_grad = (
            factor
            * jnp.einsum(
                "chrs,rchd->schd", slopes_low, query_block, preferred_element_type=jnp.float32
            )
        ).astype(jnp.bfloat16)
        value_grad = jnp.einsum(
            "chrs,rchd->schd", weights_low, grad_block, preferred_element_type=jnp.float32
        ).astype(jnp.bfloat16)
        updates = (query_grad, key_grad, value_grad)
        return tuple(
            (
                lax.dynamic_update_slice_in_dim(
                    buffer, update.reshape(total_rows, columns, span_width), offset, 2
                )
                for buffer, update in zip(buffers, updates)
            )
        )

    return lax.fori_loop(0, H // head_block, head_step, (zeros_grad, zeros_grad, zeros_grad))


def local(row_query, row_key, row_value, row_out_grad, col_query, col_key, col_value, col_out_grad):
    total_rows = row_query.shape[0] * lax.axis_size("row")
    row_factor = 1.0 / math.sqrt(HD * total_rows)
    query_rows, key_rows, value_rows, grad_rows = (
        lax.all_to_all(row_query, "col", split_axis=0, concat_axis=1, tiled=True),
        lax.all_to_all(row_key, "col", split_axis=0, concat_axis=1, tiled=True),
        lax.all_to_all(row_value, "col", split_axis=0, concat_axis=1, tiled=True),
        lax.all_to_all(row_out_grad, "col", split_axis=0, concat_axis=1, tiled=True),
    )
    local_rows, all_columns, features = query_rows.shape
    query_heads = to_heads(query_rows)
    key_heads = to_heads(key_rows)
    value_heads = to_heads(value_rows)
    grad_heads = to_heads(grad_rows)
    logit_terms = jnp.einsum(
        "rihd,rjhd->hij", query_heads, key_heads, preferred_element_type=jnp.float32
    )
    dprob_terms = jnp.einsum(
        "rihd,rjhd->hij", grad_heads, value_heads, preferred_element_type=jnp.float32
    )
    tied_logits, tied_dprobs = lax.psum((logit_terms, dprob_terms), ("row", "col"))
    tied_weights, tied_slopes = attention_softmax(tied_logits, tied_dprobs, row_factor)
    weights_low = tied_weights.astype(jnp.bfloat16)
    slopes_low = tied_slopes.astype(jnp.bfloat16)
    query_grad = (
        (
            row_factor
            * jnp.einsum(
                "hij,rjhd->rihd", slopes_low, key_heads, preferred_element_type=jnp.float32
            )
        )
        .astype(jnp.bfloat16)
        .reshape(local_rows, all_columns, features)
    )
    key_grad = (
        (
            row_factor
            * jnp.einsum(
                "hij,rihd->rjhd", slopes_low, query_heads, preferred_element_type=jnp.float32
            )
        )
        .astype(jnp.bfloat16)
        .reshape(local_rows, all_columns, features)
    )
    value_grad = (
        jnp.einsum("hij,rihd->rjhd", weights_low, grad_heads, preferred_element_type=jnp.float32)
        .astype(jnp.bfloat16)
        .reshape(local_rows, all_columns, features)
    )
    row_query_grad, row_key_grad, row_value_grad = (
        lax.all_to_all(query_grad, "col", split_axis=1, concat_axis=0, tiled=True),
        lax.all_to_all(key_grad, "col", split_axis=1, concat_axis=0, tiled=True),
        lax.all_to_all(value_grad, "col", split_axis=1, concat_axis=0, tiled=True),
    )
    groups = lax.axis_size("row")
    rows_here, columns_here, col_features = col_query.shape
    per_group = columns_here // groups

    def grouped(tensor):
        return tensor.reshape(rows_here, groups, per_group, col_features)

    def squeezed(tensor):
        return tensor.reshape(tensor.shape[0], tensor.shape[2], tensor.shape[3])

    def lifted(tensor):
        return tensor.reshape(tensor.shape[0], 1, tensor.shape[1], tensor.shape[2])

    query_part = lax.all_to_all(grouped(col_query), "row", split_axis=1, concat_axis=0, tiled=True)
    key_part = lax.all_to_all(grouped(col_key), "row", split_axis=1, concat_axis=0, tiled=True)
    value_part = lax.all_to_all(grouped(col_value), "row", split_axis=1, concat_axis=0, tiled=True)
    grad_part = lax.all_to_all(
        grouped(col_out_grad), "row", split_axis=1, concat_axis=0, tiled=True
    )
    column_grads = column_backward(
        squeezed(query_part), squeezed(key_part), squeezed(value_part), squeezed(grad_part)
    )
    return (
        row_query_grad,
        row_key_grad,
        row_value_grad,
        lax.all_to_all(
            lifted(column_grads[0]), "row", split_axis=0, concat_axis=1, tiled=True
        ).reshape(rows_here, columns_here, col_features),
        lax.all_to_all(
            lifted(column_grads[1]), "row", split_axis=0, concat_axis=1, tiled=True
        ).reshape(rows_here, columns_here, col_features),
        lax.all_to_all(
            lifted(column_grads[2]), "row", split_axis=0, concat_axis=1, tiled=True
        ).reshape(rows_here, columns_here, col_features),
    )


def solution(mesh):
    return jax.shard_map(
        local,
        mesh=mesh,
        in_specs=(
            P("row", "col", None),
            P("row", "col", None),
            P("row", "col", None),
            P("row", "col", None),
            P("row", "col", None),
            P("row", "col", None),
            P("row", "col", None),
            P("row", "col", None),
        ),
        out_specs=(
            P("row", "col", None),
            P("row", "col", None),
            P("row", "col", None),
            P("row", "col", None),
            P("row", "col", None),
            P("row", "col", None),
        ),
        check_vma=False,
    )
```

profile of v0, /device:TPU:1, one launch (start us, length us, event | category | flops | bytes accessed | tf_op | source)
XLA Modules:
  0.0 560.9 jit_solution(141624587668551745)
XLA Ops:
  7.2 26.5 %all_to_all.219 = bf16[32,32,768]{2,1,0:T(8,128)(2,1)} all-to-all(bf16[32,32,768]{2,1,0:T(8,128)(2,1)} %param.10), channel_id=1, replica_groups=mesh['row'=16,'col'=8] {'col'}, dimensions={0} | all-to-all | bytes 3145728 | tf_op jit(solution)/shard_map/all_to_all | solution.py:82
  33.7 23.3 %all_to_all.220 = bf16[32,32,768]{2,1,0:T(8,128)(2,1)} all-to-all(bf16[32,32,768]{2,1,0:T(8,128)(2,1)S(1)} %copy-done.21), channel_id=1, replica_groups=mesh['row'=16,'col'=8] {'col'}, dimensions={0} | all-to-all | bytes 3145728 | tf_op jit(solution)/shard_map/all_to_all | solution.py:83
  57.1 22.2 %all_to_all.221 = bf16[32,32,768]{2,1,0:T(8,128)(2,1)} all-to-all(bf16[32,32,768]{2,1,0:T(8,128)(2,1)S(1)} %copy-done.22), channel_id=1, replica_groups=mesh['row'=16,'col'=8] {'col'}, dimensions={0} | all-to-all | bytes 3145728 | tf_op jit(solution)/shard_map/all_to_all | solution.py:85
  79.3 3.7 all-to-all-start.3
  85.0 19.3 %all-to-all-done.3 = bf16[32,32,768]{2,1,0:T(8,128)(2,1)S(1)} async-done(((bf16[32,32,768]{2,1,0:T(8,128)(2,1)}), bf16[32,32,768]{2,1,0:T(8,128)(2,1)S(1)}, u32[]{:S(2)}, u32[]{:S(2)}) %all-to-all-start.3) | async-done | bytes 1572896 | tf_op jit(solution)/shard_map/all_to_all | solution.py:84
  105.5 8.5 %all-to-all-start.7 = ((bf16[32,16,2,768]{3,0,2,1:T(8,128)(2,1)}), bf16[32,16,2,768]{3,0,2,1:T(8,128)(2,1)S(1)}, u32[]{:S(2)}, u32[]{:S(2)}) async-start(bf16[32,16,2,768]{3,0,2,1:T(8,128)(2,1)} %bitcast.46), calls=%async_computation.7 | async-start | bytes 3145728 | tf_op jit(solution)/shard_map/all_to_all | solution.py:146
  116.0 20.8 %all-to-all-done.7 = bf16[32,16,2,768]{3,0,2,1:T(8,128)(2,1)S(1)} async-done(((bf16[32,16,2,768]{3,0,2,1:T(8,128)(2,1)}), bf16[32,16,2,768]{3,0,2,1:T(8,128)(2,1)S(1)}, u32[]{:S(2)}, u32[]{:S(2)}) %all-to-all-start.7) | async-done | bytes 1572896 | tf_op jit(solution)/shard_map/all_to_all | solution.py:146
  138.0 4.4 all-to-all-start.8
  142.5 3.4 copy.125
  145.9 19.5 %all-to-all-done.8 = bf16[32,16,2,768]{3,0,2,1:T(8,128)(2,1)S(1)} async-done(((bf16[32,16,2,768]{3,0,2,1:T(8,128)(2,1)}), bf16[32,16,2,768]{3,0,2,1:T(8,128)(2,1)S(1)}, u32[]{:S(2)}, u32[]{:S(2)}) %all-to-all-start.8) | async-done | bytes 1572896 | tf_op jit(solution)/shard_map/all_to_all | solution.py:145
  166.6 4.4 all-to-all-start.9
  171.0 3.4 copy.127
  174.4 19.5 %all-to-all-done.9 = bf16[32,16,2,768]{3,0,2,1:T(8,128)(2,1)S(1)} async-done(((bf16[32,16,2,768]{3,0,2,1:T(8,128)(2,1)}), bf16[32,16,2,768]{3,0,2,1:T(8,128)(2,1)S(1)}, u32[]{:S(2)}, u32[]{:S(2)}) %all-to-all-start.9) | async-done | bytes 1572896 | tf_op jit(solution)/shard_map/all_to_all | solution.py:148
  195.1 5.1 all-to-all-start.10
  200.8 3.8 reshape.141
  204.7 4.5 copy.100
  210.6 5.9 %reshape.142 = bf16[4,256,12,64]{3,2,1,0:T(8,128)(2,1)} reshape(bf16[4,8,32,768]{3,2,1,0:T(8,128)(2,1)} %bitcast.200) | data formatting | bytes 3145728 | tf_op jit(solution)/shard_map/reshape | solution.py:19
  216.5 4.4 copy.101
  220.8 3.2 copy.169
  224.1 5.9 %reshape.143 = bf16[4,256,12,64]{3,2,1,0:T(8,128)(2,1)} reshape(bf16[4,8,32,768]{3,2,1,0:T(8,128)(2,1)} %bitcast.201) | data formatting | bytes 3145728 | tf_op jit(solution)/shard_map/reshape | solution.py:19
  230.0 5.3 copy.104
  238.0 5.9 %reshape.144 = bf16[4,256,12,64]{3,2,1,0:T(8,128)(2,1)} reshape(bf16[4,8,32,768]{3,2,1,0:T(8,128)(2,1)} %bitcast.202) | data formatting | bytes 3145728 | tf_op jit(solution)/shard_map/reshape | solution.py:19
  247.7 3.4 fusion.21
  257.8 3.1 copy.128
  266.8 116.9 %while.17 = (s32[]{:T(128)}, bf16[512,2,768]{2,1,0:T(2,128)(2,1)}, bf16[512,2,768]{2,1,0:T(2,128)(2,1)}, bf16[512,2,768]{2,1,0:T(2,128)(2,1)}, bf16[512,2,768]{2...) while((s32[]{:T(128)}, bf16[512,2,768]{2,1,0:T(2,128)(2,1)}, ...), condition=%wide.region_9.0_spmd, body=%wide.region_5.0_spmd.sunk | while | flops 684325376 | bytes 58245336 | solution.py:75
  269.2 3.5 fusion.81
  275.0 3.2 multiply_reduce_fusion.5
  288.9 3.5 fusion.81
  308.3 3.5 fusion.81
  314.0 3.1 multiply_reduce_fusion.5
  327.6 3.5 fusion.81
  333.4 3.1 multiply_reduce_fusion.5
  347.1 3.5 fusion.81
  352.8 3.1 multiply_reduce_fusion.5
  366.5 3.5 fusion.81
  383.7 34.3 %all_to_all.222 = bf16[512,1,2,768]{3,2,1,0:T(2,128)(2,1)} all-to-all(bf16[512,1,2,768]{3,2,1,0:T(2,128)(2,1)} %bitcast.185), channel_id=1, replica_groups=mesh['row'=16,'col'=8] {'row'}, dimensions={0} | all-to-all | bytes 3145728 | tf_op jit(solution)/shard_map/all_to_all | solution.py:158
  418.0 5.0 all-to-all-start.12
  423.1 3.9 fusion.35
  427.0 19.1 %all-to-all-done.12 = bf16[512,1,2,768]{3,2,1,0:T(2,128)(2,1)} async-done(((bf16[512,1,2,768]{3,2,1,0:T(2,128)(2,1)}), bf16[512,1,2,768]{3,2,1,0:T(2,128)(2,1)}, u32[]{:S(2)}, u32[]{:S(2)}) %all-to-all-start.12) | async-done | bytes 1572896 | tf_op jit(solution)/shard_map/all_to_all | solution.py:161
  446.1 5.1 all-to-all-start.13
  458.9 15.3 %all-to-all-done.13 = bf16[512,1,2,768]{3,2,1,0:T(2,128)(2,1)} async-done(((bf16[512,1,2,768]{3,2,1,0:T(2,128)(2,1)}), bf16[512,1,2,768]{3,2,1,0:T(2,128)(2,1)}, u32[]{:S(2)}, u32[]{:S(2)}) %all-to-all-start.13) | async-done | bytes 1572896 | tf_op jit(solution)/shard_map/all_to_all | solution.py:164
  474.2 4.3 all-to-all-start.5
  481.9 18.1 %all-to-all-done.5 = bf16[4,256,768]{2,0,1:T(4,128)(2,1)} async-done(((bf16[4,256,768]{2,0,1:T(4,128)(2,1)}), bf16[4,256,768]{2,0,1:T(4,128)(2,1)}, u32[]{:S(2)}, u32[]{:S(2)}) %all-to-all-start.5) | async-done | bytes 1572896 | tf_op jit(solution)/shard_map/all_to_all | solution.py:129
  499.9 3.8 all-to-all-start.4
  503.8 10.0 %fusion.26 = f32[12,256,256]{1,2,0} fusion(bf16[12,256,256]{1,2,0:T(8,128)(2,1)S(1)} %bitcast.203, f32[12,256]{1,0:T(8,128)S(1)} %get-tuple-element.210, f32[12,256,256]{2,1,0:T(8,128)} %get-tuple-element.203), kind=kOutput, calls=%fused_computation.43 | convolution fusion | flops 406588672 | bytes 7876608
  518.2 6.9 %all-to-all-done.4 = bf16[4,256,768]{2,0,1:T(4,128)(2,1)S(1)} async-done(((bf16[4,256,768]{2,0,1:T(4,128)(2,1)}), bf16[4,256,768]{2,0,1:T(4,128)(2,1)S(1)}, u32[]{:S(2)}, u32[]{:S(2)}) %all-to-all-start.4) | async-done | bytes 1572896 | tf_op jit(solution)/shard_map/all_to_all | solution.py:128
  525.2 4.3 all-to-all-start.6
  543.7 7.3 %all-to-all-done.6 = bf16[4,256,768]{2,0,1:T(4,128)(2,1)} async-done(((bf16[4,256,768]{2,0,1:T(4,128)(2,1)}), bf16[4,256,768]{2,0,1:T(4,128)(2,1)}, u32[]{:S(2)}, u32[]{:S(2)}) %all-to-all-start.6) | async-done | bytes 1572896 | tf_op jit(solution)/shard_map/all_to_all | solution.py:130
  (208 shorter events, 144.9 us)
Async XLA Ops:
  7.2 26.6 %copy-start.21 = (bf16[32,32,768]{2,1,0:T(8,128)(2,1)S(1)}, bf16[32,32,768]{2,1,0:T(8,128)(2,1)}, u32[]{:S(2)}) copy-start(bf16[32,32,768]{2,1,0:T(8,128)(2,1)} %param.11) | copy-start | bytes 4718596
  33.7 23.3 %copy-start.22 = (bf16[32,32,768]{2,1,0:T(8,128)(2,1)S(1)}, bf16[32,32,768]{2,1,0:T(8,128)(2,1)}, u32[]{:S(2)}) copy-start(bf16[32,32,768]{2,1,0:T(8,128)(2,1)} %param.13) | copy-start | bytes 4718596
  79.3 3.7 copy-start.23
  79.3 25.1 %all-to-all-start.3 = ((bf16[32,32,768]{2,1,0:T(8,128)(2,1)}), bf16[32,32,768]{2,1,0:T(8,128)(2,1)S(1)}, u32[]{:S(2)}, u32[]{:S(2)}) async-start(bf16[32,32,768]{2,1,0:T(8,128)(2,1)} %param.12), calls=%async_computation.3 | async-start | bytes 3145728 | tf_op jit(solution)/shard_map/all_to_all | solution.py:84
  104.4 1.1 copy-start.12
  104.4 9.7 %copy-start.24 = (bf16[32,32,768]{2,1,0:T(8,128)(2,1)S(1)}, bf16[32,32,768]{2,1,0:T(8,128)(2,1)}, u32[]{:S(2)}) copy-start(bf16[32,32,768]{2,1,0:T(8,128)(2,1)} %param.14) | copy-start | bytes 4718596
  105.5 31.4 %all-to-all-start.7 = ((bf16[32,16,2,768]{3,0,2,1:T(8,128)(2,1)}), bf16[32,16,2,768]{3,0,2,1:T(8,128)(2,1)S(1)}, u32[]{:S(2)}, u32[]{:S(2)}) async-start(bf16[32,16,2,768]{3,0,2,1:T(8,128)(2,1)} %bitcast.46), calls=%async_computation.7 | async-start | bytes 3145728 | tf_op jit(solution)/shard_map/all_to_all | solution.py:146
  136.9 1.1 copy-start.10
  138.0 27.4 %all-to-all-start.8 = ((bf16[32,16,2,768]{3,0,2,1:T(8,128)(2,1)}), bf16[32,16,2,768]{3,0,2,1:T(8,128)(2,1)S(1)}, u32[]{:S(2)}, u32[]{:S(2)}) async-start(bf16[32,16,2,768]{3,0,2,1:T(8,128)(2,1)} %bitcast.183), calls=%async_computation.8 | async-start | bytes 3145728 | tf_op jit(solution)/shard_map/all_to_all | solution.py:145
  165.4 1.2 copy-start.13
  166.6 27.4 %all-to-all-start.9 = ((bf16[32,16,2,768]{3,0,2,1:T(8,128)(2,1)}), bf16[32,16,2,768]{3,0,2,1:T(8,128)(2,1)S(1)}, u32[]{:S(2)}, u32[]{:S(2)}) async-start(bf16[32,16,2,768]{3,0,2,1:T(8,128)(2,1)} %bitcast.184), calls=%async_computation.9 | async-start | bytes 3145728 | tf_op jit(solution)/shard_map/all_to_all | solution.py:148
  193.9 1.2 copy-start.16
  193.9 6.8 %copy-start.18 = (bf16[32,32,768]{2,1,0:T(8,128)(2,1)S(1)}, bf16[32,32,768]{2,1,0:T(8,128)(2,1)}, u32[]{:S(2)}) copy-start(bf16[32,32,768]{2,1,0:T(8,128)(2,1)} %all_to_all.219) | copy-start | bytes 4718596
  195.1 62.7 %all-to-all-start.10 = ((bf16[32,16,2,768]{3,0,2,1:T(8,128)(2,1)}), bf16[32,16,2,768]{3,0,2,1:T(8,128)(2,1)}, u32[]{:S(2)}, u32[]{:S(2)}) async-start(bf16[32,16,2,768]{3,0,2,1:T(8,128)(2,1)} %bitcast.58), calls=%async_computation.10 | async-start | bytes 3145728 | tf_op jit(solution)/shard_map/all_to_all | solution.py:147
  200.2 222.8 %all-reduce.3.cloned.1.call-start = ((), (), s32[]{:S(2)}) async-start(), calls=%async_computation.14 | async-start | bytes 12582912 | tf_op jit(solution)/shard_map/psum | solution.py:98
  204.7 4.5 copy-start.15
  209.2 34.7 %copy-start.3 = (bf16[4,256,12,64]{1,3,0,2:T(8,128)(2,1)}, bf16[4,256,12,64]{1,3,0,2:T(8,128)(2,1)S(1)}, u32[]{:S(2)}) copy-start(bf16[4,256,12,64]{1,3,0,2:T(8,128)(2,1)S(1)} %copy.100) | copy-start | bytes 4718596
  220.8 23.1 %copy-start.1 = (bf16[4,256,12,64]{1,3,0,2:T(8,128)(2,1)}, bf16[4,256,12,64]{1,3,0,2:T(8,128)(2,1)S(1)}, u32[]{:S(2)}) copy-start(bf16[4,256,12,64]{1,3,0,2:T(8,128)(2,1)S(1)} %copy.101) | copy-start | bytes 4718596
  243.9 3.3 copy-start.7
  243.9 3.8 copy-start.19
  251.1 1.4 copy-start.11
  252.5 2.0 copy-start.14
  254.5 2.0 copy-start.17
  275.0 3.7 copy-start
  294.6 3.5 copy-start
  314.0 3.5 copy-start
  333.4 3.5 copy-start
  352.8 3.5 copy-start
  372.2 3.5 copy-start
  418.0 28.1 %all-to-all-start.12 = ((bf16[512,1,2,768]{3,2,1,0:T(2,128)(2,1)}), bf16[512,1,2,768]{3,2,1,0:T(2,128)(2,1)}, u32[]{:S(2)}, u32[]{:S(2)}) async-start(bf16[512,1,2,768]{3,2,1,0:T(2,128)(2,1)} %bitcast.66), calls=%async_computation.12 | async-start | bytes 3145728 | tf_op jit(solution)/shard_map/all_to_all | solution.py:161
  446.1 28.1 %all-to-all-start.13 = ((bf16[512,1,2,768]{3,2,1,0:T(2,128)(2,1)}), bf16[512,1,2,768]{3,2,1,0:T(2,128)(2,1)}, u32[]{:S(2)}, u32[]{:S(2)}) async-start(bf16[512,1,2,768]{3,2,1,0:T(2,128)(2,1)} %bitcast.186), calls=%async_computation.13 | async-start | bytes 3145728 | tf_op jit(solution)/shard_map/all_to_all | solution.py:164
  451.1 2.8 copy-start.8
  454.0 1.4 copy-start.4
  455.0 1.1 copy-start.5
  458.9 19.6 %copy-start.2 = (bf16[4,256,12,64]{1,3,0,2:T(8,128)(2,1)S(1)}, bf16[4,256,12,64]{1,3,0,2:T(8,128)(2,1)}, u32[]{:S(2)}) copy-start(bf16[4,256,12,64]{1,3,0,2:T(8,128)(2,1)} %copy-done.1) | copy-start | bytes 4718596
  458.9 19.6 %copy-start.6 = (bf16[12,256,256]{2,1,0:T(8,128)(2,1)S(1)}, bf16[12,256,256]{2,1,0:T(8,128)(2,1)}, u32[]{:S(2)}) copy-start(bf16[12,256,256]{2,1,0:T(8,128)(2,1)} %copy-done.5) | copy-start | bytes 4718596
  474.2 25.8 %all-to-all-start.5 = ((bf16[4,256,768]{2,0,1:T(4,128)(2,1)}), bf16[4,256,768]{2,0,1:T(4,128)(2,1)}, u32[]{:S(2)}, u32[]{:S(2)}) async-start(bf16[4,256,768]{2,0,1:T(4,128)(2,1)} %copy.113), calls=%async_computation.5 | async-start | bytes 3145728 | tf_op jit(solution)/shard_map/all_to_all | solution.py:129
  481.9 21.9 %copy-start.20 = (bf16[4,256,12,64]{1,3,0,2:T(8,128)(2,1)S(1)}, bf16[4,256,12,64]{1,3,0,2:T(8,128)(2,1)}, u32[]{:S(2)}) copy-start(bf16[4,256,12,64]{1,3,0,2:T(8,128)(2,1)} %copy.104) | copy-start | bytes 4718596
  499.9 25.2 %all-to-all-start.4 = ((bf16[4,256,768]{2,0,1:T(4,128)(2,1)}), bf16[4,256,768]{2,0,1:T(4,128)(2,1)S(1)}, u32[]{:S(2)}, u32[]{:S(2)}) async-start(bf16[4,256,768]{2,0,1:T(4,128)(2,1)} %copy.108), calls=%async_computation.4 | async-start | bytes 3145728 | tf_op jit(solution)/shard_map/all_to_all | solution.py:128
  518.2 11.3 %copy-start.9 = (bf16[512,1,2,768]{3,2,1,0:T(2,128)(2,1)S(1)}, bf16[512,1,2,768]{3,2,1,0:T(2,128)(2,1)}, u32[]{:S(2)}) copy-start(bf16[512,1,2,768]{3,2,1,0:T(2,128)(2,1)} %all_to_all.222) | copy-start | bytes 4718596
  525.2 25.8 %all-to-all-start.6 = ((bf16[4,256,768]{2,0,1:T(4,128)(2,1)}), bf16[4,256,768]{2,0,1:T(4,128)(2,1)}, u32[]{:S(2)}, u32[]{:S(2)}) async-start(bf16[4,256,768]{2,0,1:T(4,128)(2,1)} %copy.118), calls=%async_computation.6 | async-start | bytes 3145728 | tf_op jit(solution)/shard_map/all_to_all | solution.py:130
Sparse Core Ops, SparseCore 0:
  251.3 169.6 all-reduce.2
where the time goes:
time: 568 us; the launch traced here: 561 us
  waiting for transfers between devices  146 us (26%)
  local copies, waits for them, and re-layouts  145 us (26%)
  blocking collectives  106 us (19%)
  matrix products  81.9 us (14%)
  starting transfers between devices  49.1 us (9%)
  other arithmetic  17.6 us (3%)
  between operations  14.6 us (3%)
    reshape x7, local copies, waits for them, and re-layouts, to_heads(): return tensor.reshape(tensor.shape[0], tensor.shape[1], H, HD)  35.7 us
    all_to_all x1, blocking collectives, local(): lax.all_to_all(lifted(column_grads[0]), 'row', split_axis=0, concat_axis=...  34.3 us
    dynamic_slice x48, local copies, waits for them, and re-layouts, take_block(): lax.dynamic_slice_in_dim(tensor, offset, span_width, 2)  26.8 us
    unnamed x55, local copies, waits for them, and re-layouts  26.6 us
    all_to_all x1, blocking collectives, local(): lax.all_to_all(row_query, 'col', split_axis=0, concat_axis=1, tiled=True)  26.5 us
    all_to_all x1, blocking collectives, local(): lax.all_to_all(row_key, 'col', split_axis=0, concat_axis=1, tiled=True)  23.3 us
    all_to_all x1, blocking collectives, local(): lax.all_to_all(row_out_grad, 'col', split_axis=0, concat_axis=1, tiled=True)  22.2 us
    sub x6, matrix products, attention_softmax(): weights = jax.nn.softmax(logits * factor, axis=-1)  20.9 us
  transfers between devices with their start and end apart: 11, of which 9 were waited for; matrix products, arithmetic and copies ran while one was open for 41% of the time, Pallas kernels for 0%

commit v1 on v0

v1 whole, which is shorter than its diff:
```python
import functools
import math

import jax
import jax.numpy as jnp
from jax import lax
from jax.experimental import pallas as pl
from jax.experimental.pallas import tpu as pltpu
from jax.sharding import Mesh
from jax.sharding import PartitionSpec as P

H = 12
HD = 64
PAIR = 2 * HD
LOG2E = 1.4426950408889634
ROWS = ("z", "yh", "core")
VMEM = 48 * 1024 * 1024


def params():
    return pltpu.CompilerParams(vmem_limit_bytes=VMEM)


def nt(a, b):
    return lax.dot_general(a, b, (((1,), (1,)), ((), ())), preferred_element_type=jnp.float32)


def nn(a, b):
    return lax.dot_general(a, b, (((1,), (0,)), ((), ())), preferred_element_type=jnp.float32)


def column_kernel(x_ref, o_ref, *, chunk):
    groups, _, rows, width = x_ref.shape
    total = groups * rows
    query, key, value, grad = (x_ref[:, i].reshape(total, width) for i in range(4))
    low = lax.broadcasted_iota(jnp.int32, (total, width), 1) < HD
    zero = jnp.zeros_like(key)
    key_t = key.T
    scale = 1.0 / math.sqrt(HD)
    key_grads, value_grads, query_grads = [], [], []
    for head in range(2):
        keep = low if head == 0 else jnp.logical_not(low)
        key_h = jnp.where(keep, key, zero)
        value_h = jnp.where(keep, value, zero)
        key_th = key_t[head * HD : (head + 1) * HD]
        key_grad, value_grad, parts = None, None, []
        for at in range(0, total, chunk):
            query_c, grad_c = query[at : at + chunk], grad[at : at + chunk]
            logits = nt(key_h, query_c)
            dprobs = nt(value_h, grad_c)
            top = jnp.max(logits, axis=0, keepdims=True)
            probs = jnp.exp2((logits - top) * (scale * LOG2E))
            probs = probs * (1.0 / jnp.sum(probs, axis=0, keepdims=True))
            slopes = probs * (dprobs - jnp.sum(probs * dprobs, axis=0, keepdims=True))
            weights = probs.astype(jnp.bfloat16)
            slopes = slopes.astype(jnp.bfloat16)
            more_key, more_value = nn(slopes, query_c), nn(weights, grad_c)
            key_grad = more_key if key_grad is None else key_grad + more_key
            value_grad = more_value if value_grad is None else value_grad + more_value
            parts.append(nn(key_th, slopes))
        key_grads.append(key_grad)
        value_grads.append(value_grad)
        query_grads.append(jnp.concatenate(parts, axis=1))
    query_grad = jnp.concatenate(query_grads, axis=0).T * scale
    key_grad = jnp.where(low, key_grads[0], key_grads[1]) * scale
    value_grad = jnp.where(low, value_grads[0], value_grads[1])
    for i, grad in enumerate((query_grad, key_grad, value_grad)):
        o_ref[:, i] = grad.astype(jnp.bfloat16).reshape(groups, rows, width)


def column_backward(x, chunk=256):
    groups, _, rows, features = x.shape
    pairs = features // PAIR
    total = groups * rows
    return pl.pallas_call(
        functools.partial(column_kernel, chunk=chunk),
        grid=(pairs,),
        in_specs=[pl.BlockSpec((groups, 4, rows, PAIR), lambda i: (0, 0, 0, i))],
        out_specs=pl.BlockSpec((groups, 3, rows, PAIR), lambda i: (0, 0, 0, i)),
        out_shape=jax.ShapeDtypeStruct((groups, 3, rows, features), jnp.bfloat16),
        compiler_params=params(),
        cost_estimate=pl.CostEstimate(
            flops=20 * pairs * total * total * PAIR,
            bytes_accessed=14 * total * features,
            transcendentals=2 * pairs * total * total,
        ),
        name="column_attention",
    )(x)


def pack_kernel(*refs):
    ins, o_ref = refs[:-1], refs[-1]
    for i, ref in enumerate(ins):
        for r in range(0, ref.shape[0], 2):
            first, second = ref[r], ref[r + 1]
            lanes = slice(r * HD, r * HD + PAIR)
            o_ref[0, i, :, lanes] = jnp.concatenate([first[:, :HD], second[:, :HD]], axis=1)
            o_ref[1, i, :, lanes] = jnp.concatenate([first[:, HD:], second[:, HD:]], axis=1)


def pack_rows(*arrays):
    rows, columns, features = arrays[0].shape
    n = len(arrays)
    return pl.pallas_call(
        pack_kernel,
        grid=(features // PAIR,),
        in_specs=[pl.BlockSpec((rows, columns, PAIR), lambda i: (0, 0, i))] * n,
        out_specs=pl.BlockSpec((2, n, columns, rows * HD), lambda i: (i, 0, 0, 0)),
        out_shape=jax.ShapeDtypeStruct((features // HD, n, columns, rows * HD), jnp.bfloat16),
        compiler_params=params(),
        cost_estimate=pl.CostEstimate(
            flops=0, bytes_accessed=4 * n * rows * columns * features, transcendentals=0
        ),
        name="pack_rows",
    )(*arrays)


def unpack_kernel(x_ref, *o_refs):
    for i, ref in enumerate(o_refs):
        for r in range(0, ref.shape[0], 2):
            lanes = slice(r * HD, r * HD + PAIR)
            first, second = x_ref[0, i, :, lanes], x_ref[1, i, :, lanes]
            ref[r] = jnp.concatenate([first[:, :HD], second[:, :HD]], axis=1)
            ref[r + 1] = jnp.concatenate([first[:, HD:], second[:, HD:]], axis=1)


def unpack_rows(x):
    heads, n, columns, width = x.shape
    rows, features = width // HD, heads * HD
    return pl.pallas_call(
        unpack_kernel,
        grid=(heads // 2,),
        in_specs=[pl.BlockSpec((2, n, columns, width), lambda i: (i, 0, 0, 0))],
        out_specs=[pl.BlockSpec((rows, columns, PAIR), lambda i: (0, 0, i))] * n,
        out_shape=[jax.ShapeDtypeStruct((rows, columns, features), jnp.bfloat16)] * n,
        compiler_params=params(),
        cost_estimate=pl.CostEstimate(
            flops=0, bytes_accessed=4 * n * rows * columns * features, transcendentals=0
        ),
        name="unpack_rows",
    )(x)


def joined(refs, i):
    return jnp.concatenate([ref[0, i] for ref in refs], axis=0)


def logits_kernel(*refs, parts, slices):
    own, other, keys, o_ref = (
        refs[:parts],
        refs[parts : 2 * parts],
        refs[2 * parts : 3 * parts],
        refs[-1],
    )
    for i in range(2):
        right = joined(keys, i)
        for side, left in enumerate((own, other)):
            terms = nt(joined(left, i), right)
            o_ref[:, i, 0, side] = terms.reshape(slices, terms.shape[0] // slices, -1)


def tied_terms(own, other, keys, slices):
    parts = len(own)
    heads, _, columns, width = own[0].shape
    wide = parts * columns
    step = wide // slices
    return pl.pallas_call(
        functools.partial(logits_kernel, parts=parts, slices=slices),
        grid=(heads,),
        in_specs=[pl.BlockSpec((1, 2, columns, width), lambda i: (i, 0, 0, 0))] * (3 * parts),
        out_specs=pl.BlockSpec((slices, 2, 1, 2, step, wide), lambda i: (0, 0, i, 0, 0, 0)),
        out_shape=jax.ShapeDtypeStruct((slices, 2, heads, 2, step, wide), jnp.float32),
        compiler_params=params(),
        cost_estimate=pl.CostEstimate(
            flops=8 * heads * wide * wide * width,
            bytes_accessed=12 * heads * wide * width,
            transcendentals=0,
        ),
        name="tied_terms",
    )(*own, *other, *keys)


def grads_kernel(*refs, parts, factor):
    own, other, keys, other_keys = (refs[i * parts : (i + 1) * parts] for i in range(4))
    s_query, s_key, w_value, o_ref = refs[4 * parts :]
    results = (
        nn(s_query[0], jnp.concatenate([joined(keys, 0), joined(other_keys, 0)], axis=0)) * factor,
        nn(s_key[0], jnp.concatenate([joined(own, 0), joined(other, 0)], axis=0)) * factor,
        nn(w_value[0], jnp.concatenate([joined(own, 1), joined(other, 1)], axis=0)),
    )
    for i, result in enumerate(results):
        o_ref[:, 0, i] = result.astype(jnp.bfloat16).reshape(parts, -1, result.shape[1])


def tied_grads(own, other, keys, other_keys, s_query, s_key, w_value, factor):
    parts = len(own)
    heads, _, columns, width = own[0].shape
    wide = parts * columns
    two = pl.BlockSpec((1, 2, columns, width), lambda i: (i, 0, 0, 0))
    one = pl.BlockSpec((1, 1, columns, width), lambda i: (i, 0, 0, 0))
    square = pl.BlockSpec((1, wide, 2 * wide), lambda i: (i, 0, 0))
    return pl.pallas_call(
        functools.partial(grads_kernel, parts=parts, factor=factor),
        grid=(heads,),
        in_specs=[two] * (2 * parts) + [one] * (2 * parts) + [square] * 3,
        out_specs=pl.BlockSpec((parts, 1, 3, columns, width), lambda i: (0, i, 0, 0, 0)),
        out_shape=jax.ShapeDtypeStruct((parts, heads, 3, columns, width), jnp.bfloat16),
        compiler_params=params(),
        cost_estimate=pl.CostEstimate(
            flops=12 * heads * wide * wide * width,
            bytes_accessed=18 * heads * wide * width,
            transcendentals=0,
        ),
        name="tied_grads",
    )(*own, *other, *keys, *other_keys, s_query, s_key, w_value)


def shift(x, axis, by):
    n = lax.axis_size(axis)
    return lax.ppermute(x, axis, [(i, (i + by) % n) for i in range(n)])


def over_rows(x):
    return lax.all_to_all(x, ROWS, split_axis=0, concat_axis=0, tiled=True)


def column_in(arrays, piece, groups):
    stacked = jnp.stack([a[:, piece * groups : (piece + 1) * groups] for a in arrays])
    return over_rows(jnp.transpose(stacked, (2, 0, 1, 3)))


def local(row_query, row_key, row_value, row_out_grad, col_query, col_key, col_value, col_out_grad):
    groups = 1
    for axis in ROWS:
        groups *= lax.axis_size(axis)
    parts = lax.axis_size("x")
    here = lax.axis_index("x")
    rows, columns, features = row_query.shape
    row_factor = 1.0 / math.sqrt(HD * rows * groups)
    head_group = H // parts
    pieces = columns // groups

    def spread(packed):
        mine = [
            lax.dynamic_slice_in_dim(packed, head_group * ((here + s) % parts), head_group, 0)
            for s in range(parts)
        ]
        return [mine[0]] + [shift(mine[s], "x", s) for s in range(1, parts)]

    col_arrays = (col_query, col_key, col_value, col_out_grad)
    col_parts = [column_in(col_arrays, p, groups) for p in range(pieces)]

    own = spread(pack_rows(row_query, row_out_grad))
    other = [shift(c, "yl", 1) for c in own]
    keys = spread(pack_rows(row_key, row_value))
    other_keys = [shift(c[:, :1], "yl", 1) for c in keys]

    terms = over_rows(tied_terms(own, other, keys, groups))
    sums = jnp.sum(terms, axis=0)
    across = shift(sums[:, :, 1], "yl", 1)
    logits, dprobs = jnp.concatenate([sums[:, :, 0], across], axis=-1)
    probs = jax.nn.softmax(logits * row_factor, axis=-1)
    slopes = probs * (dprobs - jnp.sum(probs * dprobs, axis=-1, keepdims=True))
    both = jnp.stack([slopes, probs]).astype(jnp.bfloat16)
    wide = both.shape[-1] // 2
    crossed = shift(both[..., wide:], "yl", 1)
    payload = jnp.concatenate([both[..., :wide], both[:1, ..., wide:], crossed], axis=0)
    whole = over_rows(jnp.broadcast_to(payload[None], (groups,) + payload.shape))
    whole = jnp.transpose(whole, (1, 2, 0, 3, 4)).reshape(5, head_group, wide, wide)
    s_own, w_own, s_right, s_below, w_below = whole
    s_query = jnp.concatenate([s_own, s_right], axis=-1)
    s_key = jnp.swapaxes(jnp.concatenate([s_own, s_below], axis=1), 1, 2)
    w_value = jnp.swapaxes(jnp.concatenate([w_own, w_below], axis=1), 1, 2)

    grads = tied_grads(own, other, keys, other_keys, s_query, s_key, w_value, row_factor)
    gathered = jnp.zeros((H, 3, columns, rows * HD), jnp.bfloat16)
    for s in range(parts):
        piece = grads[s] if s == 0 else shift(grads[s], "x", parts - s)
        gathered = lax.dynamic_update_slice_in_dim(
            gathered, piece, head_group * ((here + s) % parts), 0
        )
    row_grads = unpack_rows(gathered)

    col_back = [over_rows(column_backward(p)) for p in col_parts]
    col_grads = [
        jnp.concatenate([jnp.transpose(p[:, i], (1, 0, 2)) for p in col_back], axis=1)
        for i in range(3)
    ]
    return (*row_grads, *col_grads)


def solution(mesh):
    split = Mesh(mesh.devices.reshape(4, 2, 2, 2, 4), ("z", "yh", "core", "yl", "x"))
    spec = P(ROWS, ("yl", "x"), None)
    return jax.shard_map(
        local, mesh=split, in_specs=(spec,) * 8, out_specs=(spec,) * 6, check_vma=False
    )
```

time: 568 us -> 427 us (0.75); the launches traced: 561 us -> 426 us
  blocking collectives: 106 us -> 0 us
  waiting for transfers between devices: 146 us -> 235 us
  local copies, waits for them, and re-layouts: 145 us -> 61.1 us
  matrix products: 81.9 us -> 0 us
  Pallas kernels: 0 us -> 56.5 us
  starting transfers between devices: 49.1 us -> 64.1 us
  between operations: 14.6 us -> 1.04 us
  other arithmetic: 17.6 us -> 7.99 us
    ppermute x0 -> x19, waiting for transfers between devices: none -> 162 us  [shift(): return lax.ppermute(x, axis, [(i, (i + by) % n) for i in range(n)])]
    all_to_all x4 -> x0, blocking collectives: 106 us -> none  [the longest x1 34.3 us: local(): lax.all_to_all(lifted(column_grads[0]), 'row', split_axis=0, concat_axis=...]
    all_to_all x10 -> x6, waiting for transfers between devices: 146 us -> 73.4 us  [over_rows(): return lax.all_to_all(x, ROWS, split_axis=0, concat_axis=0, tiled=True)]
    pallas_call x0 -> x7, Pallas kernels: none -> 56.5 us  [the longest x2 35 us: column_backward(): pl.pallas_call(functools.partial(column_kernel, chunk=chunk), grid=(pairs...]
    dot_general x26 -> x0, matrix products: 49.8 us -> none  [the longest x6 18.8 us: head_step(): jnp.einsum('rchd,schd->chrs', grad_block, value_block, preferred_element_...]
    reshape x10 -> x0, local copies, waits for them, and re-layouts: 42.3 us -> none  [the longest x7 35.7 us: to_heads(): return tensor.reshape(tensor.shape[0], tensor.shape[1], H, HD)]
    all_to_all x20 -> x1, local copies, waits for them, and re-layouts: 25.4 us -> 1.15 us  [over_rows(): return lax.all_to_all(x, ROWS, split_axis=0, concat_axis=0, tiled=True)]
    dynamic_slice x48 -> x2, local copies, waits for them, and re-layouts: 26.8 us -> 5.53 us  [spread(): lax.dynamic_slice_in_dim(packed, head_group * ((here + s) % parts), head_...]
  transfers between devices with their start and end apart: 11 -> 25, of which waited for: 9 -> 17; matrix products, arithmetic and copies ran while one was open for 41% -> 11% of each run, Pallas kernels for 0% -> 11%
where the time goes in v1:
time: 427 us; the launch traced here: 426 us
  waiting for transfers between devices  235 us (55%)
  starting transfers between devices  64.1 us (15%)
  local copies, waits for them, and re-layouts  61.1 us (14%)
  Pallas kernels  56.5 us (13%)
  other arithmetic  7.99 us (2%)
    ppermute x19, waiting for transfers between devices, shift(): return lax.ppermute(x, axis, [(i, (i + by) % n) for i in range(n)])  162 us
    all_to_all x6, waiting for transfers between devices, over_rows(): return lax.all_to_all(x, ROWS, split_axis=0, concat_axis=0, tiled=True)  73.4 us
    all_to_all x6, starting transfers between devices, over_rows(): return lax.all_to_all(x, ROWS, split_axis=0, concat_axis=0, tiled=True)  43 us
    pallas_call x2, Pallas kernels, column_backward(): pl.pallas_call(functools.partial(column_kernel, chunk=chunk), grid=(pairs...  35 us
    ppermute x19, starting transfers between devices, shift(): return lax.ppermute(x, axis, [(i, (i + by) % n) for i in range(n)])  21 us
    unnamed x49, local copies, waits for them, and re-layouts  15.9 us
  transfers between devices with their start and end apart: 25, of which 17 were waited for; matrix products, arithmetic and copies ran while one was open for 11% of the time, Pallas kernels for 11%

profile of v1, /device:TPU:1, one launch (start us, length us, event | category | flops | bytes accessed | tf_op | source)
XLA Modules:
  0.0 426.1 jit_solution(12546215762342317986)
XLA Ops:
  3.5 3.7 pack_rows.2
  7.2 2.4 constant_dynamic-slice_fusion.5
  9.6 2.1 collective-permute-start
  11.7 2.5 collective-permute-start.1
  16.6 3.7 pack_rows.3
  20.3 3.1 constant_dynamic-slice_fusion.1
  23.7 6.1 %collective-permute-done.refs_1_ = bf16[3,2,32,2048]{3,2,1,0:T(8,128)(2,1)S(1)} collective-permute-done((bf16[3,2,32,2048]{3,2,1,0:T(8,128)(2,1)S(1)}, bf16[3,2,32,2048]{3,2,1,0:T(8,128)(2,1)S(1)}, u32[]{:S(2)}, u32[]{:S(2)}) %collective-permute-start) | collective-permute-done | bytes 786464 | tf_op jit(solution)/shard_map/ppermute | solution.py:220
  29.8 1.9 collective-permute-start.8
  31.7 16.3 %collective-permute-done.1.refs_2_ = bf16[3,2,32,2048]{3,2,1,0:T(8,128)(2,1)S(1)} collective-permute-done((bf16[3,2,32,2048]{3,2,1,0:T(8,128)(2,1)S(1)}, bf16[3,2,32,2048]{3,2,1,0:T(8,128)(2,1)S(1)}, u32[]{:S(2)}, u32[]{:S(2)}) %collective-permute-start.1) | collective-permute-done | bytes 786464 | tf_op jit(solution)/shard_map/ppermute | solution.py:220
  49.8 13.7 %collective-permute-done.7.refs_9_ = bf16[3,2,32,2048]{3,2,1,0:T(8,128)(2,1)S(1)} collective-permute-done((bf16[3,2,32,2048]{3,2,1,0:T(8,128)(2,1)S(1)}, bf16[3,2,32,2048]{3,2,1,0:T(8,128)(2,1)S(1)}, u32[]{:S(2)}, u32[]{:S(2)}) %collective-permute-start.7) | collective-permute-done | bytes 786464 | tf_op jit(solution)/shard_map/ppermute | solution.py:220
  65.1 16.6 %collective-permute-done.8.refs_10_ = bf16[3,2,32,2048]{3,2,1,0:T(8,128)(2,1)S(1)} collective-permute-done((bf16[3,2,32,2048]{3,2,1,0:T(8,128)(2,1)S(1)}, bf16[3,2,32,2048]{3,2,1,0:T(8,128)(2,1)S(1)}, u32[]{:S(2)}, u32[]{:S(2)}) %collective-permute-start.8) | collective-permute-done | bytes 786464 | tf_op jit(solution)/shard_map/ppermute | solution.py:220
  81.7 16.1 %collective-permute-done.6.refs_7_ = bf16[3,2,32,2048]{3,2,1,0:T(8,128)(2,1)S(1)} collective-permute-done((bf16[3,2,32,2048]{3,2,1,0:T(8,128)(2,1)S(1)}, bf16[3,2,32,2048]{3,2,1,0:T(8,128)(2,1)S(1)}, u32[]{:S(2)}, u32[]{:S(2)}) %collective-permute-start.6) | collective-permute-done | bytes 786464 | tf_op jit(solution)/shard_map/ppermute | solution.py:220
  98.7 4.2 tied_terms.1
  105.6 12.2 %all-to-all-start = ((f32[16,2,3,2,8,128]{5,4,3,2,1,0:T(8,128)}), f32[16,2,3,2,8,128]{5,4,3,2,1,0:T(8,128)}, u32[]{:S(2)}, u32[]{:S(2)}) async-start(f32[16,2,3,2,8,128]{5,4,3,2,1,0:T(8,128)} %copy-done.3), calls=%async_computation | async-start | bytes 1572864 | tf_op jit(solution)/shard_map/all_to_all | solution.py:224
  117.8 2.6 fusion.12
  122.9 9.3 %all-to-all-done = f32[16,2,3,2,8,128]{5,4,3,2,1,0:T(8,128)} async-done(((f32[16,2,3,2,8,128]{5,4,3,2,1,0:T(8,128)}), f32[16,2,3,2,8,128]{5,4,3,2,1,0:T(8,128)}, u32[]{:S(2)}, u32[]{:S(2)}) %all-to-all-start) | async-done | bytes 786464 | tf_op jit(solution)/shard_map/all_to_all | solution.py:224
  134.0 2.6 fusion.10
  140.7 6.8 %all-to-all-start.1 = ((bf16[16,5,3,8,128]{4,3,2,1,0:T(8,128)(2,1)}), bf16[16,5,3,8,128]{4,3,2,1,0:T(8,128)(2,1)}, u32[]{:S(2)}, u32[]{:S(2)}) async-start(bf16[16,5,3,8,128]{4,3,2,1,0:T(8,128)(2,1)} %broadcast_in_dim.5), calls=%async_computation.1 | async-start | bytes 983040 | tf_op jit(solution)/shard_map/all_to_all | solution.py:224
  147.5 2.0 copy_bitcast_fusion.6
  149.4 1.9 maximum_bitcast_fusion
  151.3 7.2 %all-to-all-done.1 = bf16[16,5,3,8,128]{4,3,2,1,0:T(8,128)(2,1)} async-done(((bf16[16,5,3,8,128]{4,3,2,1,0:T(8,128)(2,1)}), bf16[16,5,3,8,128]{4,3,2,1,0:T(8,128)(2,1)}, u32[]{:S(2)}, u32[]{:S(2)}) %all-to-all-start.1) | async-done | bytes 491552 | tf_op jit(solution)/shard_map/all_to_all | solution.py:224
  158.6 5.4 %all-to-all-start.2 = ((bf16[16,4,32,768]{3,2,1,0:T(8,128)(2,1)}), bf16[16,4,32,768]{3,2,1,0:T(8,128)(2,1)}, u32[]{:S(2)}, u32[]{:S(2)}) async-start(bf16[16,4,32,768]{3,2,1,0:T(8,128)(2,1)} %maximum_bitcast_fusion), calls=%async_computation.2 | async-start | bytes 6291456 | tf_op jit(solution)/shard_map/all_to_all | solution.py:224
  164.0 2.0 copy_bitcast_fusion
  166.4 1.9 maximum_bitcast_fusion.1
  168.4 35.5 %all-to-all-done.2.x_ref = bf16[16,4,32,768]{3,2,1,0:T(8,128)(2,1)} async-done(((bf16[16,4,32,768]{3,2,1,0:T(8,128)(2,1)}), bf16[16,4,32,768]{3,2,1,0:T(8,128)(2,1)}, u32[]{:S(2)}, u32[]{:S(2)}) %all-to-all-start.2) | async-done | bytes 3145760 | tf_op jit(solution)/shard_map/all_to_all | solution.py:224
  203.9 5.2 %all-to-all-start.4 = ((bf16[16,4,32,768]{3,2,1,0:T(8,128)(2,1)}), bf16[16,4,32,768]{3,2,1,0:T(8,128)(2,1)}, u32[]{:S(2)}, u32[]{:S(2)}) async-start(bf16[16,4,32,768]{3,2,1,0:T(8,128)(2,1)} %maximum_bitcast_fusion.1), calls=%async_computation.4 | async-start | bytes 6291456 | tf_op jit(solution)/shard_map/all_to_all | solution.py:224
  209.1 17.3 %column_attention.2 = bf16[16,3,32,768]{3,2,1,0:T(8,128)(2,1)S(1)} custom-call(bf16[16,4,32,768]{3,2,1,0:T(8,128)(2,1)} %all-to-all-done.2.x_ref), custom_call_target="tpu_custom_call" | custom-call | flops 4026531840 | bytes 5505024 | tf_op jit(solution)/shard_map/column_attention/pallas_call | solution.py:75
  227.7 21.3 %all-to-all-done.4.x_ref = bf16[16,4,32,768]{3,2,1,0:T(8,128)(2,1)} async-done(((bf16[16,4,32,768]{3,2,1,0:T(8,128)(2,1)}), bf16[16,4,32,768]{3,2,1,0:T(8,128)(2,1)}, u32[]{:S(2)}, u32[]{:S(2)}) %all-to-all-start.4) | async-done | bytes 3145760 | tf_op jit(solution)/shard_map/all_to_all | solution.py:224
  249.0 5.1 %all-to-all-start.3 = ((bf16[16,3,32,768]{3,2,1,0:T(8,128)(2,1)}), bf16[16,3,32,768]{3,2,1,0:T(8,128)(2,1)}, u32[]{:S(2)}, u32[]{:S(2)}) async-start(bf16[16,3,32,768]{3,2,1,0:T(8,128)(2,1)} %copy-done.4), calls=%async_computation.3 | async-start | bytes 4718592 | tf_op jit(solution)/shard_map/all_to_all | solution.py:224
  254.1 1.9 constant_dynamic-slice_fusion
  256.6 1.8 slice.114
  259.2 1.8 slice.115
  273.9 16.8 %collective-permute-done.10.refs_12_ = bf16[3,1,32,2048]{3,2,1,0:T(8,128)(2,1)S(1)} collective-permute-done((bf16[3,1,32,2048]{3,2,1,0:T(8,128)(2,1)}, bf16[3,1,32,2048]{3,2,1,0:T(8,128)(2,1)S(1)}, u32[]{:S(2)}, u32[]{:S(2)}) %collective-permute-start.10) | collective-permute-done | bytes 393248 | tf_op jit(solution)/shard_map/ppermute | solution.py:220
  290.7 8.5 %collective-permute-done.11.refs_13_ = bf16[3,1,32,2048]{3,2,1,0:T(8,128)(2,1)} collective-permute-done((bf16[3,1,32,2048]{3,2,1,0:T(8,128)(2,1)}, bf16[3,1,32,2048]{3,2,1,0:T(8,128)(2,1)}, u32[]{:S(2)}, u32[]{:S(2)}) %collective-permute-start.11) | collective-permute-done | bytes 393248 | tf_op jit(solution)/shard_map/ppermute | solution.py:220
  299.2 8.4 %collective-permute-done.12.refs_14_ = bf16[3,1,32,2048]{3,2,1,0:T(8,128)(2,1)} collective-permute-done((bf16[3,1,32,2048]{3,2,1,0:T(8,128)(2,1)}, bf16[3,1,32,2048]{3,2,1,0:T(8,128)(2,1)}, u32[]{:S(2)}, u32[]{:S(2)}) %collective-permute-start.12) | collective-permute-done | bytes 393248 | tf_op jit(solution)/shard_map/ppermute | solution.py:220
  307.6 8.4 %collective-permute-done.13.refs_15_ = bf16[3,1,32,2048]{3,2,1,0:T(8,128)(2,1)} collective-permute-done((bf16[3,1,32,2048]{3,2,1,0:T(8,128)(2,1)}, bf16[3,1,32,2048]{3,2,1,0:T(8,128)(2,1)}, u32[]{:S(2)}, u32[]{:S(2)}) %collective-permute-start.13) | collective-permute-done | bytes 393248 | tf_op jit(solution)/shard_map/ppermute | solution.py:220
  317.2 6.3 %tied_grads.1 = bf16[4,3,3,32,2048]{4,3,2,1,0:T(8,128)(2,1)} custom-call(bf16[3,2,32,2048]{3,2,1,0:T(8,128)(2,1)S(1)} %get-tuple-element.42.refs_0_, bf16[3,2,32,2048]{3,2,1,0:T(8,128)(2,1)S(1)} %collective-permute-done.refs_1_, bf16[3,2,32,2048]{3,2,1,0:T(8,128)(2,1)S(1)} %collective-permute-done.1.refs_2_, ...), custom_call_target="tpu_custom_call" | custom-call | flops 1207959552 | bytes 14155776 | tf_op jit(solution)/shard_map/tied_grads/pallas_call | solution.py:202
  323.5 3.8 slice_bitcast_fusion
  327.3 3.9 collective-permute-start.16
  331.2 17.8 %column_attention.3 = bf16[16,3,32,768]{3,2,1,0:T(8,128)(2,1)} custom-call(bf16[16,4,32,768]{3,2,1,0:T(8,128)(2,1)} %all-to-all-done.4.x_ref), custom_call_target="tpu_custom_call" | custom-call | flops 4026531840 | bytes 5505024 | tf_op jit(solution)/shard_map/column_attention/pallas_call | solution.py:75
  349.0 8.5 %all-to-all-start.5 = ((bf16[16,3,32,768]{3,2,1,0:T(8,128)(2,1)}), bf16[16,3,32,768]{3,2,1,0:T(8,128)(2,1)S(1)}, u32[]{:S(2)}, u32[]{:S(2)}) async-start(bf16[16,3,32,768]{3,2,1,0:T(8,128)(2,1)} %column_attention.3), calls=%async_computation.5 | async-start | bytes 4718592 | tf_op jit(solution)/shard_map/all_to_all | solution.py:224
  361.2 25.4 %collective-permute-done.17 = bf16[3,3,32,2048]{3,2,1,0:T(8,128)(2,1)S(1)} collective-permute-done((bf16[3,3,32,2048]{3,2,1,0:T(8,128)(2,1)}, bf16[3,3,32,2048]{3,2,1,0:T(8,128)(2,1)S(1)}, u32[]{:S(2)}, u32[]{:S(2)}) %collective-permute-start.17) | collective-permute-done | bytes 1179680 | tf_op jit(solution)/shard_map/ppermute | solution.py:220
  386.7 25.2 %collective-permute-done.18 = bf16[3,3,32,2048]{3,2,1,0:T(8,128)(2,1)S(1)} collective-permute-done((bf16[3,3,32,2048]{3,2,1,0:T(8,128)(2,1)S(1)}, bf16[3,3,32,2048]{3,2,1,0:T(8,128)(2,1)S(1)}, u32[]{:S(2)}, u32[]{:S(2)}) %collective-permute-start.18) | collective-permute-done | bytes 1179680 | tf_op jit(solution)/shard_map/ppermute | solution.py:220
  412.1 3.5 unpack_rows.1
  415.6 2.9 slice_bitcast_fusion.5
  419.8 2.0 copy.64
  421.9 2.0 copy.65
  424.1 2.0 copy.66
  (103 shorter events, 43.7 us)
Async XLA Ops:
  0.7 1.4 copy-start.5
  2.1 1.4 copy-start.6
  7.2 9.4 %copy-start.7 = (bf16[32,32,768]{2,1,0:T(8,128)(2,1)S(1)}, bf16[32,32,768]{2,1,0:T(8,128)(2,1)}, u32[]{:S(2)}) copy-start(bf16[32,32,768]{2,1,0:T(8,128)(2,1)} %refs_0_.3) | copy-start | bytes 4718596
  7.2 9.4 %copy-start.8 = (bf16[32,32,768]{2,1,0:T(8,128)(2,1)S(1)}, bf16[32,32,768]{2,1,0:T(8,128)(2,1)}, u32[]{:S(2)}) copy-start(bf16[32,32,768]{2,1,0:T(8,128)(2,1)} %refs_1_.3) | copy-start | bytes 4718596
  9.6 20.2 %collective-permute-start = (bf16[3,2,32,2048]{3,2,1,0:T(8,128)(2,1)S(1)}, bf16[3,2,32,2048]{3,2,1,0:T(8,128)(2,1)S(1)}, u32[]{:S(2)}, u32[]{:S(2)}) collective-permute-start(bf16[3,2,32,2048]{3,2,1,0:T(8,128)(2,1)S(1)} %get-tuple-element.41), channel_id=1, source_target_pairs={{0,1},{1,2},{2,3},{3,0},{4,5},{5,6},{6,7},{7,4},{8,9},{9,10},{10,1... | collective-permute-start | bytes 2359304 | tf_op jit(solution)/shard_map/ppermute | solution.py:220
  11.7 36.3 %collective-permute-start.1 = (bf16[3,2,32,2048]{3,2,1,0:T(8,128)(2,1)S(1)}, bf16[3,2,32,2048]{3,2,1,0:T(8,128)(2,1)S(1)}, u32[]{:S(2)}, u32[]{:S(2)}) collective-permute-start(bf16[3,2,32,2048]{3,2,1,0:T(8,128)(2,1)S(1)} %get-tuple-element.40), channel_id=1, source_target_pairs={{0,2},{1,3},{2,0},{3,1},{4,6},{5,7},{6,4},{7,5},{8,10},{9,11},{10,... | collective-permute-start | bytes 2359304 | tf_op jit(solution)/shard_map/ppermute | solution.py:220
  14.1 34.2 %collective-permute-start.2 = (bf16[3,2,32,2048]{3,2,1,0:T(8,128)(2,1)S(1)}, bf16[3,2,32,2048]{3,2,1,0:T(8,128)(2,1)S(1)}, u32[]{:S(2)}, u32[]{:S(2)}) collective-permute-start(bf16[3,2,32,2048]{3,2,1,0:T(8,128)(2,1)S(1)} %get-tuple-element.39), channel_id=1, source_target_pairs={{0,3},{1,0},{2,1},{3,2},{4,7},{5,4},{6,5},{7,6},{8,11},{9,8},{10,9... | collective-permute-start | bytes 2359304 | tf_op jit(solution)/shard_map/ppermute | solution.py:220
  15.3 34.4 %collective-permute-start.3 = (bf16[3,2,32,2048]{3,2,1,0:T(8,128)(2,1)S(1)}, bf16[3,2,32,2048]{3,2,1,0:T(8,128)(2,1)S(1)}, u32[]{:S(2)}, u32[]{:S(2)}) collective-permute-start(bf16[3,2,32,2048]{3,2,1,0:T(8,128)(2,1)S(1)} %get-tuple-element.42.refs_0_), channel_id=1, source_target_pairs={{0,4},{4,0},{1,5},{5,1},{2,6},{6,2},{3,7},{7,3},{8,12},{12,8},{9,1... | collective-permute-start | bytes 2359304 | tf_op jit(solution)/shard_map/ppermute | solution.py:220
  23.4 40.1 %collective-permute-start.7 = (bf16[3,2,32,2048]{3,2,1,0:T(8,128)(2,1)S(1)}, bf16[3,2,32,2048]{3,2,1,0:T(8,128)(2,1)S(1)}, u32[]{:S(2)}, u32[]{:S(2)}) collective-permute-start(bf16[3,2,32,2048]{3,2,1,0:T(8,128)(2,1)S(1)} %get-tuple-element.37), channel_id=1, source_target_pairs={{0,1},{1,2},{2,3},{3,0},{4,5},{5,6},{6,7},{7,4},{8,9},{9,10},{10,1... | collective-permute-start | bytes 2359304 | tf_op jit(solution)/shard_map/ppermute | solution.py:220
  29.8 51.9 %collective-permute-start.8 = (bf16[3,2,32,2048]{3,2,1,0:T(8,128)(2,1)S(1)}, bf16[3,2,32,2048]{3,2,1,0:T(8,128)(2,1)S(1)}, u32[]{:S(2)}, u32[]{:S(2)}) collective-permute-start(bf16[3,2,32,2048]{3,2,1,0:T(8,128)(2,1)S(1)} %get-tuple-element.36), channel_id=1, source_target_pairs={{0,2},{1,3},{2,0},{3,1},{4,6},{5,7},{6,4},{7,5},{8,10},{9,11},{10,... | collective-permute-start | bytes 2359304 | tf_op jit(solution)/shard_map/ppermute | solution.py:220
  48.0 33.7 %collective-permute-start.9 = (bf16[3,2,32,2048]{3,2,1,0:T(8,128)(2,1)S(1)}, bf16[3,2,32,2048]{3,2,1,0:T(8,128)(2,1)S(1)}, u32[]{:S(2)}, u32[]{:S(2)}) collective-permute-start(bf16[3,2,32,2048]{3,2,1,0:T(8,128)(2,1)S(1)} %get-tuple-element.35), channel_id=1, source_target_pairs={{0,3},{1,0},{2,1},{3,2},{4,7},{5,4},{6,5},{7,6},{8,11},{9,8},{10,9... | collective-permute-start | bytes 2359304 | tf_op jit(solution)/shard_map/ppermute | solution.py:220
  48.3 33.4 %collective-permute-start.4 = (bf16[3,2,32,2048]{3,2,1,0:T(8,128)(2,1)S(1)}, bf16[3,2,32,2048]{3,2,1,0:T(8,128)(2,1)S(1)}, u32[]{:S(2)}, u32[]{:S(2)}) collective-permute-start(bf16[3,2,32,2048]{3,2,1,0:T(8,128)(2,1)S(1)} %collective-permute-done.refs_1_), channel_id=1, source_target_pairs={{0,4},{4,0},{1,5},{5,1},{2,6},{6,2},{3,7},{7,3},{8,12},{12,8},{9,1... | collective-permute-start | bytes 2359304 | tf_op jit(solution)/shard_map/ppermute | solution.py:220
  49.7 32.0 %collective-permute-start.5 = (bf16[3,2,32,2048]{3,2,1,0:T(8,128)(2,1)S(1)}, bf16[3,2,32,2048]{3,2,1,0:T(8,128)(2,1)S(1)}, u32[]{:S(2)}, u32[]{:S(2)}) collective-permute-start(bf16[3,2,32,2048]{3,2,1,0:T(8,128)(2,1)S(1)} %collective-permute-done.1.refs_2_), channel_id=1, source_target_pairs={{0,4},{4,0},{1,5},{5,1},{2,6},{6,2},{3,7},{7,3},{8,12},{12,8},{9,1... | collective-permute-start | bytes 2359304 | tf_op jit(solution)/shard_map/ppermute | solution.py:220
  63.5 34.4 %copy-start.9 = (bf16[3,2,32,2048]{3,2,1,0:T(8,128)(2,1)}, bf16[3,2,32,2048]{3,2,1,0:T(8,128)(2,1)S(1)}, u32[]{:S(2)}) copy-start(bf16[3,2,32,2048]{3,2,1,0:T(8,128)(2,1)S(1)} %collective-permute-done.7.refs_9_) | copy-start | bytes 2359300
  63.5 34.4 %collective-permute-start.6 = (bf16[3,2,32,2048]{3,2,1,0:T(8,128)(2,1)S(1)}, bf16[3,2,32,2048]{3,2,1,0:T(8,128)(2,1)S(1)}, u32[]{:S(2)}, u32[]{:S(2)}) collective-permute-start(bf16[3,2,32,2048]{3,2,1,0:T(8,128)(2,1)S(1)} %collective-permute-done.2.refs_3_), channel_id=1, source_target_pairs={{0,4},{4,0},{1,5},{5,1},{2,6},{6,2},{3,7},{7,3},{8,12},{12,8},{9,1... | collective-permute-start | bytes 2359304 | tf_op jit(solution)/shard_map/ppermute | solution.py:220
  81.7 16.2 %copy-start.10 = (bf16[3,2,32,2048]{3,2,1,0:T(8,128)(2,1)}, bf16[3,2,32,2048]{3,2,1,0:T(8,128)(2,1)S(1)}, u32[]{:S(2)}) copy-start(bf16[3,2,32,2048]{3,2,1,0:T(8,128)(2,1)S(1)} %collective-permute-done.8.refs_10_) | copy-start | bytes 2359300
  81.7 16.2 %copy-start.11 = (bf16[3,2,32,2048]{3,2,1,0:T(8,128)(2,1)}, bf16[3,2,32,2048]{3,2,1,0:T(8,128)(2,1)S(1)}, u32[]{:S(2)}) copy-start(bf16[3,2,32,2048]{3,2,1,0:T(8,128)(2,1)S(1)} %collective-permute-done.9.refs_11_) | copy-start | bytes 2359300
  81.7 16.2 %copy-start.13 = (bf16[3,2,32,2048]{3,2,1,0:T(8,128)(2,1)}, bf16[3,2,32,2048]{3,2,1,0:T(8,128)(2,1)S(1)}, u32[]{:S(2)}) copy-start(bf16[3,2,32,2048]{3,2,1,0:T(8,128)(2,1)S(1)} %collective-permute-done.5.refs_6_) | copy-start | bytes 2359300
  97.9 0.9 copy-start.14
  102.9 0.9 copy-start
  103.8 0.9 copy-start.2
  104.7 0.9 copy-start.3
  105.6 26.7 %all-to-all-start = ((f32[16,2,3,2,8,128]{5,4,3,2,1,0:T(8,128)}), f32[16,2,3,2,8,128]{5,4,3,2,1,0:T(8,128)}, u32[]{:S(2)}, u32[]{:S(2)}) async-start(f32[16,2,3,2,8,128]{5,4,3,2,1,0:T(8,128)} %copy-done.3), calls=%async_computation | async-start | bytes 1572864 | tf_op jit(solution)/shard_map/all_to_all | solution.py:224
  117.8 2.6 copy-start.21
  133.4 4.8 %copy-start.22 = (bf16[32,32,768]{2,1,0:T(8,128)(2,1)S(1)}, bf16[32,32,768]{2,1,0:T(8,128)(2,1)}, u32[]{:S(2)}) copy-start(bf16[32,32,768]{2,1,0:T(8,128)(2,1)} %param.13) | copy-start | bytes 4718596
  133.5 3.1 collective-permute-start.14
  137.1 2.6 collective-permute-start.15
  140.7 17.9 %all-to-all-start.1 = ((bf16[16,5,3,8,128]{4,3,2,1,0:T(8,128)(2,1)}), bf16[16,5,3,8,128]{4,3,2,1,0:T(8,128)(2,1)}, u32[]{:S(2)}, u32[]{:S(2)}) async-start(bf16[16,5,3,8,128]{4,3,2,1,0:T(8,128)(2,1)} %broadcast_in_dim.5), calls=%async_computation.1 | async-start | bytes 983040 | tf_op jit(solution)/shard_map/all_to_all | solution.py:224
  147.4 2.0 copy-start.15
  147.5 2.0 copy-start.16
  158.6 45.3 %all-to-all-start.2 = ((bf16[16,4,32,768]{3,2,1,0:T(8,128)(2,1)}), bf16[16,4,32,768]{3,2,1,0:T(8,128)(2,1)}, u32[]{:S(2)}, u32[]{:S(2)}) async-start(bf16[16,4,32,768]{3,2,1,0:T(8,128)(2,1)} %maximum_bitcast_fusion), calls=%async_computation.2 | async-start | bytes 6291456 | tf_op jit(solution)/shard_map/all_to_all | solution.py:224
  164.0 2.0 copy-start.19
  164.0 2.0 copy-start.20
  203.9 45.1 %all-to-all-start.4 = ((bf16[16,4,32,768]{3,2,1,0:T(8,128)(2,1)}), bf16[16,4,32,768]{3,2,1,0:T(8,128)(2,1)}, u32[]{:S(2)}, u32[]{:S(2)}) async-start(bf16[16,4,32,768]{3,2,1,0:T(8,128)(2,1)} %maximum_bitcast_fusion.1), calls=%async_computation.4 | async-start | bytes 6291456 | tf_op jit(solution)/shard_map/all_to_all | solution.py:224
  226.4 1.4 copy-start.4
  249.0 100.0 %all-to-all-start.3 = ((bf16[16,3,32,768]{3,2,1,0:T(8,128)(2,1)}), bf16[16,3,32,768]{3,2,1,0:T(8,128)(2,1)}, u32[]{:S(2)}, u32[]{:S(2)}) async-start(bf16[16,3,32,768]{3,2,1,0:T(8,128)(2,1)} %copy-done.4), calls=%async_computation.3 | async-start | bytes 4718592 | tf_op jit(solution)/shard_map/all_to_all | solution.py:224
  254.1 7.5 %copy-start.12 = (bf16[3,2,32,2048]{3,2,1,0:T(8,128)(2,1)S(1)}, bf16[3,2,32,2048]{3,2,1,0:T(8,128)(2,1)}, u32[]{:S(2)}) copy-start(bf16[3,2,32,2048]{3,2,1,0:T(8,128)(2,1)} %copy-done.11) | copy-start | bytes 2359300
  256.0 34.7 %collective-permute-start.10 = (bf16[3,1,32,2048]{3,2,1,0:T(8,128)(2,1)}, bf16[3,1,32,2048]{3,2,1,0:T(8,128)(2,1)S(1)}, u32[]{:S(2)}, u32[]{:S(2)}) collective-permute-start(bf16[3,1,32,2048]{3,2,1,0:T(8,128)(2,1)} %constant_dynamic-slice_fusion), channel_id=1, source_target_pairs={{0,4},{4,0},{1,5},{5,1},{2,6},{6,2},{3,7},{7,3},{8,12},{12,8},{9,1... | collective-permute-start | bytes 1179656 | tf_op jit(solution)/shard_map/ppermute | solution.py:220
  258.3 40.8 %collective-permute-start.11 = (bf16[3,1,32,2048]{3,2,1,0:T(8,128)(2,1)}, bf16[3,1,32,2048]{3,2,1,0:T(8,128)(2,1)}, u32[]{:S(2)}, u32[]{:S(2)}) collective-permute-start(bf16[3,1,32,2048]{3,2,1,0:T(8,128)(2,1)} %slice.114), channel_id=1, source_target_pairs={{0,4},{4,0},{1,5},{5,1},{2,6},{6,2},{3,7},{7,3},{8,12},{12,8},{9,1... | collective-permute-start | bytes 1179656 | tf_op jit(solution)/shard_map/ppermute | solution.py:220
  261.0 46.6 %collective-permute-start.12 = (bf16[3,1,32,2048]{3,2,1,0:T(8,128)(2,1)}, bf16[3,1,32,2048]{3,2,1,0:T(8,128)(2,1)}, u32[]{:S(2)}, u32[]{:S(2)}) collective-permute-start(bf16[3,1,32,2048]{3,2,1,0:T(8,128)(2,1)} %slice.115), channel_id=1, source_target_pairs={{0,4},{4,0},{1,5},{5,1},{2,6},{6,2},{3,7},{7,3},{8,12},{12,8},{9,1... | collective-permute-start | bytes 1179656 | tf_op jit(solution)/shard_map/ppermute | solution.py:220
  262.4 53.6 %collective-permute-start.13 = (bf16[3,1,32,2048]{3,2,1,0:T(8,128)(2,1)}, bf16[3,1,32,2048]{3,2,1,0:T(8,128)(2,1)}, u32[]{:S(2)}, u32[]{:S(2)}) collective-permute-start(bf16[3,1,32,2048]{3,2,1,0:T(8,128)(2,1)} %slice.116), channel_id=1, source_target_pairs={{0,4},{4,0},{1,5},{5,1},{2,6},{6,2},{3,7},{7,3},{8,12},{12,8},{9,1... | collective-permute-start | bytes 1179656 | tf_op jit(solution)/shard_map/ppermute | solution.py:220
  316.0 1.1 copy-start.1
  327.3 32.5 %collective-permute-start.16 = (bf16[3,3,32,2048]{3,2,1,0:T(8,128)(2,1)}, bf16[3,3,32,2048]{3,2,1,0:T(8,128)(2,1)}, u32[]{:S(2)}, u32[]{:S(2)}) collective-permute-start(bf16[3,3,32,2048]{3,2,1,0:T(8,128)(2,1)} %get-tuple-element.34), channel_id=1, source_target_pairs={{0,3},{1,0},{2,1},{3,2},{4,7},{5,4},{6,5},{7,6},{8,11},{9,8},{10,9... | collective-permute-start | bytes 3538952 | tf_op jit(solution)/shard_map/ppermute | solution.py:220
  349.0 69.5 %all-to-all-start.5 = ((bf16[16,3,32,768]{3,2,1,0:T(8,128)(2,1)}), bf16[16,3,32,768]{3,2,1,0:T(8,128)(2,1)S(1)}, u32[]{:S(2)}, u32[]{:S(2)}) async-start(bf16[16,3,32,768]{3,2,1,0:T(8,128)(2,1)} %column_attention.3), calls=%async_computation.5 | async-start | bytes 4718592 | tf_op jit(solution)/shard_map/all_to_all | solution.py:224
  357.4 29.2 %collective-permute-start.17 = (bf16[3,3,32,2048]{3,2,1,0:T(8,128)(2,1)}, bf16[3,3,32,2048]{3,2,1,0:T(8,128)(2,1)S(1)}, u32[]{:S(2)}, u32[]{:S(2)}) collective-permute-start(bf16[3,3,32,2048]{3,2,1,0:T(8,128)(2,1)} %get-tuple-element.33), channel_id=1, source_target_pairs={{0,2},{1,3},{2,0},{3,1},{4,6},{5,7},{6,4},{7,5},{8,10},{9,11},{10,... | collective-permute-start | bytes 3538952 | tf_op jit(solution)/shard_map/ppermute | solution.py:220
  357.5 54.5 %collective-permute-start.18 = (bf16[3,3,32,2048]{3,2,1,0:T(8,128)(2,1)S(1)}, bf16[3,3,32,2048]{3,2,1,0:T(8,128)(2,1)S(1)}, u32[]{:S(2)}, u32[]{:S(2)}) collective-permute-start(bf16[3,3,32,2048]{3,2,1,0:T(8,128)(2,1)S(1)} %get-tuple-element.32), channel_id=1, source_target_pairs={{0,1},{1,2},{2,3},{3,0},{4,5},{5,6},{6,7},{7,4},{8,9},{9,10},{10,1... | collective-permute-start | bytes 3538952 | tf_op jit(solution)/shard_map/ppermute | solution.py:220
  418.5 1.1 copy-start.18
  419.8 2.0 copy-start.17

commit v2 on v1

v2 whole, which is shorter than its diff:
```python
import functools
import math

import jax
import jax.numpy as jnp
from jax import lax
from jax.experimental import pallas as pl
from jax.experimental.pallas import tpu as pltpu
from jax.sharding import Mesh
from jax.sharding import PartitionSpec as P

H = 12
HD = 64
PAIR = 2 * HD
WIDE = 3 * PAIR
LOG2E = 1.4426950408889634
ROWS = ("z", "yh", "core")
VMEM = 48 * 1024 * 1024
VMEM_ALL = 60 * 1024 * 1024
COST = pl.CostEstimate(flops=1, bytes_accessed=1, transcendentals=0)


def params(limit=VMEM):
    return pltpu.CompilerParams(vmem_limit_bytes=limit)


def nt(a, b):
    return lax.dot_general(a, b, (((1,), (1,)), ((), ())), preferred_element_type=jnp.float32)


def nn(a, b):
    return lax.dot_general(a, b, (((1,), (0,)), ((), ())), preferred_element_type=jnp.float32)


def tn(a, b):
    return lax.dot_general(a, b, (((0,), (0,)), ((), ())), preferred_element_type=jnp.float32)


def column_kernel(x_ref, o_ref, *, chunk):
    groups, _, rows, width = x_ref.shape
    total = groups * rows
    query, key, value, grad = (x_ref[:, i].reshape(total, width) for i in range(4))
    low = lax.broadcasted_iota(jnp.int32, (total, width), 1) < HD
    zero = jnp.zeros_like(key)
    key_t = key.T
    scale = 1.0 / math.sqrt(HD)
    key_grads, value_grads, query_grads = [], [], []
    for head in range(2):
        keep = low if head == 0 else jnp.logical_not(low)
        key_h = jnp.where(keep, key, zero)
        value_h = jnp.where(keep, value, zero)
        key_th = key_t[head * HD : (head + 1) * HD]
        key_grad, value_grad, parts = None, None, []
        for at in range(0, total, chunk):
            query_c, grad_c = query[at : at + chunk], grad[at : at + chunk]
            logits = nt(key_h, query_c)
            dprobs = nt(value_h, grad_c)
            top = jnp.max(logits, axis=0, keepdims=True)
            probs = jnp.exp2((logits - top) * (scale * LOG2E))
            probs = probs * (1.0 / jnp.sum(probs, axis=0, keepdims=True))
            slopes = probs * (dprobs - jnp.sum(probs * dprobs, axis=0, keepdims=True))
            weights = probs.astype(jnp.bfloat16)
            slopes = slopes.astype(jnp.bfloat16)
            more_key, more_value = nn(slopes, query_c), nn(weights, grad_c)
            key_grad = more_key if key_grad is None else key_grad + more_key
            value_grad = more_value if value_grad is None else value_grad + more_value
            parts.append(nn(key_th, slopes))
        key_grads.append(key_grad)
        value_grads.append(value_grad)
        query_grads.append(jnp.concatenate(parts, axis=1))
    query_grad = jnp.concatenate(query_grads, axis=0).T * scale
    key_grad = jnp.where(low, key_grads[0], key_grads[1]) * scale
    value_grad = jnp.where(low, value_grads[0], value_grads[1])
    for i, grad in enumerate((query_grad, key_grad, value_grad)):
        o_ref[:, i] = grad.astype(jnp.bfloat16).reshape(groups, rows, width)


def column_backward(x, pieces, chunk=256):
    groups, _, rows, features = x.shape
    pairs, total = features // PAIR, groups * rows
    return pl.pallas_call(
        functools.partial(column_kernel, chunk=chunk),
        grid=(pieces, pairs),
        in_specs=[pl.BlockSpec((groups, 4, rows, PAIR), lambda p, i: (0, p, 0, i))],
        out_specs=pl.BlockSpec((groups, 3, rows, PAIR), lambda p, i: (0, p, 0, i)),
        out_shape=jax.ShapeDtypeStruct((groups, 3 * pieces, rows, features), jnp.bfloat16),
        compiler_params=params(),
        cost_estimate=pl.CostEstimate(
            flops=20 * pieces * pairs * total * total * PAIR,
            bytes_accessed=14 * pieces * total * features,
            transcendentals=2 * pieces * pairs * total * total,
        ),
        name="column_attention",
    )(x)


def pack_kernel(here_ref, *refs, parts):
    ins, outs, held, sems = refs[: -parts - 2], refs[-parts - 2 : -2], refs[-2], refs[-1]
    group = held.shape[1]
    for t in range(parts):
        for k in range(group):
            lanes = slice((t * group + k) * HD, (t * group + k + 1) * HD)
            for i, ref in enumerate(ins):
                for r in range(0, ref.shape[0], 2):
                    held[t, k, i, :, r * HD : r * HD + PAIR] = jnp.concatenate(
                        [ref[r, :, lanes], ref[r + 1, :, lanes]], axis=1
                    )
        for s, out in enumerate(outs):

            @pl.when(lax.rem(t + parts - here_ref[0], parts) == s)
            def _(t=t, out=out):
                pltpu.make_async_copy(held.at[t], out, sems.at[t]).start()

    for t in range(parts):
        pltpu.make_async_copy(held.at[t], outs[0], sems.at[t]).wait()


def pack_rows(here, parts, *arrays):
    rows, columns, features = arrays[0].shape
    n, group = len(arrays), features // HD // parts
    shape = (group, n, columns, rows * HD)
    return pl.pallas_call(
        functools.partial(pack_kernel, parts=parts),
        in_specs=[pl.BlockSpec(memory_space=pltpu.SMEM)]
        + [pl.BlockSpec(memory_space=pltpu.VMEM)] * n,
        out_specs=[pl.BlockSpec(memory_space=pl.ANY)] * parts,
        out_shape=[jax.ShapeDtypeStruct(shape, jnp.bfloat16)] * parts,
        scratch_shapes=[
            pltpu.VMEM((parts,) + shape, jnp.bfloat16),
            pltpu.SemaphoreType.DMA((parts,)),
        ],
        compiler_params=params(),
        cost_estimate=COST,
        name="pack_rows",
    )(here, *arrays)


def unpack_kernel(here_ref, *refs, parts):
    ins, o_refs, held, sems = refs[:parts], refs[parts:-2], refs[-2], refs[-1]
    group = held.shape[1]
    for t in range(parts):
        for s, ref in enumerate(ins):

            @pl.when(lax.rem(t + parts - here_ref[0], parts) == s)
            def _(t=t, ref=ref):
                pltpu.make_async_copy(ref, held.at[t], sems.at[t]).start()

    for t in range(parts):
        pltpu.make_async_copy(ins[0], held.at[t], sems.at[t]).wait()
    for head in range(0, parts * group, 2):
        lanes = slice(head * HD, head * HD + PAIR)
        even, odd = divmod(head, group), divmod(head + 1, group)
        for i, ref in enumerate(o_refs):
            for r in range(0, ref.shape[0], 2):
                span = slice(r * HD, r * HD + PAIR)
                first, second = held[*even, i, :, span], held[*odd, i, :, span]
                ref[r, :, lanes] = jnp.concatenate([first[:, :HD], second[:, :HD]], axis=1)
                ref[r + 1, :, lanes] = jnp.concatenate([first[:, HD:], second[:, HD:]], axis=1)


def unpack_rows(here, chunks):
    parts = len(chunks)
    group, n, columns, width = chunks[0].shape
    rows, features = width // HD, parts * group * HD
    return pl.pallas_call(
        functools.partial(unpack_kernel, parts=parts),
        in_specs=[pl.BlockSpec(memory_space=pltpu.SMEM)]
        + [pl.BlockSpec(memory_space=pl.ANY)] * parts,
        out_specs=[pl.BlockSpec(memory_space=pltpu.VMEM)] * n,
        out_shape=[jax.ShapeDtypeStruct((rows, columns, features), jnp.bfloat16)] * n,
        scratch_shapes=[
            pltpu.VMEM((parts,) + chunks[0].shape, jnp.bfloat16),
            pltpu.SemaphoreType.DMA((parts,)),
        ],
        compiler_params=params(),
        cost_estimate=COST,
        name="unpack_rows",
    )(here, *chunks)


def joined(refs, i):
    return jnp.concatenate([ref[0, i] for ref in refs], axis=0)


def logits_kernel(*refs, parts, slices):
    own, other, keys, values = (refs[i * parts : (i + 1) * parts] for i in range(4))
    o_ref = refs[-1]
    for i in range(2):
        right = joined(values if i else keys, 0)
        for side, left in enumerate((own, other)):
            terms = nt(joined(left, i), right)
            o_ref[:, i, 0, side] = terms.reshape(slices, terms.shape[0] // slices, -1)


def tied_terms(own, other, keys, values, slices):
    parts = len(own)
    heads, _, columns, width = own[0].shape
    wide = parts * columns
    step = wide // slices
    return pl.pallas_call(
        functools.partial(logits_kernel, parts=parts, slices=slices),
        grid=(heads,),
        in_specs=[pl.BlockSpec((1, 2, columns, width), lambda i: (i, 0, 0, 0))] * (2 * parts)
        + [pl.BlockSpec((1, 1, columns, width), lambda i: (i, 0, 0, 0))] * (2 * parts),
        out_specs=pl.BlockSpec((slices, 2, 1, 2, step, wide), lambda i: (0, 0, i, 0, 0, 0)),
        out_shape=jax.ShapeDtypeStruct((slices, 2, heads, 2, step, wide), jnp.float32),
        compiler_params=params(VMEM_ALL),
        cost_estimate=COST,
        name="tied_terms",
    )(*own, *other, *keys, *values)


def grads_kernel(*refs, parts, factor):
    own, other, keys, other_keys = (refs[i * parts : (i + 1) * parts] for i in range(4))
    tied_ref, outs = refs[4 * parts], refs[4 * parts + 1 :]
    s_own, w_own, s_right, s_below, w_below = (tied_ref[i, 0] for i in range(5))
    s_query = jnp.concatenate([s_own, s_right], axis=1)
    s_key = jnp.concatenate([s_own, s_below], axis=0)
    w_value = jnp.concatenate([w_own, w_below], axis=0)
    results = (
        nn(s_query, jnp.concatenate([joined(keys, 0), joined(other_keys, 0)], axis=0)) * factor,
        tn(s_key, jnp.concatenate([joined(own, 0), joined(other, 0)], axis=0)) * factor,
        tn(w_value, jnp.concatenate([joined(own, 1), joined(other, 1)], axis=0)),
    )
    for i, result in enumerate(results):
        result = result.astype(jnp.bfloat16)
        for s, out in enumerate(outs):
            out[0, i] = result[s * out.shape[2] : (s + 1) * out.shape[2]]


def tied_grads(own, other, keys, other_keys, tied, factor):
    parts = len(own)
    heads, _, columns, width = own[0].shape
    wide = parts * columns
    two = pl.BlockSpec((1, 2, columns, width), lambda i: (i, 0, 0, 0))
    one = pl.BlockSpec((1, 1, columns, width), lambda i: (i, 0, 0, 0))
    square = pl.BlockSpec((5, 1, wide, wide), lambda i: (0, i, 0, 0))
    return pl.pallas_call(
        functools.partial(grads_kernel, parts=parts, factor=factor),
        grid=(heads,),
        in_specs=[two] * (2 * parts) + [one] * (2 * parts) + [square],
        out_specs=[pl.BlockSpec((1, 3, columns, width), lambda i: (i, 0, 0, 0))] * parts,
        out_shape=[jax.ShapeDtypeStruct((heads, 3, columns, width), jnp.bfloat16)] * parts,
        compiler_params=params(VMEM_ALL),
        cost_estimate=COST,
        name="tied_grads",
    )(*own, *other, *keys, *other_keys, tied)


def shift(x, axis, by):
    n = lax.axis_size(axis)
    return lax.ppermute(x, axis, [(i, (i + by) % n) for i in range(n)])


def over_rows(x):
    return lax.all_to_all(x, ROWS, split_axis=0, concat_axis=0, tiled=True)


def after(x, *others):
    return lax.optimization_barrier((x, others))[0]


def turned(x):
    outer, inner, width = x.shape
    n = outer * inner
    to = lax.broadcasted_iota(jnp.int32, (n, n), 0)
    source = lax.broadcasted_iota(jnp.int32, (n, n), 1)
    turn = jnp.where(source == (to % outer) * inner + to // outer, 1.0, 0.0).astype(x.dtype)
    return nn(turn, x.reshape(n, width)).astype(x.dtype).reshape(inner, outer, width)


def column_pack_kernel(*refs):
    ins, o_ref = refs[:-1], refs[-1]
    groups, _, rows, _ = o_ref.shape
    for i, ref in enumerate(ins):
        for r in range(0, rows, groups):
            o_ref[:, i, r : r + groups] = turned(ref[r : r + groups])


def column_pack(arrays, pieces, groups):
    rows, _, features = arrays[0].shape
    n = len(arrays)
    return pl.pallas_call(
        column_pack_kernel,
        grid=(pieces, features // WIDE),
        in_specs=[pl.BlockSpec((rows, groups, WIDE), lambda p, i: (0, p, i))] * n,
        out_specs=pl.BlockSpec((groups, n, rows, WIDE), lambda p, i: (0, p, 0, i)),
        out_shape=jax.ShapeDtypeStruct((groups, n * pieces, rows, features), jnp.bfloat16),
        compiler_params=params(),
        cost_estimate=COST,
        name="column_pack",
    )(*arrays)


def column_unpack_kernel(x_ref, *o_refs):
    groups, _, rows, _ = x_ref.shape
    for i, ref in enumerate(o_refs):
        for r in range(0, rows, groups):
            ref[r : r + groups] = turned(x_ref[:, i, r : r + groups])


def column_unpack(x, pieces):
    groups, parts, rows, features = x.shape
    n = parts // pieces
    return pl.pallas_call(
        column_unpack_kernel,
        grid=(pieces, features // WIDE),
        in_specs=[pl.BlockSpec((groups, n, rows, WIDE), lambda p, i: (0, p, 0, i))],
        out_specs=[pl.BlockSpec((rows, groups, WIDE), lambda p, i: (0, p, i))] * n,
        out_shape=[jax.ShapeDtypeStruct((rows, pieces * groups, features), jnp.bfloat16)] * n,
        compiler_params=params(),
        cost_estimate=COST,
        name="column_unpack",
    )(x)


def local(row_query, row_key, row_value, row_out_grad, col_query, col_key, col_value, col_out_grad):
    groups = 1
    for axis in ROWS:
        groups *= lax.axis_size(axis)
    parts = lax.axis_size("x")
    here = lax.axis_index("x")
    rows, columns, features = row_query.shape
    row_factor = 1.0 / math.sqrt(HD * rows * groups)
    head_group = H // parts
    pieces = columns // groups

    def spread(chunks):
        return [chunks[0]] + [shift(chunks[s], "x", s) for s in range(1, parts)]

    here = jnp.reshape(here, (1,)).astype(jnp.int32)
    col_ready = column_pack((col_query, col_key, col_value, col_out_grad), pieces, groups)
    col_in = over_rows(col_ready)

    row_arrays = after((row_query, row_out_grad, row_key, row_value), col_ready)
    own = spread(pack_rows(here, parts, *row_arrays[:2]))
    keys = spread(pack_rows(here, parts, row_arrays[2]))
    values = spread(pack_rows(here, parts, row_arrays[3]))
    other = [shift(c, "yl", 1) for c in own]
    col_done = column_backward(col_in, pieces)

    other_keys = [shift(c, "yl", 1) for c in after(keys[:2], other[-2])]
    terms = tied_terms(*after((own, other, keys, values), col_done), groups)
    terms = over_rows(after(terms, other_keys[0]))
    sums = jnp.sum(after(terms, other_keys), axis=0)
    across = shift(sums, "yl", 1)
    other_keys += [shift(c, "yl", 1) for c in after(keys[2:], across)]

    logits, dprobs = jnp.concatenate([sums, jnp.flip(across, 2)], axis=-1)
    probs = jax.nn.softmax(logits * row_factor, axis=-1)
    slopes = probs * (dprobs - jnp.sum(probs * dprobs, axis=-1, keepdims=True))
    probs, slopes = probs.astype(jnp.bfloat16), slopes.astype(jnp.bfloat16)
    wide = probs.shape[-1] // 2
    payload = jnp.stack(
        [
            slopes[:, 0, :, :wide],
            probs[:, 0, :, :wide],
            slopes[:, 0, :, wide:],
            slopes[:, 1, :, :wide],
            probs[:, 1, :, :wide],
        ]
    )
    whole = over_rows(jnp.broadcast_to(payload[None], (groups,) + payload.shape))
    col_grads = column_unpack(over_rows(after(col_done, whole, other_keys)), pieces)
    whole = jnp.transpose(whole, (1, 2, 0, 3, 4)).reshape(5, head_group, wide, wide)
    grads = tied_grads(own, other, keys, other_keys, whole, row_factor)
    chunks = [grads[0]] + [shift(grads[s], "x", parts - s) for s in range(1, parts)]
    row_grads = unpack_rows(here, chunks)
    return (*row_grads, *col_grads)


def solution(mesh):
    split = Mesh(mesh.devices.reshape(4, 2, 2, 2, 4), ("z", "yh", "core", "yl", "x"))
    spec = P(ROWS, ("yl", "x"), None)
    return jax.shard_map(
        local, mesh=split, in_specs=(spec,) * 8, out_specs=(spec,) * 6, check_vma=False
    )
```

time: 427 us -> 318 us (0.74)
  waiting for transfers between devices: 235 us -> 175 us
  local copies, waits for them, and re-layouts: 61.1 us -> 11.8 us
  Pallas kernels: 56.5 us -> 70 us
  other arithmetic: 7.99 us -> 1.68 us
  starting transfers between devices: 64.1 us -> 58.4 us
    all_to_all x6 -> x4, waiting for transfers between devices: 73.4 us -> 0.01 us  [over_rows(): return lax.all_to_all(x, ROWS, split_axis=0, concat_axis=0, tiled=True)]
    slice x9 -> x0, local copies, waits for them, and re-layouts: 13.7 us -> none  [the longest x4 7.5 us: column_in(): a[:, piece * groups:(piece + 1) * groups]]
    another operation x9 -> x1, local copies, waits for them, and re-layouts: 13.4 us -> 0.01 us  [local(): jnp.stack([slopes[:, 0, :, :wide], probs[:, 0, :, :wide], slopes[:, 0, :,...]
    ppermute x19 -> x21, waiting for transfers between devices: 162 us -> 175 us  [shift(): return lax.ppermute(x, axis, [(i, (i + by) % n) for i in range(n)])]
    pallas_call x5 -> x7, Pallas kernels: 45.9 us -> 56.7 us  [the longest x1 33.6 us: column_backward(): pl.pallas_call(functools.partial(column_kernel, chunk=chunk), grid=(piece...]
    all_to_all x6 -> x4, starting transfers between devices: 43 us -> 34.1 us  [over_rows(): return lax.all_to_all(x, ROWS, split_axis=0, concat_axis=0, tiled=True)]
    unnamed x49 -> x54, local copies, waits for them, and re-layouts: 15.9 us -> 9.97 us
    dynamic_slice x2 -> x0, local copies, waits for them, and re-layouts: 5.53 us -> none  [spread(): lax.dynamic_slice_in_dim(packed, head_group * ((here + s) % parts), head_...]
  transfers between devices with their start and end apart: 25 -> 25, of which waited for: 17 -> 13; matrix products, arithmetic and copies ran while one was open for 11% -> 0% of each run, Pallas kernels for 11% -> 18%
where the time goes in v2:
time: 318 us; the launch traced here: 317 us
  waiting for transfers between devices  175 us (55%)
  Pallas kernels  70 us (22%)
  starting transfers between devices  58.4 us (18%)
  local copies, waits for them, and re-layouts  11.8 us (4%)
    ppermute x21, waiting for transfers between devices, shift(): return lax.ppermute(x, axis, [(i, (i + by) % n) for i in range(n)])  175 us
    all_to_all x4, starting transfers between devices, over_rows(): return lax.all_to_all(x, ROWS, split_axis=0, concat_axis=0, tiled=True)  34.1 us
    pallas_call x1, Pallas kernels, column_backward(): pl.pallas_call(functools.partial(column_kernel, chunk=chunk), grid=(piece...  33.6 us
    ppermute x21, starting transfers between devices, shift(): return lax.ppermute(x, axis, [(i, (i + by) % n) for i in range(n)])  24.3 us
    unnamed x54, local copies, waits for them, and re-layouts  9.97 us
    pallas_call x1, Pallas kernels, tied_grads(): pl.pallas_call(functools.partial(grads_kernel, parts=parts, factor=factor...  7.23 us
  transfers between devices with their start and end apart: 25, of which 13 were waited for; matrix products, arithmetic and copies ran while one was open for 0% of the time, Pallas kernels for 18%

profile of v2, /device:TPU:1, one launch (start us, length us, event | category | flops | bytes accessed | tf_op | source)
XLA Modules:
  0.0 317.5 jit_solution(2244057115677258874)
XLA Ops:
  0.6 1.4 copy-done.3
  2.0 1.4 copy-done.4
  3.5 1.4 copy-done.5
  4.9 6.2 %column_pack.1 = bf16[16,8,32,768]{3,2,1,0:T(8,128)(2,1)} custom-call(bf16[32,32,768]{2,1,0:T(8,128)(2,1)S(1)} %copy-done.3, bf16[32,32,768]{2,1,0:T(8,128)(2,1)S(1)} %copy-done.4, bf16[32,32,768]{2,1,0:T(8,128)(2,1)S(1)} %copy-done.5, bf16[32,32,768]{2,1,0:T(8,128)(2,1)} %refs_3_.1), custom_call_target="tpu_custom_call" | custom-call | flops 1 | bytes 1 | tf_op jit(solution)/shard_map/column_pack/pallas_call | solution.py:283
  11.0 9.6 %all-to-all-start = ((bf16[16,8,32,768]{3,2,1,0:T(8,128)(2,1)}), bf16[16,8,32,768]{3,2,1,0:T(8,128)(2,1)}, u32[]{:S(2)}, u32[]{:S(2)}) async-start(bf16[16,8,32,768]{3,2,1,0:T(8,128)(2,1)} %column_pack.1), calls=%async_computation | async-start | bytes 12582912 | tf_op jit(solution)/shard_map/all_to_all | solution.py:256
  20.6 3.0 pack_rows.3
  23.7 2.8 collective-permute-start.1
  26.5 1.6 pack_rows.4
  28.6 2.6 collective-permute-start.2
  31.1 13.2 %collective-permute-done.1.refs_2_ = bf16[3,2,32,2048]{3,2,1,0:T(8,128)(2,1)S(1)} collective-permute-done((bf16[3,2,32,2048]{3,2,1,0:T(8,128)(2,1)S(1)}, bf16[3,2,32,2048]{3,2,1,0:T(8,128)(2,1)S(1)}, u32[]{:S(2)}, u32[]{:S(2)}) %collective-permute-start.1) | collective-permute-done | bytes 786464 | tf_op jit(solution)/shard_map/ppermute | solution.py:252
  44.8 2.7 collective-permute-start.8
  47.5 5.7 %collective-permute-done.7.refs_9_ = bf16[3,1,32,2048]{3,2,1,0:T(8,128)(2,1)S(1)} collective-permute-done((bf16[3,1,32,2048]{3,2,1,0:T(8,128)(2,1)S(1)}, bf16[3,1,32,2048]{3,2,1,0:T(8,128)(2,1)S(1)}, u32[]{:S(2)}, u32[]{:S(2)}) %collective-permute-start.7) | collective-permute-done | bytes 393248 | tf_op jit(solution)/shard_map/ppermute | solution.py:252
  53.3 1.6 pack_rows.5
  54.9 0.7 copy-done.10
  55.6 22.5 %collective-permute-done.8.refs_10_ = bf16[3,1,32,2048]{3,2,1,0:T(8,128)(2,1)S(1)} collective-permute-done((bf16[3,1,32,2048]{3,2,1,0:T(8,128)(2,1)S(1)}, bf16[3,1,32,2048]{3,2,1,0:T(8,128)(2,1)S(1)}, u32[]{:S(2)}, u32[]{:S(2)}) %collective-permute-start.8) | collective-permute-done | bytes 393248 | tf_op jit(solution)/shard_map/ppermute | solution.py:252
  78.2 2.7 collective-permute-start.13
  81.4 1.1 collective-permute-start.4
  82.5 25.4 %collective-permute-done.5.refs_6_ = bf16[3,2,32,2048]{3,2,1,0:T(8,128)(2,1)S(1)} collective-permute-done((bf16[3,2,32,2048]{3,2,1,0:T(8,128)(2,1)S(1)}, bf16[3,2,32,2048]{3,2,1,0:T(8,128)(2,1)S(1)}, u32[]{:S(2)}, u32[]{:S(2)}) %collective-permute-start.5) | collective-permute-done | bytes 786464 | tf_op jit(solution)/shard_map/ppermute | solution.py:252
  107.9 1.1 collective-permute-start.6
  109.0 2.5 collective-permute-start.14
  111.5 0.7 copy-done.22
  112.6 33.6 %column_attention.1 = bf16[16,6,32,768]{3,2,1,0:T(8,128)(2,1)S(1)} custom-call(bf16[16,8,32,768]{3,2,1,0:T(8,128)(2,1)} %all-to-all-done.x_ref), custom_call_target="tpu_custom_call" | custom-call | flops 8053063680 | bytes 11010048 | tf_op jit(solution)/shard_map/column_attention/pallas_call | solution.py:81
  146.3 2.1 copy-done
  148.5 10.1 %collective-permute-done.6.refs_7_ = bf16[3,2,32,2048]{3,2,1,0:T(8,128)(2,1)} collective-permute-done((bf16[3,2,32,2048]{3,2,1,0:T(8,128)(2,1)}, bf16[3,2,32,2048]{3,2,1,0:T(8,128)(2,1)}, u32[]{:S(2)}, u32[]{:S(2)}) %collective-permute-start.6) | collective-permute-done | bytes 786464 | tf_op jit(solution)/shard_map/ppermute | solution.py:252
  158.6 6.0 %tied_terms.1 = f32[16,2,3,2,8,128]{5,4,3,2,1,0:T(8,128)} custom-call(bf16[3,2,32,2048]{3,2,1,0:T(8,128)(2,1)} %copy-done.1, bf16[3,2,32,2048]{3,2,1,0:T(8,128)(2,1)} %copy-done.12, bf16[3,2,32,2048]{3,2,1,0:T(8,128)(2,1)} %copy-done.11, bf16[3,2,32,2048]{3,2,1,0:T(8,128)(2,1)} %collective-permute-done.2.refs_3_, ...), custom_call_target="tpu_custom_call" | custom-call | flops 1 | bytes 1 | tf_op jit(solution)/shard_map/tied_terms/pallas_call | solution.py:200
  164.6 2.4 collective-permute-done.10.refs_12_
  167.0 7.4 %all-to-all-start.1 = ((f32[16,2,3,2,8,128]{5,4,3,2,1,0:T(8,128)}), f32[16,2,3,2,8,128]{5,4,3,2,1,0:T(8,128)S(1)}, u32[]{:S(2)}, u32[]{:S(2)}) async-start(f32[16,2,3,2,8,128]{5,4,3,2,1,0:T(8,128)} %tied_terms.1), calls=%async_computation.1 | async-start | bytes 1572864 | tf_op jit(solution)/shard_map/all_to_all | solution.py:256
  174.5 17.8 %collective-permute-done.11.refs_13_ = bf16[3,1,32,2048]{3,2,1,0:T(8,128)(2,1)S(1)} collective-permute-done((bf16[3,1,32,2048]{3,2,1,0:T(8,128)(2,1)S(1)}, bf16[3,1,32,2048]{3,2,1,0:T(8,128)(2,1)S(1)}, u32[]{:S(2)}, u32[]{:S(2)}) %collective-permute-start.11) | collective-permute-done | bytes 393248 | tf_op jit(solution)/shard_map/ppermute | solution.py:252
  192.4 1.7 collective-permute-start.15
  194.2 1.5 collective-permute-done.15
  195.7 1.4 fusion.26
  197.3 0.8 broadcast_in_dim.2
  198.2 9.0 %all-to-all-start.2 = ((bf16[16,5,3,8,128]{4,3,2,1,0:T(8,128)(2,1)}), bf16[16,5,3,8,128]{4,3,2,1,0:T(8,128)(2,1)S(1)}, u32[]{:S(2)}, u32[]{:S(2)}) async-start(bf16[16,5,3,8,128]{4,3,2,1,0:T(8,128)(2,1)} %broadcast_in_dim.2), calls=%async_computation.2 | async-start | bytes 983040 | tf_op jit(solution)/shard_map/all_to_all | solution.py:256
  207.7 1.1 collective-permute-start.17
  208.8 13.8 %collective-permute-done.16.refs_14_ = bf16[3,1,32,2048]{3,2,1,0:T(8,128)(2,1)S(1)} collective-permute-done((bf16[3,1,32,2048]{3,2,1,0:T(8,128)(2,1)S(1)}, bf16[3,1,32,2048]{3,2,1,0:T(8,128)(2,1)S(1)}, u32[]{:S(2)}, u32[]{:S(2)}) %collective-permute-start.16) | collective-permute-done | bytes 393248 | tf_op jit(solution)/shard_map/ppermute | solution.py:252
  222.6 8.4 %collective-permute-done.17.refs_15_ = bf16[3,1,32,2048]{3,2,1,0:T(8,128)(2,1)S(1)} collective-permute-done((bf16[3,1,32,2048]{3,2,1,0:T(8,128)(2,1)S(1)}, bf16[3,1,32,2048]{3,2,1,0:T(8,128)(2,1)S(1)}, u32[]{:S(2)}, u32[]{:S(2)}) %collective-permute-start.17) | collective-permute-done | bytes 393248 | tf_op jit(solution)/shard_map/ppermute | solution.py:252
  231.0 0.7 copy-done.24
  231.8 8.1 %all-to-all-start.3 = ((bf16[16,6,32,768]{3,2,1,0:T(8,128)(2,1)}), bf16[16,6,32,768]{3,2,1,0:T(8,128)(2,1)}, u32[]{:S(2)}, u32[]{:S(2)}) async-start(bf16[16,6,32,768]{3,2,1,0:T(8,128)(2,1)} %copy-done), calls=%async_computation.3 | async-start | bytes 9437184 | tf_op jit(solution)/shard_map/all_to_all | solution.py:256
  239.8 0.9 copy_bitcast_fusion.refs_16_
  240.8 7.2 %tied_grads.1 = (bf16[3,3,32,2048]{3,2,1,0:T(8,128)(2,1)}, bf16[3,3,32,2048]{3,2,1,0:T(8,128)(2,1)}, bf16[3,3,32,2048]{3,2,1,0:T(8,128)(2,1)}, bf16[3,3,32,2048]{3,2,1,0:T(8,128)(2,1)}) custom-call(bf16[3,2,32,2048]{3,2,1,0:T(8,128)(2,1)} %copy-done.1, bf16[3,2,32,2048]{3,2,1,0:T(8,128)(2,1)} %copy-done.12, bf16[3,2,32,2048]{3,2,1,0:T(8,128)(2,1)} %copy-done.11, ...), custom_call_target="tpu_custom_call" | custom-call | flops 1 | bytes 1 | tf_op jit(solution)/shard_map/tied_grads/pallas_call | solution.py:238
  248.0 2.5 collective-permute-start.18
  250.5 0.5 collective-permute-start.19
  251.1 0.6 collective-permute-start.20
  251.7 49.5 %collective-permute-done.18.refs_1_ = bf16[3,3,32,2048]{3,2,1,0:T(8,128)(2,1)S(1)} collective-permute-done((bf16[3,3,32,2048]{3,2,1,0:T(8,128)(2,1)}, bf16[3,3,32,2048]{3,2,1,0:T(8,128)(2,1)S(1)}, u32[]{:S(2)}, u32[]{:S(2)}) %collective-permute-start.18) | collective-permute-done | bytes 1179680 | tf_op jit(solution)/shard_map/ppermute | solution.py:252
  301.2 4.2 %collective-permute-done.20.refs_3_ = bf16[3,3,32,2048]{3,2,1,0:T(8,128)(2,1)S(1)} collective-permute-done((bf16[3,3,32,2048]{3,2,1,0:T(8,128)(2,1)}, bf16[3,3,32,2048]{3,2,1,0:T(8,128)(2,1)S(1)}, u32[]{:S(2)}, u32[]{:S(2)}) %collective-permute-start.20) | collective-permute-done | bytes 1179680 | tf_op jit(solution)/shard_map/ppermute | solution.py:252
  305.4 1.3 copy-done.9
  306.7 4.6 %unpack_rows.1 = (bf16[32,32,768]{2,1,0:T(8,128)(2,1)}, bf16[32,32,768]{2,1,0:T(8,128)(2,1)}, bf16[32,32,768]{2,1,0:T(8,128)(2,1)}) custom-call(s32[1]{0:T(128)} %bitcast.here_ref, bf16[3,3,32,2048]{3,2,1,0:T(8,128)(2,1)S(1)} %copy-done.9, bf16[3,3,32,2048]{3,2,1,0:T(8,128)(2,1)S(1)} %collective-permute-done.18.refs_1_, ...), custom_call_target="tpu_custom_call" | custom-call | flops 1 | bytes 1 | tf_op jit(solution)/shard_map/unpack_rows/pallas_call | solution.py:165
  311.3 6.2 %column_unpack.1 = (bf16[32,32,768]{2,1,0:T(8,128)(2,1)}, bf16[32,32,768]{2,1,0:T(8,128)(2,1)}, bf16[32,32,768]{2,1,0:T(8,128)(2,1)}) custom-call(bf16[16,6,32,768]{3,2,1,0:T(8,128)(2,1)} %all-to-all-done.3.x_ref), custom_call_target="tpu_custom_call" | custom-call | flops 1 | bytes 1 | tf_op jit(solution)/shard_map/column_unpack/pallas_call | solution.py:305
  (75 shorter events, 2.9 us)
Async XLA Ops:
  0.6 1.4 copy-start.3
  2.0 1.4 copy-start.4
  3.5 1.4 copy-start.5
  11.0 9.6 %copy-start.8 = (bf16[32,32,768]{2,1,0:T(8,128)(2,1)S(1)}, bf16[32,32,768]{2,1,0:T(8,128)(2,1)}, u32[]{:S(2)}) copy-start(bf16[32,32,768]{2,1,0:T(8,128)(2,1)} %refs_0_.2) | copy-start | bytes 4718596
  11.0 101.6 %all-to-all-start = ((bf16[16,8,32,768]{3,2,1,0:T(8,128)(2,1)}), bf16[16,8,32,768]{3,2,1,0:T(8,128)(2,1)}, u32[]{:S(2)}, u32[]{:S(2)}) async-start(bf16[16,8,32,768]{3,2,1,0:T(8,128)(2,1)} %column_pack.1), calls=%async_computation | async-start | bytes 12582912 | tf_op jit(solution)/shard_map/all_to_all | solution.py:256
  20.6 5.9 %copy-start.6 = (bf16[32,32,768]{2,1,0:T(8,128)(2,1)S(1)}, bf16[32,32,768]{2,1,0:T(8,128)(2,1)}, u32[]{:S(2)}) copy-start(bf16[32,32,768]{2,1,0:T(8,128)(2,1)} %refs_0_.3) | copy-start | bytes 4718596
  23.6 57.3 %copy-start.1 = (bf16[3,2,32,2048]{3,2,1,0:T(8,128)(2,1)}, bf16[3,2,32,2048]{3,2,1,0:T(8,128)(2,1)S(1)}, u32[]{:S(2)}) copy-start(bf16[3,2,32,2048]{3,2,1,0:T(8,128)(2,1)S(1)} %get-tuple-element.73.refs_0_) | copy-start | bytes 2359300
  23.6 29.6 %copy-start.7 = (bf16[32,32,768]{2,1,0:T(8,128)(2,1)S(1)}, bf16[32,32,768]{2,1,0:T(8,128)(2,1)}, u32[]{:S(2)}) copy-start(bf16[32,32,768]{2,1,0:T(8,128)(2,1)} %refs_0_.4) | copy-start | bytes 4718596
  23.7 20.7 %collective-permute-start.1 = (bf16[3,2,32,2048]{3,2,1,0:T(8,128)(2,1)S(1)}, bf16[3,2,32,2048]{3,2,1,0:T(8,128)(2,1)S(1)}, u32[]{:S(2)}, u32[]{:S(2)}) collective-permute-start(bf16[3,2,32,2048]{3,2,1,0:T(8,128)(2,1)S(1)} %get-tuple-element.59), channel_id=1, source_target_pairs={{0,2},{1,3},{2,0},{3,1},{4,6},{5,7},{6,4},{7,5},{8,10},{9,11},{10,... | collective-permute-start | bytes 2359304 | tf_op jit(solution)/shard_map/ppermute | solution.py:252
  28.1 118.2 %copy-start.2 = (bf16[3,1,32,2048]{3,2,1,0:T(8,128)(2,1)}, bf16[3,1,32,2048]{3,2,1,0:T(8,128)(2,1)S(1)}, u32[]{:S(2)}) copy-start(bf16[3,1,32,2048]{3,2,1,0:T(8,128)(2,1)S(1)} %get-tuple-element.81.refs_8_) | copy-start | bytes 1179652
  28.1 25.2 %collective-permute-start.7 = (bf16[3,1,32,2048]{3,2,1,0:T(8,128)(2,1)S(1)}, bf16[3,1,32,2048]{3,2,1,0:T(8,128)(2,1)S(1)}, u32[]{:S(2)}, u32[]{:S(2)}) collective-permute-start(bf16[3,1,32,2048]{3,2,1,0:T(8,128)(2,1)S(1)} %get-tuple-element.63), channel_id=1, source_target_pairs={{0,1},{1,2},{2,3},{3,0},{4,5},{5,6},{6,7},{7,4},{8,9},{9,10},{10,1... | collective-permute-start | bytes 1179656 | tf_op jit(solution)/shard_map/ppermute | solution.py:252
  28.5 52.5 %collective-permute-start = (bf16[3,2,32,2048]{3,2,1,0:T(8,128)(2,1)S(1)}, bf16[3,2,32,2048]{3,2,1,0:T(8,128)(2,1)S(1)}, u32[]{:S(2)}, u32[]{:S(2)}) collective-permute-start(bf16[3,2,32,2048]{3,2,1,0:T(8,128)(2,1)S(1)} %get-tuple-element.58), channel_id=1, source_target_pairs={{0,1},{1,2},{2,3},{3,0},{4,5},{5,6},{6,7},{7,4},{8,9},{9,10},{10,1... | collective-permute-start | bytes 2359304 | tf_op jit(solution)/shard_map/ppermute | solution.py:252
  28.6 52.9 %collective-permute-start.2 = (bf16[3,2,32,2048]{3,2,1,0:T(8,128)(2,1)S(1)}, bf16[3,2,32,2048]{3,2,1,0:T(8,128)(2,1)}, u32[]{:S(2)}, u32[]{:S(2)}) collective-permute-start(bf16[3,2,32,2048]{3,2,1,0:T(8,128)(2,1)S(1)} %get-tuple-element.60), channel_id=1, source_target_pairs={{0,3},{1,0},{2,1},{3,2},{4,7},{5,4},{6,5},{7,6},{8,11},{9,8},{10,9... | collective-permute-start | bytes 2359304 | tf_op jit(solution)/shard_map/ppermute | solution.py:252
  44.4 101.9 %copy-start.11 = (bf16[3,2,32,2048]{3,2,1,0:T(8,128)(2,1)}, bf16[3,2,32,2048]{3,2,1,0:T(8,128)(2,1)S(1)}, u32[]{:S(2)}) copy-start(bf16[3,2,32,2048]{3,2,1,0:T(8,128)(2,1)S(1)} %collective-permute-done.1.refs_2_) | copy-start | bytes 2359300
  44.4 63.5 %collective-permute-start.5 = (bf16[3,2,32,2048]{3,2,1,0:T(8,128)(2,1)S(1)}, bf16[3,2,32,2048]{3,2,1,0:T(8,128)(2,1)S(1)}, u32[]{:S(2)}, u32[]{:S(2)}) collective-permute-start(bf16[3,2,32,2048]{3,2,1,0:T(8,128)(2,1)S(1)} %collective-permute-done.1.refs_2_), channel_id=1, source_target_pairs={{0,4},{4,0},{1,5},{5,1},{2,6},{6,2},{3,7},{7,3},{8,12},{12,8},{9,1... | collective-permute-start | bytes 2359304 | tf_op jit(solution)/shard_map/ppermute | solution.py:252
  44.8 33.3 %collective-permute-start.8 = (bf16[3,1,32,2048]{3,2,1,0:T(8,128)(2,1)S(1)}, bf16[3,1,32,2048]{3,2,1,0:T(8,128)(2,1)S(1)}, u32[]{:S(2)}, u32[]{:S(2)}) collective-permute-start(bf16[3,1,32,2048]{3,2,1,0:T(8,128)(2,1)S(1)} %get-tuple-element.64), channel_id=1, source_target_pairs={{0,2},{1,3},{2,0},{3,1},{4,6},{5,7},{6,4},{7,5},{8,10},{9,11},{10,... | collective-permute-start | bytes 1179656 | tf_op jit(solution)/shard_map/ppermute | solution.py:252
  53.2 93.0 %copy-start.14 = (bf16[3,1,32,2048]{3,2,1,0:T(8,128)(2,1)}, bf16[3,1,32,2048]{3,2,1,0:T(8,128)(2,1)S(1)}, u32[]{:S(2)}) copy-start(bf16[3,1,32,2048]{3,2,1,0:T(8,128)(2,1)S(1)} %collective-permute-done.7.refs_9_) | copy-start | bytes 1179652
  53.2 25.0 %collective-permute-start.9 = (bf16[3,1,32,2048]{3,2,1,0:T(8,128)(2,1)S(1)}, bf16[3,1,32,2048]{3,2,1,0:T(8,128)(2,1)S(1)}, u32[]{:S(2)}, u32[]{:S(2)}) collective-permute-start(bf16[3,1,32,2048]{3,2,1,0:T(8,128)(2,1)S(1)} %get-tuple-element.65), channel_id=1, source_target_pairs={{0,3},{1,0},{2,1},{3,2},{4,7},{5,4},{6,5},{7,6},{8,11},{9,8},{10,9... | collective-permute-start | bytes 1179656 | tf_op jit(solution)/shard_map/ppermute | solution.py:252
  78.1 33.4 %copy-start.16 = (bf16[3,1,32,2048]{3,2,1,0:T(8,128)(2,1)}, bf16[3,1,32,2048]{3,2,1,0:T(8,128)(2,1)S(1)}, u32[]{:S(2)}) copy-start(bf16[3,1,32,2048]{3,2,1,0:T(8,128)(2,1)S(1)} %collective-permute-done.8.refs_10_) | copy-start | bytes 1179652
  78.1 30.9 %collective-permute-start.12 = (bf16[3,1,32,2048]{3,2,1,0:T(8,128)(2,1)S(1)}, bf16[3,1,32,2048]{3,2,1,0:T(8,128)(2,1)S(1)}, u32[]{:S(2)}, u32[]{:S(2)}) collective-permute-start(bf16[3,1,32,2048]{3,2,1,0:T(8,128)(2,1)S(1)} %get-tuple-element.70), channel_id=1, source_target_pairs={{0,1},{1,2},{2,3},{3,0},{4,5},{5,6},{6,7},{7,4},{8,9},{9,10},{10,1... | collective-permute-start | bytes 1179656 | tf_op jit(solution)/shard_map/ppermute | solution.py:252
  78.2 33.2 %copy-start.18 = (bf16[3,1,32,2048]{3,2,1,0:T(8,128)(2,1)}, bf16[3,1,32,2048]{3,2,1,0:T(8,128)(2,1)S(1)}, u32[]{:S(2)}) copy-start(bf16[3,1,32,2048]{3,2,1,0:T(8,128)(2,1)S(1)} %collective-permute-done.9.refs_11_) | copy-start | bytes 1179652
  78.2 33.2 %collective-permute-start.13 = (bf16[3,1,32,2048]{3,2,1,0:T(8,128)(2,1)S(1)}, bf16[3,1,32,2048]{3,2,1,0:T(8,128)(2,1)S(1)}, u32[]{:S(2)}, u32[]{:S(2)}) collective-permute-start(bf16[3,1,32,2048]{3,2,1,0:T(8,128)(2,1)S(1)} %get-tuple-element.71), channel_id=1, source_target_pairs={{0,2},{1,3},{2,0},{3,1},{4,6},{5,7},{6,4},{7,5},{8,10},{9,11},{10,... | collective-permute-start | bytes 1179656 | tf_op jit(solution)/shard_map/ppermute | solution.py:252
  80.9 65.4 %copy-start.12 = (bf16[3,2,32,2048]{3,2,1,0:T(8,128)(2,1)}, bf16[3,2,32,2048]{3,2,1,0:T(8,128)(2,1)S(1)}, u32[]{:S(2)}) copy-start(bf16[3,2,32,2048]{3,2,1,0:T(8,128)(2,1)S(1)} %collective-permute-done.refs_1_) | copy-start | bytes 2359300
  80.9 67.5 %collective-permute-start.3 = (bf16[3,2,32,2048]{3,2,1,0:T(8,128)(2,1)S(1)}, bf16[3,2,32,2048]{3,2,1,0:T(8,128)(2,1)}, u32[]{:S(2)}, u32[]{:S(2)}) collective-permute-start(bf16[3,2,32,2048]{3,2,1,0:T(8,128)(2,1)S(1)} %get-tuple-element.73.refs_0_), channel_id=1, source_target_pairs={{0,4},{4,0},{1,5},{5,1},{2,6},{6,2},{3,7},{7,3},{8,12},{12,8},{9,1... | collective-permute-start | bytes 2359304 | tf_op jit(solution)/shard_map/ppermute | solution.py:252
  81.4 67.0 %collective-permute-start.4 = (bf16[3,2,32,2048]{3,2,1,0:T(8,128)(2,1)S(1)}, bf16[3,2,32,2048]{3,2,1,0:T(8,128)(2,1)}, u32[]{:S(2)}, u32[]{:S(2)}) collective-permute-start(bf16[3,2,32,2048]{3,2,1,0:T(8,128)(2,1)S(1)} %collective-permute-done.refs_1_), channel_id=1, source_target_pairs={{0,4},{4,0},{1,5},{5,1},{2,6},{6,2},{3,7},{7,3},{8,12},{12,8},{9,1... | collective-permute-start | bytes 2359304 | tf_op jit(solution)/shard_map/ppermute | solution.py:252
  107.9 3.6 %copy-start.13 = (bf16[3,2,32,2048]{3,2,1,0:T(8,128)(2,1)}, bf16[3,2,32,2048]{3,2,1,0:T(8,128)(2,1)S(1)}, u32[]{:S(2)}) copy-start(bf16[3,2,32,2048]{3,2,1,0:T(8,128)(2,1)S(1)} %collective-permute-done.5.refs_6_) | copy-start | bytes 2359300
  107.9 50.7 %collective-permute-start.6 = (bf16[3,2,32,2048]{3,2,1,0:T(8,128)(2,1)}, bf16[3,2,32,2048]{3,2,1,0:T(8,128)(2,1)}, u32[]{:S(2)}, u32[]{:S(2)}) collective-permute-start(bf16[3,2,32,2048]{3,2,1,0:T(8,128)(2,1)} %collective-permute-done.2.refs_3_), channel_id=1, source_target_pairs={{0,4},{4,0},{1,5},{5,1},{2,6},{6,2},{3,7},{7,3},{8,12},{12,8},{9,1... | collective-permute-start | bytes 2359304 | tf_op jit(solution)/shard_map/ppermute | solution.py:252
  109.0 2.5 copy-start.21
  109.0 39.5 %collective-permute-start.14 = (bf16[3,1,32,2048]{3,2,1,0:T(8,128)(2,1)S(1)}, bf16[3,1,32,2048]{3,2,1,0:T(8,128)(2,1)}, u32[]{:S(2)}, u32[]{:S(2)}) collective-permute-start(bf16[3,1,32,2048]{3,2,1,0:T(8,128)(2,1)S(1)} %get-tuple-element.72), channel_id=1, source_target_pairs={{0,3},{1,0},{2,1},{3,2},{4,7},{5,4},{6,5},{7,6},{8,11},{9,8},{10,9... | collective-permute-start | bytes 1179656 | tf_op jit(solution)/shard_map/ppermute | solution.py:252
  112.2 54.8 %collective-permute-start.10 = (bf16[3,1,32,2048]{3,2,1,0:T(8,128)(2,1)S(1)}, bf16[3,1,32,2048]{3,2,1,0:T(8,128)(2,1)}, u32[]{:S(2)}, u32[]{:S(2)}) collective-permute-start(bf16[3,1,32,2048]{3,2,1,0:T(8,128)(2,1)S(1)} %get-tuple-element.81.refs_8_), channel_id=1, source_target_pairs={{0,4},{4,0},{1,5},{5,1},{2,6},{6,2},{3,7},{7,3},{8,12},{12,8},{9,1... | collective-permute-start | bytes 1179656 | tf_op jit(solution)/shard_map/ppermute | solution.py:252
  146.3 2.2 copy-start
  164.6 9.8 %copy-start.15 = (bf16[3,1,32,2048]{3,2,1,0:T(8,128)(2,1)S(1)}, bf16[3,1,32,2048]{3,2,1,0:T(8,128)(2,1)}, u32[]{:S(2)}) copy-start(bf16[3,1,32,2048]{3,2,1,0:T(8,128)(2,1)} %copy-done.14) | copy-start | bytes 1179652
  167.0 25.4 %all-to-all-start.1 = ((f32[16,2,3,2,8,128]{5,4,3,2,1,0:T(8,128)}), f32[16,2,3,2,8,128]{5,4,3,2,1,0:T(8,128)S(1)}, u32[]{:S(2)}, u32[]{:S(2)}) async-start(f32[16,2,3,2,8,128]{5,4,3,2,1,0:T(8,128)} %tied_terms.1), calls=%async_computation.1 | async-start | bytes 1572864 | tf_op jit(solution)/shard_map/all_to_all | solution.py:256
  174.4 32.8 %copy-start.17 = (bf16[3,1,32,2048]{3,2,1,0:T(8,128)(2,1)S(1)}, bf16[3,1,32,2048]{3,2,1,0:T(8,128)(2,1)}, u32[]{:S(2)}) copy-start(bf16[3,1,32,2048]{3,2,1,0:T(8,128)(2,1)} %copy-done.16) | copy-start | bytes 1179652
  174.4 33.3 %copy-start.19 = (bf16[3,1,32,2048]{3,2,1,0:T(8,128)(2,1)S(1)}, bf16[3,1,32,2048]{3,2,1,0:T(8,128)(2,1)}, u32[]{:S(2)}) copy-start(bf16[3,1,32,2048]{3,2,1,0:T(8,128)(2,1)} %copy-done.18) | copy-start | bytes 1179652
  174.5 17.9 %collective-permute-start.11 = (bf16[3,1,32,2048]{3,2,1,0:T(8,128)(2,1)S(1)}, bf16[3,1,32,2048]{3,2,1,0:T(8,128)(2,1)S(1)}, u32[]{:S(2)}, u32[]{:S(2)}) collective-permute-start(bf16[3,1,32,2048]{3,2,1,0:T(8,128)(2,1)S(1)} %copy-done.15), channel_id=1, source_target_pairs={{0,4},{4,0},{1,5},{5,1},{2,6},{6,2},{3,7},{7,3},{8,12},{12,8},{9,1... | collective-permute-start | bytes 1179656 | tf_op jit(solution)/shard_map/ppermute | solution.py:252
  192.4 5.8 %copy-start.20 = (bf16[3,1,32,2048]{3,2,1,0:T(8,128)(2,1)}, bf16[3,1,32,2048]{3,2,1,0:T(8,128)(2,1)S(1)}, u32[]{:S(2)}) copy-start(bf16[3,1,32,2048]{3,2,1,0:T(8,128)(2,1)S(1)} %collective-permute-done.11.refs_13_) | copy-start | bytes 1179652
  192.4 3.2 %collective-permute-start.15 = (f32[2,3,2,8,128]{4,3,2,1,0:T(8,128)S(1)}, f32[2,3,2,8,128]{4,3,2,1,0:T(8,128)S(1)}, u32[]{:S(2)}, u32[]{:S(2)}) collective-permute-start(f32[2,3,2,8,128]{4,3,2,1,0:T(8,128)S(1)} %reduce_sum.27), channel_id=1, source_target_pairs={{0,4},{4,0},{1,5},{5,1},{2,6},{6,2},{3,7},{7,3},{8,12},{12,8},{9,1... | collective-permute-start | bytes 147464 | tf_op jit(solution)/shard_map/ppermute | solution.py:252
  198.2 32.8 %all-to-all-start.2 = ((bf16[16,5,3,8,128]{4,3,2,1,0:T(8,128)(2,1)}), bf16[16,5,3,8,128]{4,3,2,1,0:T(8,128)(2,1)S(1)}, u32[]{:S(2)}, u32[]{:S(2)}) async-start(bf16[16,5,3,8,128]{4,3,2,1,0:T(8,128)(2,1)} %broadcast_in_dim.2), calls=%async_computation.2 | async-start | bytes 983040 | tf_op jit(solution)/shard_map/all_to_all | solution.py:256
  207.2 15.3 %collective-permute-start.16 = (bf16[3,1,32,2048]{3,2,1,0:T(8,128)(2,1)S(1)}, bf16[3,1,32,2048]{3,2,1,0:T(8,128)(2,1)S(1)}, u32[]{:S(2)}, u32[]{:S(2)}) collective-permute-start(bf16[3,1,32,2048]{3,2,1,0:T(8,128)(2,1)S(1)} %copy-done.17), channel_id=1, source_target_pairs={{0,4},{4,0},{1,5},{5,1},{2,6},{6,2},{3,7},{7,3},{8,12},{12,8},{9,1... | collective-permute-start | bytes 1179656 | tf_op jit(solution)/shard_map/ppermute | solution.py:252
  207.7 23.3 %collective-permute-start.17 = (bf16[3,1,32,2048]{3,2,1,0:T(8,128)(2,1)S(1)}, bf16[3,1,32,2048]{3,2,1,0:T(8,128)(2,1)S(1)}, u32[]{:S(2)}, u32[]{:S(2)}) collective-permute-start(bf16[3,1,32,2048]{3,2,1,0:T(8,128)(2,1)S(1)} %copy-done.19), channel_id=1, source_target_pairs={{0,4},{4,0},{1,5},{5,1},{2,6},{6,2},{3,7},{7,3},{8,12},{12,8},{9,1... | collective-permute-start | bytes 1179656 | tf_op jit(solution)/shard_map/ppermute | solution.py:252
  222.6 8.4 %copy-start.23 = (bf16[3,1,32,2048]{3,2,1,0:T(8,128)(2,1)}, bf16[3,1,32,2048]{3,2,1,0:T(8,128)(2,1)S(1)}, u32[]{:S(2)}) copy-start(bf16[3,1,32,2048]{3,2,1,0:T(8,128)(2,1)S(1)} %collective-permute-done.16.refs_14_) | copy-start | bytes 1179652
  231.0 0.8 copy-start.24
  231.8 79.5 %all-to-all-start.3 = ((bf16[16,6,32,768]{3,2,1,0:T(8,128)(2,1)}), bf16[16,6,32,768]{3,2,1,0:T(8,128)(2,1)}, u32[]{:S(2)}, u32[]{:S(2)}) async-start(bf16[16,6,32,768]{3,2,1,0:T(8,128)(2,1)} %copy-done), calls=%async_computation.3 | async-start | bytes 9437184 | tf_op jit(solution)/shard_map/all_to_all | solution.py:256
  248.0 53.2 %collective-permute-start.18 = (bf16[3,3,32,2048]{3,2,1,0:T(8,128)(2,1)}, bf16[3,3,32,2048]{3,2,1,0:T(8,128)(2,1)S(1)}, u32[]{:S(2)}, u32[]{:S(2)}) collective-permute-start(bf16[3,3,32,2048]{3,2,1,0:T(8,128)(2,1)} %get-tuple-element.94), channel_id=1, source_target_pairs={{0,3},{1,0},{2,1},{3,2},{4,7},{5,4},{6,5},{7,6},{8,11},{9,8},{10,9... | collective-permute-start | bytes 3538952 | tf_op jit(solution)/shard_map/ppermute | solution.py:252
  250.5 50.7 %collective-permute-start.19 = (bf16[3,3,32,2048]{3,2,1,0:T(8,128)(2,1)}, bf16[3,3,32,2048]{3,2,1,0:T(8,128)(2,1)S(1)}, u32[]{:S(2)}, u32[]{:S(2)}) collective-permute-start(bf16[3,3,32,2048]{3,2,1,0:T(8,128)(2,1)} %get-tuple-element.95), channel_id=1, source_target_pairs={{0,2},{1,3},{2,0},{3,1},{4,6},{5,7},{6,4},{7,5},{8,10},{9,11},{10,... | collective-permute-start | bytes 3538952 | tf_op jit(solution)/shard_map/ppermute | solution.py:252
  251.1 54.4 %collective-permute-start.20 = (bf16[3,3,32,2048]{3,2,1,0:T(8,128)(2,1)}, bf16[3,3,32,2048]{3,2,1,0:T(8,128)(2,1)S(1)}, u32[]{:S(2)}, u32[]{:S(2)}) collective-permute-start(bf16[3,3,32,2048]{3,2,1,0:T(8,128)(2,1)} %get-tuple-element.96), channel_id=1, source_target_pairs={{0,1},{1,2},{2,3},{3,0},{4,5},{5,6},{6,7},{7,4},{8,9},{9,10},{10,1... | collective-permute-start | bytes 3538952 | tf_op jit(solution)/shard_map/ppermute | solution.py:252
  305.4 1.3 copy-start.9
  (2 other events, 1.5 us)

commit v3 on v2

--- a/solution.py
+++ b/solution.py
@@ -12,7 +12,6 @@
 H = 12
 HD = 64
 PAIR = 2 * HD
-WIDE = 3 * PAIR
 LOG2E = 1.4426950408889634
 ROWS = ("z", "yh", "core")
 VMEM = 48 * 1024 * 1024
@@ -75,7 +74,7 @@
         o_ref[:, i] = grad.astype(jnp.bfloat16).reshape(groups, rows, width)
 
 
-def column_backward(x, pieces, chunk=256):
+def column_backward(x, pieces, chunk=512):
     groups, _, rows, features = x.shape
     pairs, total = features // PAIR, groups * rows
     return pl.pallas_call(
@@ -182,69 +181,77 @@
     return jnp.concatenate([ref[0, i] for ref in refs], axis=0)
 
 
-def logits_kernel(*refs, parts, slices):
-    own, other, keys, values = (refs[i * parts : (i + 1) * parts] for i in range(4))
+def terms_kernel(*refs, parts):
+    left, keys, values = (refs[i * parts : (i + 1) * parts] for i in range(3))
     o_ref = refs[-1]
-    for i in range(2):
-        right = joined(values if i else keys, 0)
-        for side, left in enumerate((own, other)):
-            terms = nt(joined(left, i), right)
-            o_ref[:, i, 0, side] = terms.reshape(slices, terms.shape[0] // slices, -1)
-
-
-def tied_terms(own, other, keys, values, slices):
-    parts = len(own)
-    heads, _, columns, width = own[0].shape
+    for i, right in enumerate((keys, values)):
+        terms = nt(joined(left, i), joined(right, 0))
+        o_ref[:, i, 0, 0] = terms.reshape(o_ref.shape[0], -1, terms.shape[1])
+
+
+def tied_terms(left, keys, values, slices, side, held=()):
+    parts = len(left)
+    heads, _, columns, width = left[0].shape
     wide = parts * columns
     step = wide // slices
     return pl.pallas_call(
-        functools.partial(logits_kernel, parts=parts, slices=slices),
+        functools.partial(terms_kernel, parts=parts),
         grid=(heads,),
-        in_specs=[pl.BlockSpec((1, 2, columns, width), lambda i: (i, 0, 0, 0))] * (2 * parts)
-        + [pl.BlockSpec((1, 1, columns, width), lambda i: (i, 0, 0, 0))] * (2 * parts),
-        out_specs=pl.BlockSpec((slices, 2, 1, 2, step, wide), lambda i: (0, 0, i, 0, 0, 0)),
+        in_specs=[pl.BlockSpec((1, 2, columns, width), lambda i: (i, 0, 0, 0))] * parts
+        + [pl.BlockSpec((1, 1, columns, width), lambda i: (i, 0, 0, 0))] * (2 * parts)
+        + [pl.BlockSpec(memory_space=pl.ANY)] * len(held),
+        out_specs=pl.BlockSpec(
+            (slices, 2, 1, 1, step, wide), lambda i: (0, 0, i, side, 0, 0)
+        ),
         out_shape=jax.ShapeDtypeStruct((slices, 2, heads, 2, step, wide), jnp.float32),
+        input_output_aliases={3 * parts: 0} if held else {},
         compiler_params=params(VMEM_ALL),
         cost_estimate=COST,
         name="tied_terms",
-    )(*own, *other, *keys, *values)
-
-
-def grads_kernel(*refs, parts, factor):
-    own, other, keys, other_keys = (refs[i * parts : (i + 1) * parts] for i in range(4))
-    tied_ref, outs = refs[4 * parts], refs[4 * parts + 1 :]
-    s_own, w_own, s_right, s_below, w_below = (tied_ref[i, 0] for i in range(5))
-    s_query = jnp.concatenate([s_own, s_right], axis=1)
+    )(*left, *keys, *values, *held)
+
+
+def pair_grads_kernel(*refs, parts, factor):
+    own, other, (tied_ref, *outs) = refs[:parts], refs[parts : 2 * parts], refs[2 * parts :]
+    s_own, w_own, _, s_below, w_below = (tied_ref[i, 0] for i in range(5))
     s_key = jnp.concatenate([s_own, s_below], axis=0)
     w_value = jnp.concatenate([w_own, w_below], axis=0)
     results = (
-        nn(s_query, jnp.concatenate([joined(keys, 0), joined(other_keys, 0)], axis=0)) * factor,
         tn(s_key, jnp.concatenate([joined(own, 0), joined(other, 0)], axis=0)) * factor,
         tn(w_value, jnp.concatenate([joined(own, 1), joined(other, 1)], axis=0)),
     )
     for i, result in enumerate(results):
         result = result.astype(jnp.bfloat16)
-        for s, out in enumerate(outs):
-            out[0, i] = result[s * out.shape[2] : (s + 1) * out.shape[2]]
-
-
-def tied_grads(own, other, keys, other_keys, tied, factor):
+        for s, out in enumerate(outs[i * parts : (i + 1) * parts]):
+            out[0, 0] = result[s * out.shape[2] : (s + 1) * out.shape[2]]
+
+
+def query_grads_kernel(*refs, parts, factor):
+    keys, other_keys, (tied_ref, *outs) = refs[:parts], refs[parts : 2 * parts], refs[2 * parts :]
+    s_query = jnp.concatenate([tied_ref[0, 0], tied_ref[2, 0]], axis=1)
+    result = nn(s_query, jnp.concatenate([joined(keys, 0), joined(other_keys, 0)], axis=0))
+    result = (result * factor).astype(jnp.bfloat16)
+    for s, out in enumerate(outs):
+        out[0, 0] = result[s * out.shape[2] : (s + 1) * out.shape[2]]
+
+
+def tied_grads(kernel, own, other, tied, factor, name):
     parts = len(own)
-    heads, _, columns, width = own[0].shape
+    heads, n, columns, width = own[0].shape
     wide = parts * columns
-    two = pl.BlockSpec((1, 2, columns, width), lambda i: (i, 0, 0, 0))
+    chunk = pl.BlockSpec((1, n, columns, width), lambda i: (i, 0, 0, 0))
     one = pl.BlockSpec((1, 1, columns, width), lambda i: (i, 0, 0, 0))
     square = pl.BlockSpec((5, 1, wide, wide), lambda i: (0, i, 0, 0))
     return pl.pallas_call(
-        functools.partial(grads_kernel, parts=parts, factor=factor),
+        functools.partial(kernel, parts=parts, factor=factor),
         grid=(heads,),
-        in_specs=[two] * (2 * parts) + [one] * (2 * parts) + [square],
-        out_specs=[pl.BlockSpec((1, 3, columns, width), lambda i: (i, 0, 0, 0))] * parts,
-        out_shape=[jax.ShapeDtypeStruct((heads, 3, columns, width), jnp.bfloat16)] * parts,
+        in_specs=[chunk] * (2 * parts) + [square],
+        out_specs=[one] * (n * parts),
+        out_shape=[jax.ShapeDtypeStruct((heads, 1, columns, width), jnp.bfloat16)] * (n * parts),
         compiler_params=params(VMEM_ALL),
         cost_estimate=COST,
-        name="tied_grads",
-    )(*own, *other, *keys, *other_keys, tied)
+        name=name,
+    )(*own, *other, tied)
 
 
 def shift(x, axis, by):
@@ -282,11 +289,11 @@
     n = len(arrays)
     return pl.pallas_call(
         column_pack_kernel,
-        grid=(pieces, features // WIDE),
-        in_specs=[pl.BlockSpec((rows, groups, WIDE), lambda p, i: (0, p, i))] * n,
-        out_specs=pl.BlockSpec((groups, n, rows, WIDE), lambda p, i: (0, p, 0, i)),
+        grid=(pieces,),
+        in_specs=[pl.BlockSpec((rows, groups, features), lambda p: (0, p, 0))] * n,
+        out_specs=pl.BlockSpec((groups, n, rows, features), lambda p: (0, p, 0, 0)),
         out_shape=jax.ShapeDtypeStruct((groups, n * pieces, rows, features), jnp.bfloat16),
-        compiler_params=params(),
+        compiler_params=params(VMEM_ALL),
         cost_estimate=COST,
         name="column_pack",
     )(*arrays)
@@ -304,9 +311,9 @@
     n = parts // pieces
     return pl.pallas_call(
         column_unpack_kernel,
-        grid=(pieces, features // WIDE),
-        in_specs=[pl.BlockSpec((groups, n, rows, WIDE), lambda p, i: (0, p, 0, i))],
-        out_specs=[pl.BlockSpec((rows, groups, WIDE), lambda p, i: (0, p, i))] * n,
+        grid=(pieces,),
+        in_specs=[pl.BlockSpec((groups, n, rows, features), lambda p: (0, p, 0, 0))],
+        out_specs=[pl.BlockSpec((rows, groups, features), lambda p: (0, p, 0))] * n,
         out_shape=[jax.ShapeDtypeStruct((rows, pieces * groups, features), jnp.bfloat16)] * n,
         compiler_params=params(),
         cost_estimate=COST,
@@ -337,16 +344,22 @@
     keys = spread(pack_rows(here, parts, row_arrays[2]))
     values = spread(pack_rows(here, parts, row_arrays[3]))
     other = [shift(c, "yl", 1) for c in own]
-    col_done = column_backward(col_in, pieces)
-
-    other_keys = [shift(c, "yl", 1) for c in after(keys[:2], other[-2])]
-    terms = tied_terms(*after((own, other, keys, values), col_done), groups)
+    half = tied_terms(own, keys, values, groups, 0)
+    col_done = column_backward(after(col_in, half), pieces)
+
+    def across(keys, *others):
+        return [shift(c, "yl", 1) for c in after(keys, others)]
+
+    other_keys = across(keys[:2], other[-2])
+    left, half = after((other, half), col_done)
+    terms = tied_terms(left, keys, values, groups, 1, (half,))
     terms = over_rows(after(terms, other_keys[0]))
-    sums = jnp.sum(after(terms, other_keys), axis=0)
-    across = shift(sums, "yl", 1)
-    other_keys += [shift(c, "yl", 1) for c in after(keys[2:], across)]
-
-    logits, dprobs = jnp.concatenate([sums, jnp.flip(across, 2)], axis=-1)
+    sums = jnp.sum(after(terms, other_keys[1]), axis=0)
+    swapped = shift(sums, "yl", 1)
+    late = across([jnp.concatenate(keys[2:])], swapped)[0]
+    other_keys += [late[at : at + head_group] for at in range(0, late.shape[0], head_group)]
+
+    logits, dprobs = jnp.concatenate([sums, jnp.flip(swapped, 2)], axis=-1)
     probs = jax.nn.softmax(logits * row_factor, axis=-1)
     slopes = probs * (dprobs - jnp.sum(probs * dprobs, axis=-1, keepdims=True))
     probs, slopes = probs.astype(jnp.bfloat16), slopes.astype(jnp.bfloat16)
@@ -361,11 +374,18 @@
         ]
     )
     whole = over_rows(jnp.broadcast_to(payload[None], (groups,) + payload.shape))
-    col_grads = column_unpack(over_rows(after(col_done, whole, other_keys)), pieces)
     whole = jnp.transpose(whole, (1, 2, 0, 3, 4)).reshape(5, head_group, wide, wide)
-    grads = tied_grads(own, other, keys, other_keys, whole, row_factor)
-    chunks = [grads[0]] + [shift(grads[s], "x", parts - s) for s in range(1, parts)]
-    row_grads = unpack_rows(here, chunks)
+    def back(chunks):
+        return [chunks[0]] + [shift(chunks[s], "x", parts - s) for s in range(1, parts)]
+
+    pair_grads = tied_grads(pair_grads_kernel, own, other, whole, row_factor, "pair_grads")
+    key_chunks, value_chunks = back(pair_grads[:parts]), back(pair_grads[parts:])
+    col_grads = column_unpack(over_rows(after(col_done, whole, late)), pieces)
+    keys = after(keys, value_chunks[1])
+    query_grads = tied_grads(query_grads_kernel, keys, other_keys, whole, row_factor, "query_grads")
+    chunks = (back(query_grads), key_chunks, value_chunks)
+    row_grads = [unpack_rows(here, c)[0] for c in chunks]
+
     return (*row_grads, *col_grads)
 
 

time: 318 us -> 297 us (0.934)
  waiting for transfers between devices: 175 us -> 138 us
  blocking collectives: 0 us -> 25.3 us
  starting transfers between devices: 58.4 us -> 50.8 us
  local copies, waits for them, and re-layouts: 11.8 us -> 6.46 us
    ppermute x21 -> x26, waiting for transfers between devices: 175 us -> 138 us  [shift(): return lax.ppermute(x, axis, [(i, (i + by) % n) for i in range(n)])]
    all_to_all x0 -> x1, blocking collectives: none -> 25.3 us  [over_rows(): return lax.all_to_all(x, ROWS, split_axis=0, concat_axis=0, tiled=True)]
    all_to_all x4 -> x3, starting transfers between devices: 34.1 us -> 22.7 us  [over_rows(): return lax.all_to_all(x, ROWS, split_axis=0, concat_axis=0, tiled=True)]
    unnamed x54 -> x52, local copies, waits for them, and re-layouts: 9.97 us -> 4.52 us
    pallas_call x4 -> x6, Pallas kernels: 25.6 us -> 29.8 us  [the longest x2 10 us: tied_grads(): pl.pallas_call(functools.partial(kernel, parts=parts, factor=factor), gri...]
    pallas_call x1, Pallas kernels: 33.6 us -> 29.5 us  [column_backward(): pl.pallas_call(functools.partial(column_kernel, chunk=chunk), grid=(piece...]
    ppermute x21 -> x26, starting transfers between devices: 24.3 us -> 28.1 us  [shift(): return lax.ppermute(x, axis, [(i, (i + by) % n) for i in range(n)])]
    pallas_call x1 -> x3, Pallas kernels: 4.55 us -> 7.7 us  [unpack_rows(): pl.pallas_call(functools.partial(unpack_kernel, parts=parts), in_specs=[p...]
  transfers between devices with their start and end apart: 25 -> 29, of which waited for: 13 -> 16; matrix products, arithmetic and copies ran while one was open for 0% -> 1% of each run, Pallas kernels for 18% -> 21%
where the time goes in v3:
time: 297 us; the launch traced here: 296 us
  waiting for transfers between devices  138 us (46%)
  Pallas kernels  73.1 us (25%)
  starting transfers between devices  50.8 us (17%)
  blocking collectives  25.3 us (9%)
  local copies, waits for them, and re-layouts  6.46 us (2%)
    ppermute x26, waiting for transfers between devices, shift(): return lax.ppermute(x, axis, [(i, (i + by) % n) for i in range(n)])  138 us
    pallas_call x1, Pallas kernels, column_backward(): pl.pallas_call(functools.partial(column_kernel, chunk=chunk), grid=(piece...  29.5 us
    ppermute x26, starting transfers between devices, shift(): return lax.ppermute(x, axis, [(i, (i + by) % n) for i in range(n)])  28.1 us
    all_to_all x1, blocking collectives, over_rows(): return lax.all_to_all(x, ROWS, split_axis=0, concat_axis=0, tiled=True)  25.3 us
    all_to_all x3, starting transfers between devices, over_rows(): return lax.all_to_all(x, ROWS, split_axis=0, concat_axis=0, tiled=True)  22.7 us
    pallas_call x2, Pallas kernels, tied_grads(): pl.pallas_call(functools.partial(kernel, parts=parts, factor=factor), gri...  10 us
    pallas_call x2, Pallas kernels, tied_terms(): pl.pallas_call(functools.partial(terms_kernel, parts=parts), grid=(heads,...  9.51 us
    pallas_call x3, Pallas kernels, unpack_rows(): pl.pallas_call(functools.partial(unpack_kernel, parts=parts), in_specs=[p...  7.7 us
  transfers between devices with their start and end apart: 29, of which 16 were waited for; matrix products, arithmetic and copies ran while one was open for 1% of the time, Pallas kernels for 21%

profile of v3, /device:TPU:1, one launch (start us, length us, event | category | flops | bytes accessed | tf_op | source)
XLA Modules:
  0.0 296.0 jit_solution(8625212706655091685)
XLA Ops:
  0.6 5.6 %column_pack.1 = bf16[16,8,32,768]{3,2,1,0:T(8,128)(2,1)} custom-call(bf16[32,32,768]{2,1,0:T(8,128)(2,1)} %refs_0_.1, bf16[32,32,768]{2,1,0:T(8,128)(2,1)} %refs_1_.1, bf16[32,32,768]{2,1,0:T(8,128)(2,1)} %refs_2_.1, bf16[32,32,768]{2,1,0:T(8,128)(2,1)} %refs_3_.1), custom_call_target="tpu_custom_call" | custom-call | flops 1 | bytes 1 | tf_op jit(solution)/shard_map/column_pack/pallas_call | solution.py:290
  6.2 9.6 %all-to-all-start = ((bf16[16,8,32,768]{3,2,1,0:T(8,128)(2,1)}), bf16[16,8,32,768]{3,2,1,0:T(8,128)(2,1)}, u32[]{:S(2)}, u32[]{:S(2)}) async-start(bf16[16,8,32,768]{3,2,1,0:T(8,128)(2,1)} %column_pack.1), calls=%async_computation | async-start | bytes 12582912 | tf_op jit(solution)/shard_map/all_to_all | solution.py:263
  15.8 3.0 %pack_rows.4 = (bf16[3,2,32,2048]{3,2,1,0:T(8,128)(2,1)S(1)}, bf16[3,2,32,2048]{3,2,1,0:T(8,128)(2,1)S(1)}, bf16[3,2,32,2048]{3,2,1,0:T(8,128)(2,1)S(1)}, bf16[3,2,32,2048]{3,2,1,0:T(8,128)(2,1)S(1)}) custom-call(s32[1]{0:T(128)} %bitcast.here_ref, bf16[32,32,768]{2,1,0:T(8,128)(2,1)S(1)} %copy-done.6, bf16[32,32,768]{2,1,0:T(8,128)(2,1)} %refs_1_.2), custom_call_target="tpu_custom_call" | custom-call | flops 1 | bytes 1 | tf_op jit(solution)/shard_map/pack_rows/pallas_call | solution.py:121
  18.8 2.8 collective-permute-start.4
  21.7 1.6 pack_rows.3
  24.3 1.7 collective-permute-start.1
  27.5 21.3 %collective-permute-done.refs_5_.refs_1_ = bf16[3,1,32,2048]{3,2,1,0:T(8,128)(2,1)S(1)} collective-permute-done((bf16[3,1,32,2048]{3,2,1,0:T(8,128)(2,1)S(1)}, bf16[3,1,32,2048]{3,2,1,0:T(8,128)(2,1)S(1)}, u32[]{:S(2)}, u32[]{:S(2)}) %collective-permute-start) | collective-permute-done | bytes 393248 | tf_op jit(solution)/shard_map/ppermute | solution.py:259
  48.9 1.6 pack_rows.5
  51.2 5.1 %collective-permute-done.1.refs_6_.refs_2_ = bf16[3,1,32,2048]{3,2,1,0:T(8,128)(2,1)S(1)} collective-permute-done((bf16[3,1,32,2048]{3,2,1,0:T(8,128)(2,1)S(1)}, bf16[3,1,32,2048]{3,2,1,0:T(8,128)(2,1)S(1)}, u32[]{:S(2)}, u32[]{:S(2)}) %collective-permute-start.1) | collective-permute-done | bytes 393248 | tf_op jit(solution)/shard_map/ppermute | solution.py:259
  56.9 2.9 collective-permute-start.11
  59.7 22.8 %collective-permute-done.10.refs_9_ = bf16[3,1,32,2048]{3,2,1,0:T(8,128)(2,1)S(1)} collective-permute-done((bf16[3,1,32,2048]{3,2,1,0:T(8,128)(2,1)S(1)}, bf16[3,1,32,2048]{3,2,1,0:T(8,128)(2,1)S(1)}, u32[]{:S(2)}, u32[]{:S(2)}) %collective-permute-start.10) | collective-permute-done | bytes 393248 | tf_op jit(solution)/shard_map/ppermute | solution.py:259
  82.5 7.6 %collective-permute-done.11.refs_10_ = bf16[3,1,32,2048]{3,2,1,0:T(8,128)(2,1)S(1)} collective-permute-done((bf16[3,1,32,2048]{3,2,1,0:T(8,128)(2,1)S(1)}, bf16[3,1,32,2048]{3,2,1,0:T(8,128)(2,1)S(1)}, u32[]{:S(2)}, u32[]{:S(2)}) %collective-permute-start.11) | collective-permute-done | bytes 393248 | tf_op jit(solution)/shard_map/ppermute | solution.py:259
  90.6 1.1 collective-permute-start.7
  93.7 4.8 %tied_terms.2.refs_12_ = f32[16,2,3,2,8,128]{5,4,3,2,1,0:T(8,128)} custom-call(bf16[3,2,32,2048]{3,2,1,0:T(8,128)(2,1)} %copy-done.3, bf16[3,2,32,2048]{3,2,1,0:T(8,128)(2,1)} %collective-permute-done.3.refs_1_, bf16[3,2,32,2048]{3,2,1,0:T(8,128)(2,1)} %copy-done.17, bf16[3,2,32,2048]{3,2,1,0:T(8,128)(2,1)} %collective-permute-done.5.refs_3_, ...), custom_call_target="tpu_custom_call" | custom-call | flops 1 | bytes 1 | tf_op jit(solution)/shard_map/tied_terms/pallas_call | solution.py:197
  98.5 4.7 %collective-permute-done.8.refs_2_.refs_6_ = bf16[3,2,32,2048]{3,2,1,0:T(8,128)(2,1)} collective-permute-done((bf16[3,2,32,2048]{3,2,1,0:T(8,128)(2,1)S(1)}, bf16[3,2,32,2048]{3,2,1,0:T(8,128)(2,1)}, u32[]{:S(2)}, u32[]{:S(2)}) %collective-permute-start.8) | collective-permute-done | bytes 786464 | tf_op jit(solution)/shard_map/ppermute | solution.py:259
  103.2 1.1 collective-permute-start.13
  104.3 29.5 %column_attention.1 = bf16[16,6,32,768]{3,2,1,0:T(8,128)(2,1)S(1)} custom-call(bf16[16,8,32,768]{3,2,1,0:T(8,128)(2,1)} %all-to-all-done.x_ref), custom_call_target="tpu_custom_call" | custom-call | flops 8053063680 | bytes 11010048 | tf_op jit(solution)/shard_map/column_attention/pallas_call | solution.py:80
  133.7 2.1 copy-done
  135.9 1.0 collective-permute-done.7.refs_1_.refs_5_
  136.9 16.9 %collective-permute-done.9.refs_3_.refs_7_ = bf16[3,2,32,2048]{3,2,1,0:T(8,128)(2,1)} collective-permute-done((bf16[3,2,32,2048]{3,2,1,0:T(8,128)(2,1)}, bf16[3,2,32,2048]{3,2,1,0:T(8,128)(2,1)}, u32[]{:S(2)}, u32[]{:S(2)}) %collective-permute-start.9) | collective-permute-done | bytes 786464 | tf_op jit(solution)/shard_map/ppermute | solution.py:259
  153.7 4.7 %tied_terms.3 = f32[16,2,3,2,8,128]{5,4,3,2,1,0:T(8,128)} custom-call(bf16[3,2,32,2048]{3,2,1,0:T(8,128)(2,1)} %collective-permute-done.6.refs_0_.refs_4_, bf16[3,2,32,2048]{3,2,1,0:T(8,128)(2,1)} %collective-permute-done.7.refs_1_.refs_5_, bf16[3,2,32,2048]{3,2,1,0:T(8,128)(2,1)} %collective-permute-done.8.refs_2_.refs_6_, ...), custom_call_target="tpu_custom_call", output_to_operand_aliasing={{}: (12, {})} | custom-call | flops 1 | bytes 1 | tf_op jit(solution)/shard_map/tied_terms/pallas_call | solution.py:197
  158.4 3.6 %collective-permute-done.13.refs_4_ = bf16[3,1,32,2048]{3,2,1,0:T(8,128)(2,1)S(1)} collective-permute-done((bf16[3,1,32,2048]{3,2,1,0:T(8,128)(2,1)S(1)}, bf16[3,1,32,2048]{3,2,1,0:T(8,128)(2,1)S(1)}, u32[]{:S(2)}, u32[]{:S(2)}) %collective-permute-start.13) | collective-permute-done | bytes 393248 | tf_op jit(solution)/shard_map/ppermute | solution.py:259
  162.1 7.4 %all-to-all-start.1 = ((f32[16,2,3,2,8,128]{5,4,3,2,1,0:T(8,128)}), f32[16,2,3,2,8,128]{5,4,3,2,1,0:T(8,128)S(1)}, u32[]{:S(2)}, u32[]{:S(2)}) async-start(f32[16,2,3,2,8,128]{5,4,3,2,1,0:T(8,128)} %tied_terms.3), calls=%async_computation.1 | async-start | bytes 1572864 | tf_op jit(solution)/shard_map/all_to_all | solution.py:263
  169.6 17.9 %collective-permute-done.14.refs_5_ = bf16[3,1,32,2048]{3,2,1,0:T(8,128)(2,1)S(1)} collective-permute-done((bf16[3,1,32,2048]{3,2,1,0:T(8,128)(2,1)S(1)}, bf16[3,1,32,2048]{3,2,1,0:T(8,128)(2,1)S(1)}, u32[]{:S(2)}, u32[]{:S(2)}) %collective-permute-start.14) | collective-permute-done | bytes 393248 | tf_op jit(solution)/shard_map/ppermute | solution.py:259
  187.5 1.7 collective-permute-start.15
  189.3 1.4 collective-permute-done.15
  190.7 1.5 collective-permute-start.17
  192.3 1.4 fusion.27
  194.0 25.3 %all_to_all.20 = bf16[16,5,3,8,128]{4,3,2,1,0:T(8,128)(2,1)S(1)} all-to-all(bf16[16,5,3,8,128]{4,3,2,1,0:T(8,128)(2,1)S(1)} %broadcast_in_dim.2), channel_id=1, replica_groups=mesh['z'=4,'yh'=2,'core'=2,'yl'=2,'x'=4] {'z','yh','core'}, dimensions={0} | all-to-all | bytes 983040 | tf_op jit(solution)/shard_map/all_to_all | solution.py:263
  219.2 0.9 copy_bitcast_fusion.refs_8_
  220.2 5.7 %all-to-all-start.3 = ((bf16[16,6,32,768]{3,2,1,0:T(8,128)(2,1)}), bf16[16,6,32,768]{3,2,1,0:T(8,128)(2,1)}, u32[]{:S(2)}, u32[]{:S(2)}) async-start(bf16[16,6,32,768]{3,2,1,0:T(8,128)(2,1)} %copy-done), calls=%async_computation.3 | async-start | bytes 9437184 | tf_op jit(solution)/shard_map/all_to_all | solution.py:263
  225.8 5.6 %pair_grads.1 = (bf16[3,1,32,2048]{3,2,1,0:T(8,128)(2,1)}, bf16[3,1,32,2048]{3,2,1,0:T(8,128)(2,1)}, bf16[3,1,32,2048]{3,2,1,0:T(8,128)(2,1)}, bf16[3,1,32,2048]...) custom-call(bf16[3,2,32,2048]{3,2,1,0:T(8,128)(2,1)} %copy-done.3, ...), custom_call_target="tpu_custom_call" | custom-call | flops 1 | bytes 1 | tf_op jit(solution)/shard_map/pair_grads/pallas_call | solution.py:245
  231.4 2.5 collective-permute-start.16
  235.1 2.1 collective-permute-start.21
  237.1 1.2 collective-permute-start.22
  238.4 1.0 fusion.26
  239.3 10.9 %collective-permute-done.16.refs_1_ = bf16[3,1,32,2048]{3,2,1,0:T(8,128)(2,1)S(1)} collective-permute-done((bf16[3,1,32,2048]{3,2,1,0:T(8,128)(2,1)}, bf16[3,1,32,2048]{3,2,1,0:T(8,128)(2,1)S(1)}, u32[]{:S(2)}, u32[]{:S(2)}) %collective-permute-start.16) | collective-permute-done | bytes 393248 | tf_op jit(solution)/shard_map/ppermute | solution.py:259
  250.3 4.5 %query_grads.1 = (bf16[3,1,32,2048]{3,2,1,0:T(8,128)(2,1)}, bf16[3,1,32,2048]{3,2,1,0:T(8,128)(2,1)}, bf16[3,1,32,2048]{3,2,1,0:T(8,128)(2,1)}, bf16[3,1,32,2048]{3,2,1,0:T(8,128)(2,1)}) custom-call(bf16[3,1,32,2048]{3,2,1,0:T(8,128)(2,1)} %copy-done.1, bf16[3,1,32,2048]{3,2,1,0:T(8,128)(2,1)} %copy-done.15, bf16[3,1,32,2048]{3,2,1,0:T(8,128)(2,1)} %copy-done.11, ...), custom_call_target="tpu_custom_call" | custom-call | flops 1 | bytes 1 | tf_op jit(solution)/shard_map/query_grads/pallas_call | solution.py:245
  254.7 4.0 %collective-permute-start.18 = (bf16[3,1,32,2048]{3,2,1,0:T(8,128)(2,1)}, bf16[3,1,32,2048]{3,2,1,0:T(8,128)(2,1)S(1)}, u32[]{:S(2)}, u32[]{:S(2)}) collective-permute-start(bf16[3,1,32,2048]{3,2,1,0:T(8,128)(2,1)} %get-tuple-element.86), channel_id=1, source_target_pairs={{0,3},{1,0},{2,1},{3,2},{4,7},{5,4},{6,5},{7,6},{8,11},{9,8},{10,9... | collective-permute-start | bytes 1179656 | tf_op jit(solution)/shard_map/ppermute | solution.py:259
  258.7 1.3 collective-permute-start.19
  260.0 7.1 %collective-permute-done.21.refs_1_ = bf16[3,1,32,2048]{3,2,1,0:T(8,128)(2,1)S(1)} collective-permute-done((bf16[3,1,32,2048]{3,2,1,0:T(8,128)(2,1)}, bf16[3,1,32,2048]{3,2,1,0:T(8,128)(2,1)S(1)}, u32[]{:S(2)}, u32[]{:S(2)}) %collective-permute-start.21) | collective-permute-done | bytes 393248 | tf_op jit(solution)/shard_map/ppermute | solution.py:259
  267.1 2.6 unpack_rows.5
  269.7 3.1 %collective-permute-done.23.refs_3_ = bf16[3,1,32,2048]{3,2,1,0:T(8,128)(2,1)S(1)} collective-permute-done((bf16[3,1,32,2048]{3,2,1,0:T(8,128)(2,1)S(1)}, bf16[3,1,32,2048]{3,2,1,0:T(8,128)(2,1)S(1)}, u32[]{:S(2)}, u32[]{:S(2)}) %collective-permute-start.23) | collective-permute-done | bytes 393248 | tf_op jit(solution)/shard_map/ppermute | solution.py:259
  272.7 2.6 unpack_rows.4
  275.3 9.2 %collective-permute-done.18.refs_1_ = bf16[3,1,32,2048]{3,2,1,0:T(8,128)(2,1)S(1)} collective-permute-done((bf16[3,1,32,2048]{3,2,1,0:T(8,128)(2,1)}, bf16[3,1,32,2048]{3,2,1,0:T(8,128)(2,1)S(1)}, u32[]{:S(2)}, u32[]{:S(2)}) %collective-permute-start.18) | collective-permute-done | bytes 393248 | tf_op jit(solution)/shard_map/ppermute | solution.py:259
  284.5 4.2 %collective-permute-done.20.refs_3_ = bf16[3,1,32,2048]{3,2,1,0:T(8,128)(2,1)S(1)} collective-permute-done((bf16[3,1,32,2048]{3,2,1,0:T(8,128)(2,1)}, bf16[3,1,32,2048]{3,2,1,0:T(8,128)(2,1)S(1)}, u32[]{:S(2)}, u32[]{:S(2)}) %collective-permute-start.20) | collective-permute-done | bytes 393248 | tf_op jit(solution)/shard_map/ppermute | solution.py:259
  288.7 2.6 unpack_rows.3
  291.3 4.7 %column_unpack.1 = (bf16[32,32,768]{2,1,0:T(8,128)(2,1)}, bf16[32,32,768]{2,1,0:T(8,128)(2,1)}, bf16[32,32,768]{2,1,0:T(8,128)(2,1)}) custom-call(bf16[16,6,32,768]{3,2,1,0:T(8,128)(2,1)} %all-to-all-done.3.x_ref), custom_call_target="tpu_custom_call" | custom-call | flops 1 | bytes 1 | tf_op jit(solution)/shard_map/column_unpack/pallas_call | solution.py:312
  (88 shorter events, 7.9 us)
Async XLA Ops:
  6.2 9.6 %copy-start.6 = (bf16[32,32,768]{2,1,0:T(8,128)(2,1)S(1)}, bf16[32,32,768]{2,1,0:T(8,128)(2,1)}, u32[]{:S(2)}) copy-start(bf16[32,32,768]{2,1,0:T(8,128)(2,1)} %refs_0_.3) | copy-start | bytes 4718596
  6.2 98.0 %all-to-all-start = ((bf16[16,8,32,768]{3,2,1,0:T(8,128)(2,1)}), bf16[16,8,32,768]{3,2,1,0:T(8,128)(2,1)}, u32[]{:S(2)}, u32[]{:S(2)}) async-start(bf16[16,8,32,768]{3,2,1,0:T(8,128)(2,1)} %column_pack.1), calls=%async_computation | async-start | bytes 12582912 | tf_op jit(solution)/shard_map/all_to_all | solution.py:263
  15.8 5.9 %copy-start.4 = (bf16[32,32,768]{2,1,0:T(8,128)(2,1)S(1)}, bf16[32,32,768]{2,1,0:T(8,128)(2,1)}, u32[]{:S(2)}) copy-start(bf16[32,32,768]{2,1,0:T(8,128)(2,1)} %refs_0_.2) | copy-start | bytes 4718596
  18.8 71.3 %copy-start.3 = (bf16[3,2,32,2048]{3,2,1,0:T(8,128)(2,1)}, bf16[3,2,32,2048]{3,2,1,0:T(8,128)(2,1)S(1)}, u32[]{:S(2)}) copy-start(bf16[3,2,32,2048]{3,2,1,0:T(8,128)(2,1)S(1)} %get-tuple-element.60.refs_0_) | copy-start | bytes 2359300
  18.8 30.0 %copy-start.5 = (bf16[32,32,768]{2,1,0:T(8,128)(2,1)S(1)}, bf16[32,32,768]{2,1,0:T(8,128)(2,1)}, u32[]{:S(2)}) copy-start(bf16[32,32,768]{2,1,0:T(8,128)(2,1)} %refs_0_.4) | copy-start | bytes 4718596
  18.8 37.5 %collective-permute-start.4 = (bf16[3,2,32,2048]{3,2,1,0:T(8,128)(2,1)S(1)}, bf16[3,2,32,2048]{3,2,1,0:T(8,128)(2,1)S(1)}, u32[]{:S(2)}, u32[]{:S(2)}) collective-permute-start(bf16[3,2,32,2048]{3,2,1,0:T(8,128)(2,1)S(1)} %get-tuple-element.62), channel_id=1, source_target_pairs={{0,2},{1,3},{2,0},{3,1},{4,6},{5,7},{6,4},{7,5},{8,10},{9,11},{10,... | collective-permute-start | bytes 2359304 | tf_op jit(solution)/shard_map/ppermute | solution.py:259
  24.0 24.9 %collective-permute-start = (bf16[3,1,32,2048]{3,2,1,0:T(8,128)(2,1)S(1)}, bf16[3,1,32,2048]{3,2,1,0:T(8,128)(2,1)S(1)}, u32[]{:S(2)}, u32[]{:S(2)}) collective-permute-start(bf16[3,1,32,2048]{3,2,1,0:T(8,128)(2,1)S(1)} %get-tuple-element.55), channel_id=1, source_target_pairs={{0,1},{1,2},{2,3},{3,0},{4,5},{5,6},{6,7},{7,4},{8,9},{9,10},{10,1... | collective-permute-start | bytes 1179656 | tf_op jit(solution)/shard_map/ppermute | solution.py:259
  24.3 32.0 %collective-permute-start.1 = (bf16[3,1,32,2048]{3,2,1,0:T(8,128)(2,1)S(1)}, bf16[3,1,32,2048]{3,2,1,0:T(8,128)(2,1)S(1)}, u32[]{:S(2)}, u32[]{:S(2)}) collective-permute-start(bf16[3,1,32,2048]{3,2,1,0:T(8,128)(2,1)S(1)} %get-tuple-element.56), channel_id=1, source_target_pairs={{0,2},{1,3},{2,0},{3,1},{4,6},{5,7},{6,4},{7,5},{8,10},{9,11},{10,... | collective-permute-start | bytes 1179656 | tf_op jit(solution)/shard_map/ppermute | solution.py:259
  26.0 30.8 %collective-permute-start.2 = (bf16[3,1,32,2048]{3,2,1,0:T(8,128)(2,1)S(1)}, bf16[3,1,32,2048]{3,2,1,0:T(8,128)(2,1)S(1)}, u32[]{:S(2)}, u32[]{:S(2)}) collective-permute-start(bf16[3,1,32,2048]{3,2,1,0:T(8,128)(2,1)S(1)} %get-tuple-element.57), channel_id=1, source_target_pairs={{0,3},{1,0},{2,1},{3,2},{4,7},{5,4},{6,5},{7,6},{8,11},{9,8},{10,9... | collective-permute-start | bytes 1179656 | tf_op jit(solution)/shard_map/ppermute | solution.py:259
  26.7 63.9 %collective-permute-start.3 = (bf16[3,2,32,2048]{3,2,1,0:T(8,128)(2,1)S(1)}, bf16[3,2,32,2048]{3,2,1,0:T(8,128)(2,1)}, u32[]{:S(2)}, u32[]{:S(2)}) collective-permute-start(bf16[3,2,32,2048]{3,2,1,0:T(8,128)(2,1)S(1)} %get-tuple-element.61), channel_id=1, source_target_pairs={{0,1},{1,2},{2,3},{3,0},{4,5},{5,6},{6,7},{7,4},{8,9},{9,10},{10,1... | collective-permute-start | bytes 2359304 | tf_op jit(solution)/shard_map/ppermute | solution.py:259
  48.9 44.8 %copy-start.15 = (bf16[3,1,32,2048]{3,2,1,0:T(8,128)(2,1)}, bf16[3,1,32,2048]{3,2,1,0:T(8,128)(2,1)S(1)}, u32[]{:S(2)}) copy-start(bf16[3,1,32,2048]{3,2,1,0:T(8,128)(2,1)S(1)} %collective-permute-done.refs_5_.refs_1_) | copy-start | bytes 1179652
  48.9 42.8 %collective-permute-start.5 = (bf16[3,2,32,2048]{3,2,1,0:T(8,128)(2,1)S(1)}, bf16[3,2,32,2048]{3,2,1,0:T(8,128)(2,1)}, u32[]{:S(2)}, u32[]{:S(2)}) collective-permute-start(bf16[3,2,32,2048]{3,2,1,0:T(8,128)(2,1)S(1)} %get-tuple-element.63), channel_id=1, source_target_pairs={{0,3},{1,0},{2,1},{3,2},{4,7},{5,4},{6,5},{7,6},{8,11},{9,8},{10,9... | collective-permute-start | bytes 2359304 | tf_op jit(solution)/shard_map/ppermute | solution.py:259
  56.3 37.3 %copy-start.11 = (bf16[3,1,32,2048]{3,2,1,0:T(8,128)(2,1)}, bf16[3,1,32,2048]{3,2,1,0:T(8,128)(2,1)S(1)}, u32[]{:S(2)}) copy-start(bf16[3,1,32,2048]{3,2,1,0:T(8,128)(2,1)S(1)} %collective-permute-done.1.refs_6_.refs_2_) | copy-start | bytes 1179652
  56.3 26.2 %collective-permute-start.10 = (bf16[3,1,32,2048]{3,2,1,0:T(8,128)(2,1)S(1)}, bf16[3,1,32,2048]{3,2,1,0:T(8,128)(2,1)S(1)}, u32[]{:S(2)}, u32[]{:S(2)}) collective-permute-start(bf16[3,1,32,2048]{3,2,1,0:T(8,128)(2,1)S(1)} %get-tuple-element.66), channel_id=1, source_target_pairs={{0,1},{1,2},{2,3},{3,0},{4,5},{5,6},{6,7},{7,4},{8,9},{9,10},{10,1... | collective-permute-start | bytes 1179656 | tf_op jit(solution)/shard_map/ppermute | solution.py:259
  56.4 37.3 %copy-start.17 = (bf16[3,2,32,2048]{3,2,1,0:T(8,128)(2,1)}, bf16[3,2,32,2048]{3,2,1,0:T(8,128)(2,1)S(1)}, u32[]{:S(2)}) copy-start(bf16[3,2,32,2048]{3,2,1,0:T(8,128)(2,1)S(1)} %collective-permute-done.4.refs_2_) | copy-start | bytes 2359300
  56.4 46.8 %collective-permute-start.8 = (bf16[3,2,32,2048]{3,2,1,0:T(8,128)(2,1)S(1)}, bf16[3,2,32,2048]{3,2,1,0:T(8,128)(2,1)}, u32[]{:S(2)}, u32[]{:S(2)}) collective-permute-start(bf16[3,2,32,2048]{3,2,1,0:T(8,128)(2,1)S(1)} %collective-permute-done.4.refs_2_), channel_id=1, source_target_pairs={{0,4},{4,0},{1,5},{5,1},{2,6},{6,2},{3,7},{7,3},{8,12},{12,8},{9,1... | collective-permute-start | bytes 2359304 | tf_op jit(solution)/shard_map/ppermute | solution.py:259
  56.8 36.8 %copy-start.13 = (bf16[3,1,32,2048]{3,2,1,0:T(8,128)(2,1)}, bf16[3,1,32,2048]{3,2,1,0:T(8,128)(2,1)S(1)}, u32[]{:S(2)}) copy-start(bf16[3,1,32,2048]{3,2,1,0:T(8,128)(2,1)S(1)} %collective-permute-done.2.refs_7_.refs_3_) | copy-start | bytes 1179652
  56.9 33.3 %collective-permute-start.11 = (bf16[3,1,32,2048]{3,2,1,0:T(8,128)(2,1)S(1)}, bf16[3,1,32,2048]{3,2,1,0:T(8,128)(2,1)S(1)}, u32[]{:S(2)}, u32[]{:S(2)}) collective-permute-start(bf16[3,1,32,2048]{3,2,1,0:T(8,128)(2,1)S(1)} %get-tuple-element.67), channel_id=1, source_target_pairs={{0,2},{1,3},{2,0},{3,1},{4,6},{5,7},{6,4},{7,5},{8,10},{9,11},{10,... | collective-permute-start | bytes 1179656 | tf_op jit(solution)/shard_map/ppermute | solution.py:259
  82.5 11.1 %copy-start.18 = (bf16[3,1,32,2048]{3,2,1,0:T(8,128)(2,1)}, bf16[3,1,32,2048]{3,2,1,0:T(8,128)(2,1)S(1)}, u32[]{:S(2)}) copy-start(bf16[3,1,32,2048]{3,2,1,0:T(8,128)(2,1)S(1)} %collective-permute-done.10.refs_9_) | copy-start | bytes 1179652
  82.5 10.3 %collective-permute-start.12 = (bf16[3,1,32,2048]{3,2,1,0:T(8,128)(2,1)S(1)}, bf16[3,1,32,2048]{3,2,1,0:T(8,128)(2,1)S(1)}, u32[]{:S(2)}, u32[]{:S(2)}) collective-permute-start(bf16[3,1,32,2048]{3,2,1,0:T(8,128)(2,1)S(1)} %get-tuple-element.68), channel_id=1, source_target_pairs={{0,3},{1,0},{2,1},{3,2},{4,7},{5,4},{6,5},{7,6},{8,11},{9,8},{10,9... | collective-permute-start | bytes 1179656 | tf_op jit(solution)/shard_map/ppermute | solution.py:259
  90.2 45.7 %collective-permute-start.6 = (bf16[3,2,32,2048]{3,2,1,0:T(8,128)(2,1)S(1)}, bf16[3,2,32,2048]{3,2,1,0:T(8,128)(2,1)}, u32[]{:S(2)}, u32[]{:S(2)}) collective-permute-start(bf16[3,2,32,2048]{3,2,1,0:T(8,128)(2,1)S(1)} %get-tuple-element.60.refs_0_), channel_id=1, source_target_pairs={{0,4},{4,0},{1,5},{5,1},{2,6},{6,2},{3,7},{7,3},{8,12},{12,8},{9,1... | collective-permute-start | bytes 2359304 | tf_op jit(solution)/shard_map/ppermute | solution.py:259
  90.6 46.3 %collective-permute-start.7 = (bf16[3,2,32,2048]{3,2,1,0:T(8,128)(2,1)}, bf16[3,2,32,2048]{3,2,1,0:T(8,128)(2,1)}, u32[]{:S(2)}, u32[]{:S(2)}) collective-permute-start(bf16[3,2,32,2048]{3,2,1,0:T(8,128)(2,1)} %collective-permute-done.3.refs_1_), channel_id=1, source_target_pairs={{0,4},{4,0},{1,5},{5,1},{2,6},{6,2},{3,7},{7,3},{8,12},{12,8},{9,1... | collective-permute-start | bytes 2359304 | tf_op jit(solution)/shard_map/ppermute | solution.py:259
  91.6 62.1 %collective-permute-start.9 = (bf16[3,2,32,2048]{3,2,1,0:T(8,128)(2,1)}, bf16[3,2,32,2048]{3,2,1,0:T(8,128)(2,1)}, u32[]{:S(2)}, u32[]{:S(2)}) collective-permute-start(bf16[3,2,32,2048]{3,2,1,0:T(8,128)(2,1)} %collective-permute-done.5.refs_3_), channel_id=1, source_target_pairs={{0,4},{4,0},{1,5},{5,1},{2,6},{6,2},{3,7},{7,3},{8,12},{12,8},{9,1... | collective-permute-start | bytes 2359304 | tf_op jit(solution)/shard_map/ppermute | solution.py:259
  93.6 9.5 %copy-start.2 = (bf16[3,1,32,2048]{3,2,1,0:T(8,128)(2,1)S(1)}, bf16[3,1,32,2048]{3,2,1,0:T(8,128)(2,1)}, u32[]{:S(2)}) copy-start(bf16[3,1,32,2048]{3,2,1,0:T(8,128)(2,1)} %copy-done.1) | copy-start | bytes 1179652
  103.2 58.9 %collective-permute-start.13 = (bf16[3,1,32,2048]{3,2,1,0:T(8,128)(2,1)S(1)}, bf16[3,1,32,2048]{3,2,1,0:T(8,128)(2,1)S(1)}, u32[]{:S(2)}, u32[]{:S(2)}) collective-permute-start(bf16[3,1,32,2048]{3,2,1,0:T(8,128)(2,1)S(1)} %copy-done.2), channel_id=1, source_target_pairs={{0,4},{4,0},{1,5},{5,1},{2,6},{6,2},{3,7},{7,3},{8,12},{12,8},{9,1... | collective-permute-start | bytes 1179656 | tf_op jit(solution)/shard_map/ppermute | solution.py:259
  158.4 11.1 %copy-start.16 = (bf16[3,1,32,2048]{3,2,1,0:T(8,128)(2,1)S(1)}, bf16[3,1,32,2048]{3,2,1,0:T(8,128)(2,1)}, u32[]{:S(2)}) copy-start(bf16[3,1,32,2048]{3,2,1,0:T(8,128)(2,1)} %copy-done.15) | copy-start | bytes 1179652
  158.4 30.8 %copy-start.12 = (bf16[3,1,32,2048]{3,2,1,0:T(8,128)(2,1)S(1)}, bf16[3,1,32,2048]{3,2,1,0:T(8,128)(2,1)}, u32[]{:S(2)}) copy-start(bf16[3,1,32,2048]{3,2,1,0:T(8,128)(2,1)} %copy-done.11) | copy-start | bytes 1179652
  158.4 30.8 %copy-start.14 = (bf16[3,1,32,2048]{3,2,1,0:T(8,128)(2,1)S(1)}, bf16[3,1,32,2048]{3,2,1,0:T(8,128)(2,1)}, u32[]{:S(2)}) copy-start(bf16[3,1,32,2048]{3,2,1,0:T(8,128)(2,1)} %copy-done.13) | copy-start | bytes 1179652
  162.1 27.3 %copy-start.21 = (bf16[3,1,32,2048]{3,2,1,0:T(8,128)(2,1)}, bf16[3,1,32,2048]{3,2,1,0:T(8,128)(2,1)S(1)}, u32[]{:S(2)}) copy-start(bf16[3,1,32,2048]{3,2,1,0:T(8,128)(2,1)S(1)} %collective-permute-done.13.refs_4_) | copy-start | bytes 1179652
  162.1 25.4 %all-to-all-start.1 = ((f32[16,2,3,2,8,128]{5,4,3,2,1,0:T(8,128)}), f32[16,2,3,2,8,128]{5,4,3,2,1,0:T(8,128)S(1)}, u32[]{:S(2)}, u32[]{:S(2)}) async-start(f32[16,2,3,2,8,128]{5,4,3,2,1,0:T(8,128)} %tied_terms.3), calls=%async_computation.1 | async-start | bytes 1572864 | tf_op jit(solution)/shard_map/all_to_all | solution.py:263
  169.5 18.0 %collective-permute-start.14 = (bf16[3,1,32,2048]{3,2,1,0:T(8,128)(2,1)S(1)}, bf16[3,1,32,2048]{3,2,1,0:T(8,128)(2,1)S(1)}, u32[]{:S(2)}, u32[]{:S(2)}) collective-permute-start(bf16[3,1,32,2048]{3,2,1,0:T(8,128)(2,1)S(1)} %copy-done.16), channel_id=1, source_target_pairs={{0,4},{4,0},{1,5},{5,1},{2,6},{6,2},{3,7},{7,3},{8,12},{12,8},{9,1... | collective-permute-start | bytes 1179656 | tf_op jit(solution)/shard_map/ppermute | solution.py:259
  187.5 6.4 %copy-start.22 = (bf16[3,1,32,2048]{3,2,1,0:T(8,128)(2,1)}, bf16[3,1,32,2048]{3,2,1,0:T(8,128)(2,1)S(1)}, u32[]{:S(2)}) copy-start(bf16[3,1,32,2048]{3,2,1,0:T(8,128)(2,1)S(1)} %collective-permute-done.14.refs_5_) | copy-start | bytes 1179652
  187.5 3.2 %collective-permute-start.15 = (f32[2,3,2,8,128]{4,3,2,1,0:T(8,128)S(1)}, f32[2,3,2,8,128]{4,3,2,1,0:T(8,128)S(1)}, u32[]{:S(2)}, u32[]{:S(2)}) collective-permute-start(f32[2,3,2,8,128]{4,3,2,1,0:T(8,128)S(1)} %reduce_sum.27), channel_id=1, source_target_pairs={{0,4},{4,0},{1,5},{5,1},{2,6},{6,2},{3,7},{7,3},{8,12},{12,8},{9,1... | collective-permute-start | bytes 147464 | tf_op jit(solution)/shard_map/ppermute | solution.py:259
  190.7 29.4 %collective-permute-start.17 = (bf16[6,1,32,2048]{3,2,1,0:T(8,128)(2,1)S(1)}, bf16[6,1,32,2048]{3,2,1,0:T(8,128)(2,1)S(1)}, u32[]{:S(2)}, u32[]{:S(2)}) collective-permute-start(bf16[6,1,32,2048]{3,2,1,0:T(8,128)(2,1)S(1)} %pad_maximum_fusion), channel_id=1, source_target_pairs={{0,4},{4,0},{1,5},{5,1},{2,6},{6,2},{3,7},{7,3},{8,12},{12,8},{9,1... | collective-permute-start | bytes 2359304 | tf_op jit(solution)/shard_map/ppermute | solution.py:259
  220.2 71.1 %all-to-all-start.3 = ((bf16[16,6,32,768]{3,2,1,0:T(8,128)(2,1)}), bf16[16,6,32,768]{3,2,1,0:T(8,128)(2,1)}, u32[]{:S(2)}, u32[]{:S(2)}) async-start(bf16[16,6,32,768]{3,2,1,0:T(8,128)(2,1)} %copy-done), calls=%async_computation.3 | async-start | bytes 9437184 | tf_op jit(solution)/shard_map/all_to_all | solution.py:263
  231.4 18.9 %copy-start.23 = (bf16[3,1,32,2048]{3,2,1,0:T(8,128)(2,1)S(1)}, bf16[3,1,32,2048]{3,2,1,0:T(8,128)(2,1)}, u32[]{:S(2)}) copy-start(bf16[3,1,32,2048]{3,2,1,0:T(8,128)(2,1)} %get-tuple-element.92) | copy-start | bytes 1179652
  231.4 18.8 %collective-permute-start.16 = (bf16[3,1,32,2048]{3,2,1,0:T(8,128)(2,1)}, bf16[3,1,32,2048]{3,2,1,0:T(8,128)(2,1)S(1)}, u32[]{:S(2)}, u32[]{:S(2)}) collective-permute-start(bf16[3,1,32,2048]{3,2,1,0:T(8,128)(2,1)} %get-tuple-element.79), channel_id=1, source_target_pairs={{0,3},{1,0},{2,1},{3,2},{4,7},{5,4},{6,5},{7,6},{8,11},{9,8},{10,9... | collective-permute-start | bytes 1179656 | tf_op jit(solution)/shard_map/ppermute | solution.py:259
  233.9 20.8 %collective-permute-start.24 = (bf16[3,1,32,2048]{3,2,1,0:T(8,128)(2,1)}, bf16[3,1,32,2048]{3,2,1,0:T(8,128)(2,1)S(1)}, u32[]{:S(2)}, u32[]{:S(2)}) collective-permute-start(bf16[3,1,32,2048]{3,2,1,0:T(8,128)(2,1)} %get-tuple-element.94), channel_id=1, source_target_pairs={{0,2},{1,3},{2,0},{3,1},{4,6},{5,7},{6,4},{7,5},{8,10},{9,11},{10,... | collective-permute-start | bytes 1179656 | tf_op jit(solution)/shard_map/ppermute | solution.py:259
  234.5 24.3 %collective-permute-start.25 = (bf16[3,1,32,2048]{3,2,1,0:T(8,128)(2,1)}, bf16[3,1,32,2048]{3,2,1,0:T(8,128)(2,1)S(1)}, u32[]{:S(2)}, u32[]{:S(2)}) collective-permute-start(bf16[3,1,32,2048]{3,2,1,0:T(8,128)(2,1)} %get-tuple-element.95), channel_id=1, source_target_pairs={{0,1},{1,2},{2,3},{3,0},{4,5},{5,6},{6,7},{7,4},{8,9},{9,10},{10,1... | collective-permute-start | bytes 1179656 | tf_op jit(solution)/shard_map/ppermute | solution.py:259
  235.1 32.0 %collective-permute-start.21 = (bf16[3,1,32,2048]{3,2,1,0:T(8,128)(2,1)}, bf16[3,1,32,2048]{3,2,1,0:T(8,128)(2,1)S(1)}, u32[]{:S(2)}, u32[]{:S(2)}) collective-permute-start(bf16[3,1,32,2048]{3,2,1,0:T(8,128)(2,1)} %get-tuple-element.90), channel_id=1, source_target_pairs={{0,3},{1,0},{2,1},{3,2},{4,7},{5,4},{6,5},{7,6},{8,11},{9,8},{10,9... | collective-permute-start | bytes 1179656 | tf_op jit(solution)/shard_map/ppermute | solution.py:259
  237.1 32.5 %collective-permute-start.22 = (bf16[3,1,32,2048]{3,2,1,0:T(8,128)(2,1)}, bf16[3,1,32,2048]{3,2,1,0:T(8,128)(2,1)S(1)}, u32[]{:S(2)}, u32[]{:S(2)}) collective-permute-start(bf16[3,1,32,2048]{3,2,1,0:T(8,128)(2,1)} %get-tuple-element.91), channel_id=1, source_target_pairs={{0,2},{1,3},{2,0},{3,1},{4,6},{5,7},{6,4},{7,5},{8,10},{9,11},{10,... | collective-permute-start | bytes 1179656 | tf_op jit(solution)/shard_map/ppermute | solution.py:259
  250.2 22.5 %collective-permute-start.23 = (bf16[3,1,32,2048]{3,2,1,0:T(8,128)(2,1)S(1)}, bf16[3,1,32,2048]{3,2,1,0:T(8,128)(2,1)S(1)}, u32[]{:S(2)}, u32[]{:S(2)}) collective-permute-start(bf16[3,1,32,2048]{3,2,1,0:T(8,128)(2,1)S(1)} %copy-done.23), channel_id=1, source_target_pairs={{0,1},{1,2},{2,3},{3,0},{4,5},{5,6},{6,7},{7,4},{8,9},{9,10},{10,1... | collective-permute-start | bytes 1179656 | tf_op jit(solution)/shard_map/ppermute | solution.py:259
  250.2 16.8 %copy-start.9 = (bf16[3,1,32,2048]{3,2,1,0:T(8,128)(2,1)S(1)}, bf16[3,1,32,2048]{3,2,1,0:T(8,128)(2,1)}, u32[]{:S(2)}) copy-start(bf16[3,1,32,2048]{3,2,1,0:T(8,128)(2,1)} %get-tuple-element.93.refs_0_) | copy-start | bytes 1179652
  254.7 29.7 %collective-permute-start.18 = (bf16[3,1,32,2048]{3,2,1,0:T(8,128)(2,1)}, bf16[3,1,32,2048]{3,2,1,0:T(8,128)(2,1)S(1)}, u32[]{:S(2)}, u32[]{:S(2)}) collective-permute-start(bf16[3,1,32,2048]{3,2,1,0:T(8,128)(2,1)} %get-tuple-element.86), channel_id=1, source_target_pairs={{0,3},{1,0},{2,1},{3,2},{4,7},{5,4},{6,5},{7,6},{8,11},{9,8},{10,9... | collective-permute-start | bytes 1179656 | tf_op jit(solution)/shard_map/ppermute | solution.py:259
  258.7 25.8 %collective-permute-start.19 = (bf16[3,1,32,2048]{3,2,1,0:T(8,128)(2,1)}, bf16[3,1,32,2048]{3,2,1,0:T(8,128)(2,1)S(1)}, u32[]{:S(2)}, u32[]{:S(2)}) collective-permute-start(bf16[3,1,32,2048]{3,2,1,0:T(8,128)(2,1)} %get-tuple-element.87), channel_id=1, source_target_pairs={{0,2},{1,3},{2,0},{3,1},{4,6},{5,7},{6,4},{7,5},{8,10},{9,11},{10,... | collective-permute-start | bytes 1179656 | tf_op jit(solution)/shard_map/ppermute | solution.py:259
  267.1 21.7 %collective-permute-start.20 = (bf16[3,1,32,2048]{3,2,1,0:T(8,128)(2,1)}, bf16[3,1,32,2048]{3,2,1,0:T(8,128)(2,1)S(1)}, u32[]{:S(2)}, u32[]{:S(2)}) collective-permute-start(bf16[3,1,32,2048]{3,2,1,0:T(8,128)(2,1)} %get-tuple-element.88), channel_id=1, source_target_pairs={{0,1},{1,2},{2,3},{3,0},{4,5},{5,6},{6,7},{7,4},{8,9},{9,10},{10,1... | collective-permute-start | bytes 1179656 | tf_op jit(solution)/shard_map/ppermute | solution.py:259
  267.1 5.6 %copy-start.8 = (bf16[3,1,32,2048]{3,2,1,0:T(8,128)(2,1)S(1)}, bf16[3,1,32,2048]{3,2,1,0:T(8,128)(2,1)}, u32[]{:S(2)}) copy-start(bf16[3,1,32,2048]{3,2,1,0:T(8,128)(2,1)} %get-tuple-element.89.refs_0_) | copy-start | bytes 1179652
  272.7 16.0 %copy-start.10 = (bf16[3,1,32,2048]{3,2,1,0:T(8,128)(2,1)S(1)}, bf16[3,1,32,2048]{3,2,1,0:T(8,128)(2,1)}, u32[]{:S(2)}) copy-start(bf16[3,1,32,2048]{3,2,1,0:T(8,128)(2,1)} %get-tuple-element.85.refs_0_) | copy-start | bytes 1179652
  (5 other events, 7.1 us)

commit v4 on v3

--- a/solution.py
+++ b/solution.py
@@ -350,14 +350,17 @@
     def across(keys, *others):
         return [shift(c, "yl", 1) for c in after(keys, others)]
 
-    other_keys = across(keys[:2], other[-2])
+    early = across([jnp.concatenate(keys[:2])], other[-2])[0]
     left, half = after((other, half), col_done)
-    terms = tied_terms(left, keys, values, groups, 1, (half,))
-    terms = over_rows(after(terms, other_keys[0]))
-    sums = jnp.sum(after(terms, other_keys[1]), axis=0)
+    terms = over_rows(tied_terms(left, keys, values, groups, 1, (half,)))
+    sums = jnp.sum(after(terms, early), axis=0)
     swapped = shift(sums, "yl", 1)
     late = across([jnp.concatenate(keys[2:])], swapped)[0]
-    other_keys += [late[at : at + head_group] for at in range(0, late.shape[0], head_group)]
+    other_keys = [
+        part[at : at + head_group]
+        for part in (early, late)
+        for at in range(0, part.shape[0], head_group)
+    ]
 
     logits, dprobs = jnp.concatenate([sums, jnp.flip(swapped, 2)], axis=-1)
     probs = jax.nn.softmax(logits * row_factor, axis=-1)
@@ -384,7 +387,8 @@
     keys = after(keys, value_chunks[1])
     query_grads = tied_grads(query_grads_kernel, keys, other_keys, whole, row_factor, "query_grads")
     chunks = (back(query_grads), key_chunks, value_chunks)
-    row_grads = [unpack_rows(here, c)[0] for c in chunks]
+    row_grads = [unpack_rows(here, c)[0] for c in chunks[1:]]
+    row_grads.insert(0, unpack_rows(here, after(chunks[0], col_grads))[0])
 
     return (*row_grads, *col_grads)
 

time: 297 us -> 285 us (0.960)
  waiting for transfers between devices: 138 us -> 130 us
    ppermute x26 -> x25, waiting for transfers between devices: 138 us -> 112 us  [shift(): return lax.ppermute(x, axis, [(i, (i + by) % n) for i in range(n)])]
    all_to_all x3, waiting for transfers between devices: 0.01 us -> 17.9 us  [over_rows(): return lax.all_to_all(x, ROWS, split_axis=0, concat_axis=0, tiled=True)]
    ppermute x26 -> x25, starting transfers between devices: 28.1 us -> 25.9 us  [shift(): return lax.ppermute(x, axis, [(i, (i + by) % n) for i in range(n)])]
  transfers between devices with their start and end apart: 29 -> 28, of which waited for: 16 -> 16; matrix products, arithmetic and copies ran while one was open for 1% -> 1% of each run, Pallas kernels for 21% -> 23%
where the time goes in v4:
time: 285 us; the launch traced here: 284 us
  waiting for transfers between devices  130 us (46%)
  Pallas kernels  72.9 us (26%)
  starting transfers between devices  48.6 us (17%)
  blocking collectives  24.3 us (9%)
  local copies, waits for them, and re-layouts  5.86 us (2%)
    ppermute x25, waiting for transfers between devices, shift(): return lax.ppermute(x, axis, [(i, (i + by) % n) for i in range(n)])  112 us
    pallas_call x1, Pallas kernels, column_backward(): pl.pallas_call(functools.partial(column_kernel, chunk=chunk), grid=(piece...  29.5 us
    ppermute x25, starting transfers between devices, shift(): return lax.ppermute(x, axis, [(i, (i + by) % n) for i in range(n)])  25.9 us
    all_to_all x1, blocking collectives, over_rows(): return lax.all_to_all(x, ROWS, split_axis=0, concat_axis=0, tiled=True)  24.3 us
    all_to_all x3, starting transfers between devices, over_rows(): return lax.all_to_all(x, ROWS, split_axis=0, concat_axis=0, tiled=True)  22.8 us
    all_to_all x3, waiting for transfers between devices, over_rows(): return lax.all_to_all(x, ROWS, split_axis=0, concat_axis=0, tiled=True)  17.9 us
    pallas_call x2, Pallas kernels, tied_grads(): pl.pallas_call(functools.partial(kernel, parts=parts, factor=factor), gri...  10 us
    pallas_call x2, Pallas kernels, tied_terms(): pl.pallas_call(functools.partial(terms_kernel, parts=parts), grid=(heads,...  9.36 us
  transfers between devices with their start and end apart: 28, of which 16 were waited for; matrix products, arithmetic and copies ran while one was open for 1% of the time, Pallas kernels for 23%

profile of v4, /device:TPU:1, one launch (start us, length us, event | category | flops | bytes accessed | tf_op | source)
XLA Modules:
  0.0 284.2 jit_solution(4303200816988084817)
XLA Ops:
  0.6 5.5 %column_pack.1 = bf16[16,8,32,768]{3,2,1,0:T(8,128)(2,1)} custom-call(bf16[32,32,768]{2,1,0:T(8,128)(2,1)} %refs_0_.1, bf16[32,32,768]{2,1,0:T(8,128)(2,1)} %refs_1_.1, bf16[32,32,768]{2,1,0:T(8,128)(2,1)} %refs_2_.1, bf16[32,32,768]{2,1,0:T(8,128)(2,1)} %refs_3_.1), custom_call_target="tpu_custom_call" | custom-call | flops 1 | bytes 1 | tf_op jit(solution)/shard_map/column_pack/pallas_call | solution.py:290
  6.2 9.6 %all-to-all-start = ((bf16[16,8,32,768]{3,2,1,0:T(8,128)(2,1)}), bf16[16,8,32,768]{3,2,1,0:T(8,128)(2,1)}, u32[]{:S(2)}, u32[]{:S(2)}) async-start(bf16[16,8,32,768]{3,2,1,0:T(8,128)(2,1)} %column_pack.1), calls=%async_computation | async-start | bytes 12582912 | tf_op jit(solution)/shard_map/all_to_all | solution.py:263
  15.8 3.0 %pack_rows.4 = (bf16[3,2,32,2048]{3,2,1,0:T(8,128)(2,1)S(1)}, bf16[3,2,32,2048]{3,2,1,0:T(8,128)(2,1)S(1)}, bf16[3,2,32,2048]{3,2,1,0:T(8,128)(2,1)S(1)}, bf16[3,2,32,2048]{3,2,1,0:T(8,128)(2,1)S(1)}) custom-call(s32[1]{0:T(128)} %bitcast.here_ref, bf16[32,32,768]{2,1,0:T(8,128)(2,1)S(1)} %copy-done.5, bf16[32,32,768]{2,1,0:T(8,128)(2,1)} %refs_1_.2), custom_call_target="tpu_custom_call" | custom-call | flops 1 | bytes 1 | tf_op jit(solution)/shard_map/pack_rows/pallas_call | solution.py:121
  18.8 2.8 collective-permute-start.4
  21.6 1.6 pack_rows.3
  23.6 1.7 collective-permute-start.1
  25.3 0.8 collective-permute-start.2
  26.8 22.0 %collective-permute-done.refs_5_.refs_1_ = bf16[3,1,32,2048]{3,2,1,0:T(8,128)(2,1)S(1)} collective-permute-done((bf16[3,1,32,2048]{3,2,1,0:T(8,128)(2,1)S(1)}, bf16[3,1,32,2048]{3,2,1,0:T(8,128)(2,1)S(1)}, u32[]{:S(2)}, u32[]{:S(2)}) %collective-permute-start) | collective-permute-done | bytes 393248 | tf_op jit(solution)/shard_map/ppermute | solution.py:259
  48.8 1.6 pack_rows.5
  50.4 5.9 %collective-permute-done.1.refs_6_.refs_2_ = bf16[3,1,32,2048]{3,2,1,0:T(8,128)(2,1)S(1)} collective-permute-done((bf16[3,1,32,2048]{3,2,1,0:T(8,128)(2,1)S(1)}, bf16[3,1,32,2048]{3,2,1,0:T(8,128)(2,1)S(1)}, u32[]{:S(2)}, u32[]{:S(2)}) %collective-permute-start.1) | collective-permute-done | bytes 393248 | tf_op jit(solution)/shard_map/ppermute | solution.py:259
  56.8 2.9 %collective-permute-start.11 = (bf16[3,1,32,2048]{3,2,1,0:T(8,128)(2,1)S(1)}, bf16[3,1,32,2048]{3,2,1,0:T(8,128)(2,1)S(1)}, u32[]{:S(2)}, u32[]{:S(2)}) collective-permute-start(bf16[3,1,32,2048]{3,2,1,0:T(8,128)(2,1)S(1)} %get-tuple-element.69), channel_id=1, source_target_pairs={{0,2},{1,3},{2,0},{3,1},{4,6},{5,7},{6,4},{7,5},{8,10},{9,11},{10,... | collective-permute-start | bytes 1179656 | tf_op jit(solution)/shard_map/ppermute | solution.py:259
  59.6 22.8 %collective-permute-done.10.refs_9_ = bf16[3,1,32,2048]{3,2,1,0:T(8,128)(2,1)S(1)} collective-permute-done((bf16[3,1,32,2048]{3,2,1,0:T(8,128)(2,1)S(1)}, bf16[3,1,32,2048]{3,2,1,0:T(8,128)(2,1)S(1)}, u32[]{:S(2)}, u32[]{:S(2)}) %collective-permute-start.10) | collective-permute-done | bytes 393248 | tf_op jit(solution)/shard_map/ppermute | solution.py:259
  82.5 7.6 %collective-permute-done.11.refs_10_ = bf16[3,1,32,2048]{3,2,1,0:T(8,128)(2,1)S(1)} collective-permute-done((bf16[3,1,32,2048]{3,2,1,0:T(8,128)(2,1)S(1)}, bf16[3,1,32,2048]{3,2,1,0:T(8,128)(2,1)S(1)}, u32[]{:S(2)}, u32[]{:S(2)}) %collective-permute-start.11) | collective-permute-done | bytes 393248 | tf_op jit(solution)/shard_map/ppermute | solution.py:259
  90.5 1.1 collective-permute-start.7
  93.6 4.7 %tied_terms.2.refs_12_ = f32[16,2,3,2,8,128]{5,4,3,2,1,0:T(8,128)} custom-call(bf16[3,2,32,2048]{3,2,1,0:T(8,128)(2,1)} %copy-done.2, bf16[3,2,32,2048]{3,2,1,0:T(8,128)(2,1)} %collective-permute-done.3.refs_1_, bf16[3,2,32,2048]{3,2,1,0:T(8,128)(2,1)} %collective-permute-done.4.refs_2_, bf16[3,2,32,2048]{3,2,1,0:T(8,128)(2,1)} %collective-permute-done.5.refs_3_, ...), custom_call_target="tpu_custom_call" | custom-call | flops 1 | bytes 1 | tf_op jit(solution)/shard_map/tied_terms/pallas_call | solution.py:197
  98.2 4.9 %collective-permute-done.8.refs_2_.refs_6_ = bf16[3,2,32,2048]{3,2,1,0:T(8,128)(2,1)} collective-permute-done((bf16[3,2,32,2048]{3,2,1,0:T(8,128)(2,1)}, bf16[3,2,32,2048]{3,2,1,0:T(8,128)(2,1)}, u32[]{:S(2)}, u32[]{:S(2)}) %collective-permute-start.8) | collective-permute-done | bytes 786464 | tf_op jit(solution)/shard_map/ppermute | solution.py:259
  103.1 1.1 collective-permute-start.13
  104.2 29.5 %column_attention.1 = bf16[16,6,32,768]{3,2,1,0:T(8,128)(2,1)S(1)} custom-call(bf16[16,8,32,768]{3,2,1,0:T(8,128)(2,1)} %all-to-all-done.x_ref), custom_call_target="tpu_custom_call" | custom-call | flops 8053063680 | bytes 11010048 | tf_op jit(solution)/shard_map/column_attention/pallas_call | solution.py:80
  133.7 2.1 copy-done.1
  135.8 1.0 collective-permute-done.7.refs_1_.refs_5_
  136.8 16.9 %collective-permute-done.9.refs_3_.refs_7_ = bf16[3,2,32,2048]{3,2,1,0:T(8,128)(2,1)} collective-permute-done((bf16[3,2,32,2048]{3,2,1,0:T(8,128)(2,1)}, bf16[3,2,32,2048]{3,2,1,0:T(8,128)(2,1)}, u32[]{:S(2)}, u32[]{:S(2)}) %collective-permute-start.9) | collective-permute-done | bytes 786464 | tf_op jit(solution)/shard_map/ppermute | solution.py:259
  153.7 4.7 %tied_terms.3 = f32[16,2,3,2,8,128]{5,4,3,2,1,0:T(8,128)} custom-call(bf16[3,2,32,2048]{3,2,1,0:T(8,128)(2,1)} %collective-permute-done.6.refs_0_.refs_4_, bf16[3,2,32,2048]{3,2,1,0:T(8,128)(2,1)} %collective-permute-done.7.refs_1_.refs_5_, bf16[3,2,32,2048]{3,2,1,0:T(8,128)(2,1)} %collective-permute-done.8.refs_2_.refs_6_, ...), custom_call_target="tpu_custom_call", output_to_operand_aliasing={{}: (12, {})} | custom-call | flops 1 | bytes 1 | tf_op jit(solution)/shard_map/tied_terms/pallas_call | solution.py:197
  158.4 8.1 %all-to-all-start.1 = ((f32[16,2,3,2,8,128]{5,4,3,2,1,0:T(8,128)}), f32[16,2,3,2,8,128]{5,4,3,2,1,0:T(8,128)S(1)}, u32[]{:S(2)}, u32[]{:S(2)}) async-start(f32[16,2,3,2,8,128]{5,4,3,2,1,0:T(8,128)} %tied_terms.3), calls=%async_computation.1 | async-start | bytes 1572864 | tf_op jit(solution)/shard_map/all_to_all | solution.py:263
  166.4 4.0 %collective-permute-done.13 = bf16[6,1,32,2048]{3,2,1,0:T(8,128)(2,1)S(1)} collective-permute-done((bf16[6,1,32,2048]{3,2,1,0:T(8,128)(2,1)S(1)}, bf16[6,1,32,2048]{3,2,1,0:T(8,128)(2,1)S(1)}, u32[]{:S(2)}, u32[]{:S(2)}) %collective-permute-start.13) | collective-permute-done | bytes 786464 | tf_op jit(solution)/shard_map/ppermute | solution.py:259
  170.4 11.5 %all-to-all-done.1 = f32[16,2,3,2,8,128]{5,4,3,2,1,0:T(8,128)S(1)} async-done(((f32[16,2,3,2,8,128]{5,4,3,2,1,0:T(8,128)}), f32[16,2,3,2,8,128]{5,4,3,2,1,0:T(8,128)S(1)}, u32[]{:S(2)}, u32[]{:S(2)}) %all-to-all-start.1) | async-done | bytes 786464 | tf_op jit(solution)/shard_map/all_to_all | solution.py:263
  182.5 2.5 collective-permute-done.14
  185.1 1.4 fusion.28
  187.2 24.3 %all_to_all.20 = bf16[16,5,3,8,128]{4,3,2,1,0:T(8,128)(2,1)S(1)} all-to-all(bf16[16,5,3,8,128]{4,3,2,1,0:T(8,128)(2,1)S(1)} %broadcast_in_dim.2), channel_id=1, replica_groups=mesh['z'=4,'yh'=2,'core'=2,'yl'=2,'x'=4] {'z','yh','core'}, dimensions={0} | all-to-all | bytes 983040 | tf_op jit(solution)/shard_map/all_to_all | solution.py:263
  211.6 0.9 copy_bitcast_fusion.refs_8_
  212.5 5.1 %all-to-all-start.3 = ((bf16[16,6,32,768]{3,2,1,0:T(8,128)(2,1)}), bf16[16,6,32,768]{3,2,1,0:T(8,128)(2,1)}, u32[]{:S(2)}, u32[]{:S(2)}) async-start(bf16[16,6,32,768]{3,2,1,0:T(8,128)(2,1)} %copy-done.1), calls=%async_computation.3 | async-start | bytes 9437184 | tf_op jit(solution)/shard_map/all_to_all | solution.py:263
  217.6 1.0 fusion.27
  218.5 5.6 %pair_grads.1 = (bf16[3,1,32,2048]{3,2,1,0:T(8,128)(2,1)}, bf16[3,1,32,2048]{3,2,1,0:T(8,128)(2,1)}, bf16[3,1,32,2048]{3,2,1,0:T(8,128)(2,1)}, bf16[3,1,32,2048]...) custom-call(bf16[3,2,32,2048]{3,2,1,0:T(8,128)(2,1)} %copy-done.2, ...), custom_call_target="tpu_custom_call" | custom-call | flops 1 | bytes 1 | tf_op jit(solution)/shard_map/pair_grads/pallas_call | solution.py:245
  224.1 2.5 collective-permute-start.15
  227.8 2.1 collective-permute-start.20
  229.8 1.2 collective-permute-start.21
  231.1 0.9 fusion.26
  232.0 11.0 %collective-permute-done.15.refs_1_ = bf16[3,1,32,2048]{3,2,1,0:T(8,128)(2,1)S(1)} collective-permute-done((bf16[3,1,32,2048]{3,2,1,0:T(8,128)(2,1)}, bf16[3,1,32,2048]{3,2,1,0:T(8,128)(2,1)S(1)}, u32[]{:S(2)}, u32[]{:S(2)}) %collective-permute-start.15) | collective-permute-done | bytes 393248 | tf_op jit(solution)/shard_map/ppermute | solution.py:259
  243.0 4.5 %query_grads.1 = (bf16[3,1,32,2048]{3,2,1,0:T(8,128)(2,1)}, bf16[3,1,32,2048]{3,2,1,0:T(8,128)(2,1)}, bf16[3,1,32,2048]{3,2,1,0:T(8,128)(2,1)}, bf16[3,1,32,2048]{3,2,1,0:T(8,128)(2,1)}) custom-call(bf16[3,1,32,2048]{3,2,1,0:T(8,128)(2,1)} %copy-done, bf16[3,1,32,2048]{3,2,1,0:T(8,128)(2,1)} %copy-done.10, bf16[3,1,32,2048]{3,2,1,0:T(8,128)(2,1)} %copy-done.11, ...), custom_call_target="tpu_custom_call" | custom-call | flops 1 | bytes 1 | tf_op jit(solution)/shard_map/query_grads/pallas_call | solution.py:245
  247.5 4.0 %collective-permute-start.17 = (bf16[3,1,32,2048]{3,2,1,0:T(8,128)(2,1)}, bf16[3,1,32,2048]{3,2,1,0:T(8,128)(2,1)S(1)}, u32[]{:S(2)}, u32[]{:S(2)}) collective-permute-start(bf16[3,1,32,2048]{3,2,1,0:T(8,128)(2,1)} %get-tuple-element.86), channel_id=1, source_target_pairs={{0,3},{1,0},{2,1},{3,2},{4,7},{5,4},{6,5},{7,6},{8,11},{9,8},{10,9... | collective-permute-start | bytes 1179656 | tf_op jit(solution)/shard_map/ppermute | solution.py:259
  251.5 1.3 collective-permute-start.18
  252.8 7.1 %collective-permute-done.20.refs_1_ = bf16[3,1,32,2048]{3,2,1,0:T(8,128)(2,1)S(1)} collective-permute-done((bf16[3,1,32,2048]{3,2,1,0:T(8,128)(2,1)}, bf16[3,1,32,2048]{3,2,1,0:T(8,128)(2,1)S(1)}, u32[]{:S(2)}, u32[]{:S(2)}) %collective-permute-start.20) | collective-permute-done | bytes 393248 | tf_op jit(solution)/shard_map/ppermute | solution.py:259
  259.8 2.6 unpack_rows.5
  262.4 3.0 %collective-permute-done.22.refs_3_ = bf16[3,1,32,2048]{3,2,1,0:T(8,128)(2,1)S(1)} collective-permute-done((bf16[3,1,32,2048]{3,2,1,0:T(8,128)(2,1)}, bf16[3,1,32,2048]{3,2,1,0:T(8,128)(2,1)S(1)}, u32[]{:S(2)}, u32[]{:S(2)}) %collective-permute-start.22) | collective-permute-done | bytes 393248 | tf_op jit(solution)/shard_map/ppermute | solution.py:259
  265.4 2.6 unpack_rows.4
  268.0 6.4 %all-to-all-done.3.x_ref = bf16[16,6,32,768]{3,2,1,0:T(8,128)(2,1)} async-done(((bf16[16,6,32,768]{3,2,1,0:T(8,128)(2,1)}), bf16[16,6,32,768]{3,2,1,0:T(8,128)(2,1)}, u32[]{:S(2)}, u32[]{:S(2)}) %all-to-all-start.3) | async-done | bytes 4718624 | tf_op jit(solution)/shard_map/all_to_all | solution.py:263
  274.4 4.7 %column_unpack.1 = (bf16[32,32,768]{2,1,0:T(8,128)(2,1)}, bf16[32,32,768]{2,1,0:T(8,128)(2,1)}, bf16[32,32,768]{2,1,0:T(8,128)(2,1)}) custom-call(bf16[16,6,32,768]{3,2,1,0:T(8,128)(2,1)} %all-to-all-done.3.x_ref), custom_call_target="tpu_custom_call" | custom-call | flops 1 | bytes 1 | tf_op jit(solution)/shard_map/column_unpack/pallas_call | solution.py:312
  279.0 2.4 collective-permute-done.19.refs_3_
  281.4 2.6 unpack_rows.3
  (76 shorter events, 6.6 us)
Async XLA Ops:
  6.2 9.6 %copy-start.5 = (bf16[32,32,768]{2,1,0:T(8,128)(2,1)S(1)}, bf16[32,32,768]{2,1,0:T(8,128)(2,1)}, u32[]{:S(2)}) copy-start(bf16[32,32,768]{2,1,0:T(8,128)(2,1)} %refs_0_.3) | copy-start | bytes 4718596
  6.2 98.0 %all-to-all-start = ((bf16[16,8,32,768]{3,2,1,0:T(8,128)(2,1)}), bf16[16,8,32,768]{3,2,1,0:T(8,128)(2,1)}, u32[]{:S(2)}, u32[]{:S(2)}) async-start(bf16[16,8,32,768]{3,2,1,0:T(8,128)(2,1)} %column_pack.1), calls=%async_computation | async-start | bytes 12582912 | tf_op jit(solution)/shard_map/all_to_all | solution.py:263
  15.8 5.9 %copy-start.3 = (bf16[32,32,768]{2,1,0:T(8,128)(2,1)S(1)}, bf16[32,32,768]{2,1,0:T(8,128)(2,1)}, u32[]{:S(2)}) copy-start(bf16[32,32,768]{2,1,0:T(8,128)(2,1)} %refs_0_.2) | copy-start | bytes 4718596
  18.8 71.3 %copy-start.2 = (bf16[3,2,32,2048]{3,2,1,0:T(8,128)(2,1)}, bf16[3,2,32,2048]{3,2,1,0:T(8,128)(2,1)S(1)}, u32[]{:S(2)}) copy-start(bf16[3,2,32,2048]{3,2,1,0:T(8,128)(2,1)S(1)} %get-tuple-element.62.refs_0_) | copy-start | bytes 2359300
  18.8 30.0 %copy-start.4 = (bf16[32,32,768]{2,1,0:T(8,128)(2,1)S(1)}, bf16[32,32,768]{2,1,0:T(8,128)(2,1)}, u32[]{:S(2)}) copy-start(bf16[32,32,768]{2,1,0:T(8,128)(2,1)} %refs_0_.4) | copy-start | bytes 4718596
  18.8 37.5 %collective-permute-start.4 = (bf16[3,2,32,2048]{3,2,1,0:T(8,128)(2,1)S(1)}, bf16[3,2,32,2048]{3,2,1,0:T(8,128)(2,1)}, u32[]{:S(2)}, u32[]{:S(2)}) collective-permute-start(bf16[3,2,32,2048]{3,2,1,0:T(8,128)(2,1)S(1)} %get-tuple-element.64), channel_id=1, source_target_pairs={{0,2},{1,3},{2,0},{3,1},{4,6},{5,7},{6,4},{7,5},{8,10},{9,11},{10,... | collective-permute-start | bytes 2359304 | tf_op jit(solution)/shard_map/ppermute | solution.py:259
  23.2 68.9 %copy-start = (bf16[3,1,32,2048]{3,2,1,0:T(8,128)(2,1)}, bf16[3,1,32,2048]{3,2,1,0:T(8,128)(2,1)S(1)}, u32[]{:S(2)}) copy-start(bf16[3,1,32,2048]{3,2,1,0:T(8,128)(2,1)S(1)} %get-tuple-element.80.refs_4_.refs_0_) | copy-start | bytes 1179652
  23.2 25.6 %collective-permute-start = (bf16[3,1,32,2048]{3,2,1,0:T(8,128)(2,1)S(1)}, bf16[3,1,32,2048]{3,2,1,0:T(8,128)(2,1)S(1)}, u32[]{:S(2)}, u32[]{:S(2)}) collective-permute-start(bf16[3,1,32,2048]{3,2,1,0:T(8,128)(2,1)S(1)} %get-tuple-element.57), channel_id=1, source_target_pairs={{0,1},{1,2},{2,3},{3,0},{4,5},{5,6},{6,7},{7,4},{8,9},{9,10},{10,1... | collective-permute-start | bytes 1179656 | tf_op jit(solution)/shard_map/ppermute | solution.py:259
  23.6 32.7 %collective-permute-start.1 = (bf16[3,1,32,2048]{3,2,1,0:T(8,128)(2,1)S(1)}, bf16[3,1,32,2048]{3,2,1,0:T(8,128)(2,1)S(1)}, u32[]{:S(2)}, u32[]{:S(2)}) collective-permute-start(bf16[3,1,32,2048]{3,2,1,0:T(8,128)(2,1)S(1)} %get-tuple-element.58), channel_id=1, source_target_pairs={{0,2},{1,3},{2,0},{3,1},{4,6},{5,7},{6,4},{7,5},{8,10},{9,11},{10,... | collective-permute-start | bytes 1179656 | tf_op jit(solution)/shard_map/ppermute | solution.py:259
  25.3 31.5 %collective-permute-start.2 = (bf16[3,1,32,2048]{3,2,1,0:T(8,128)(2,1)S(1)}, bf16[3,1,32,2048]{3,2,1,0:T(8,128)(2,1)S(1)}, u32[]{:S(2)}, u32[]{:S(2)}) collective-permute-start(bf16[3,1,32,2048]{3,2,1,0:T(8,128)(2,1)S(1)} %get-tuple-element.59), channel_id=1, source_target_pairs={{0,3},{1,0},{2,1},{3,2},{4,7},{5,4},{6,5},{7,6},{8,11},{9,8},{10,9... | collective-permute-start | bytes 1179656 | tf_op jit(solution)/shard_map/ppermute | solution.py:259
  26.1 64.4 %collective-permute-start.3 = (bf16[3,2,32,2048]{3,2,1,0:T(8,128)(2,1)S(1)}, bf16[3,2,32,2048]{3,2,1,0:T(8,128)(2,1)}, u32[]{:S(2)}, u32[]{:S(2)}) collective-permute-start(bf16[3,2,32,2048]{3,2,1,0:T(8,128)(2,1)S(1)} %get-tuple-element.63), channel_id=1, source_target_pairs={{0,1},{1,2},{2,3},{3,0},{4,5},{5,6},{6,7},{7,4},{8,9},{9,10},{10,1... | collective-permute-start | bytes 2359304 | tf_op jit(solution)/shard_map/ppermute | solution.py:259
  48.8 43.3 %copy-start.10 = (bf16[3,1,32,2048]{3,2,1,0:T(8,128)(2,1)}, bf16[3,1,32,2048]{3,2,1,0:T(8,128)(2,1)S(1)}, u32[]{:S(2)}) copy-start(bf16[3,1,32,2048]{3,2,1,0:T(8,128)(2,1)S(1)} %collective-permute-done.refs_5_.refs_1_) | copy-start | bytes 1179652
  48.8 42.8 %collective-permute-start.5 = (bf16[3,2,32,2048]{3,2,1,0:T(8,128)(2,1)S(1)}, bf16[3,2,32,2048]{3,2,1,0:T(8,128)(2,1)}, u32[]{:S(2)}, u32[]{:S(2)}) collective-permute-start(bf16[3,2,32,2048]{3,2,1,0:T(8,128)(2,1)S(1)} %get-tuple-element.65), channel_id=1, source_target_pairs={{0,3},{1,0},{2,1},{3,2},{4,7},{5,4},{6,5},{7,6},{8,11},{9,8},{10,9... | collective-permute-start | bytes 2359304 | tf_op jit(solution)/shard_map/ppermute | solution.py:259
  50.4 42.4 %copy-start.6 = (bf16[3,1,32,2048]{3,2,1,0:T(8,128)(2,1)}, bf16[3,1,32,2048]{3,2,1,0:T(8,128)(2,1)S(1)}, u32[]{:S(2)}) copy-start(bf16[3,1,32,2048]{3,2,1,0:T(8,128)(2,1)S(1)} %get-tuple-element.67.refs_8_) | copy-start | bytes 1179652
  56.3 36.5 %copy-start.11 = (bf16[3,1,32,2048]{3,2,1,0:T(8,128)(2,1)}, bf16[3,1,32,2048]{3,2,1,0:T(8,128)(2,1)S(1)}, u32[]{:S(2)}) copy-start(bf16[3,1,32,2048]{3,2,1,0:T(8,128)(2,1)S(1)} %collective-permute-done.1.refs_6_.refs_2_) | copy-start | bytes 1179652
  56.3 26.2 %collective-permute-start.10 = (bf16[3,1,32,2048]{3,2,1,0:T(8,128)(2,1)S(1)}, bf16[3,1,32,2048]{3,2,1,0:T(8,128)(2,1)S(1)}, u32[]{:S(2)}, u32[]{:S(2)}) collective-permute-start(bf16[3,1,32,2048]{3,2,1,0:T(8,128)(2,1)S(1)} %get-tuple-element.68), channel_id=1, source_target_pairs={{0,1},{1,2},{2,3},{3,0},{4,5},{5,6},{6,7},{7,4},{8,9},{9,10},{10,1... | collective-permute-start | bytes 1179656 | tf_op jit(solution)/shard_map/ppermute | solution.py:259
  56.3 46.8 %collective-permute-start.8 = (bf16[3,2,32,2048]{3,2,1,0:T(8,128)(2,1)}, bf16[3,2,32,2048]{3,2,1,0:T(8,128)(2,1)}, u32[]{:S(2)}, u32[]{:S(2)}) collective-permute-start(bf16[3,2,32,2048]{3,2,1,0:T(8,128)(2,1)} %collective-permute-done.4.refs_2_), channel_id=1, source_target_pairs={{0,4},{4,0},{1,5},{5,1},{2,6},{6,2},{3,7},{7,3},{8,12},{12,8},{9,1... | collective-permute-start | bytes 2359304 | tf_op jit(solution)/shard_map/ppermute | solution.py:259
  56.8 36.0 %copy-start.13 = (bf16[3,1,32,2048]{3,2,1,0:T(8,128)(2,1)}, bf16[3,1,32,2048]{3,2,1,0:T(8,128)(2,1)S(1)}, u32[]{:S(2)}) copy-start(bf16[3,1,32,2048]{3,2,1,0:T(8,128)(2,1)S(1)} %collective-permute-done.2.refs_7_.refs_3_) | copy-start | bytes 1179652
  56.8 33.3 %collective-permute-start.11 = (bf16[3,1,32,2048]{3,2,1,0:T(8,128)(2,1)S(1)}, bf16[3,1,32,2048]{3,2,1,0:T(8,128)(2,1)S(1)}, u32[]{:S(2)}, u32[]{:S(2)}) collective-permute-start(bf16[3,1,32,2048]{3,2,1,0:T(8,128)(2,1)S(1)} %get-tuple-element.69), channel_id=1, source_target_pairs={{0,2},{1,3},{2,0},{3,1},{4,6},{5,7},{6,4},{7,5},{8,10},{9,11},{10,... | collective-permute-start | bytes 1179656 | tf_op jit(solution)/shard_map/ppermute | solution.py:259
  82.5 10.3 %copy-start.15 = (bf16[3,1,32,2048]{3,2,1,0:T(8,128)(2,1)}, bf16[3,1,32,2048]{3,2,1,0:T(8,128)(2,1)S(1)}, u32[]{:S(2)}) copy-start(bf16[3,1,32,2048]{3,2,1,0:T(8,128)(2,1)S(1)} %collective-permute-done.10.refs_9_) | copy-start | bytes 1179652
  82.5 10.3 %collective-permute-start.12 = (bf16[3,1,32,2048]{3,2,1,0:T(8,128)(2,1)S(1)}, bf16[3,1,32,2048]{3,2,1,0:T(8,128)(2,1)S(1)}, u32[]{:S(2)}, u32[]{:S(2)}) collective-permute-start(bf16[3,1,32,2048]{3,2,1,0:T(8,128)(2,1)S(1)} %get-tuple-element.70), channel_id=1, source_target_pairs={{0,3},{1,0},{2,1},{3,2},{4,7},{5,4},{6,5},{7,6},{8,11},{9,8},{10,9... | collective-permute-start | bytes 1179656 | tf_op jit(solution)/shard_map/ppermute | solution.py:259
  90.1 2.7 copy-start.16
  90.1 45.7 %collective-permute-start.6 = (bf16[3,2,32,2048]{3,2,1,0:T(8,128)(2,1)S(1)}, bf16[3,2,32,2048]{3,2,1,0:T(8,128)(2,1)}, u32[]{:S(2)}, u32[]{:S(2)}) collective-permute-start(bf16[3,2,32,2048]{3,2,1,0:T(8,128)(2,1)S(1)} %get-tuple-element.62.refs_0_), channel_id=1, source_target_pairs={{0,4},{4,0},{1,5},{5,1},{2,6},{6,2},{3,7},{7,3},{8,12},{12,8},{9,1... | collective-permute-start | bytes 2359304 | tf_op jit(solution)/shard_map/ppermute | solution.py:259
  90.5 46.3 %collective-permute-start.7 = (bf16[3,2,32,2048]{3,2,1,0:T(8,128)(2,1)}, bf16[3,2,32,2048]{3,2,1,0:T(8,128)(2,1)}, u32[]{:S(2)}, u32[]{:S(2)}) collective-permute-start(bf16[3,2,32,2048]{3,2,1,0:T(8,128)(2,1)} %collective-permute-done.3.refs_1_), channel_id=1, source_target_pairs={{0,4},{4,0},{1,5},{5,1},{2,6},{6,2},{3,7},{7,3},{8,12},{12,8},{9,1... | collective-permute-start | bytes 2359304 | tf_op jit(solution)/shard_map/ppermute | solution.py:259
  91.6 62.1 %collective-permute-start.9 = (bf16[3,2,32,2048]{3,2,1,0:T(8,128)(2,1)}, bf16[3,2,32,2048]{3,2,1,0:T(8,128)(2,1)}, u32[]{:S(2)}, u32[]{:S(2)}) collective-permute-start(bf16[3,2,32,2048]{3,2,1,0:T(8,128)(2,1)} %collective-permute-done.5.refs_3_), channel_id=1, source_target_pairs={{0,4},{4,0},{1,5},{5,1},{2,6},{6,2},{3,7},{7,3},{8,12},{12,8},{9,1... | collective-permute-start | bytes 2359304 | tf_op jit(solution)/shard_map/ppermute | solution.py:259
  92.8 0.7 copy-start.17
  103.1 67.3 %collective-permute-start.13 = (bf16[6,1,32,2048]{3,2,1,0:T(8,128)(2,1)S(1)}, bf16[6,1,32,2048]{3,2,1,0:T(8,128)(2,1)S(1)}, u32[]{:S(2)}, u32[]{:S(2)}) collective-permute-start(bf16[6,1,32,2048]{3,2,1,0:T(8,128)(2,1)S(1)} %pad_maximum_fusion), channel_id=1, source_target_pairs={{0,4},{4,0},{1,5},{5,1},{2,6},{6,2},{3,7},{7,3},{8,12},{12,8},{9,1... | collective-permute-start | bytes 2359304 | tf_op jit(solution)/shard_map/ppermute | solution.py:259
  133.7 2.2 copy-start.1
  158.4 24.1 %copy-start.12 = (bf16[3,1,32,2048]{3,2,1,0:T(8,128)(2,1)S(1)}, bf16[3,1,32,2048]{3,2,1,0:T(8,128)(2,1)}, u32[]{:S(2)}) copy-start(bf16[3,1,32,2048]{3,2,1,0:T(8,128)(2,1)} %copy-done.11) | copy-start | bytes 1179652
  158.4 24.1 %copy-start.14 = (bf16[3,1,32,2048]{3,2,1,0:T(8,128)(2,1)S(1)}, bf16[3,1,32,2048]{3,2,1,0:T(8,128)(2,1)}, u32[]{:S(2)}) copy-start(bf16[3,1,32,2048]{3,2,1,0:T(8,128)(2,1)} %copy-done.13) | copy-start | bytes 1179652
  158.4 23.5 %all-to-all-start.1 = ((f32[16,2,3,2,8,128]{5,4,3,2,1,0:T(8,128)}), f32[16,2,3,2,8,128]{5,4,3,2,1,0:T(8,128)S(1)}, u32[]{:S(2)}, u32[]{:S(2)}) async-start(f32[16,2,3,2,8,128]{5,4,3,2,1,0:T(8,128)} %tied_terms.3), calls=%async_computation.1 | async-start | bytes 1572864 | tf_op jit(solution)/shard_map/all_to_all | solution.py:263
  182.0 3.0 %collective-permute-start.14 = (f32[2,3,2,8,128]{4,3,2,1,0:T(8,128)S(1)}, f32[2,3,2,8,128]{4,3,2,1,0:T(8,128)S(1)}, u32[]{:S(2)}, u32[]{:S(2)}) collective-permute-start(f32[2,3,2,8,128]{4,3,2,1,0:T(8,128)S(1)} %reduce_sum.27), channel_id=1, source_target_pairs={{0,4},{4,0},{1,5},{5,1},{2,6},{6,2},{3,7},{7,3},{8,12},{12,8},{9,1... | collective-permute-start | bytes 147464 | tf_op jit(solution)/shard_map/ppermute | solution.py:259
  186.7 25.8 %collective-permute-start.16 = (bf16[6,1,32,2048]{3,2,1,0:T(8,128)(2,1)S(1)}, bf16[6,1,32,2048]{3,2,1,0:T(8,128)(2,1)S(1)}, u32[]{:S(2)}, u32[]{:S(2)}) collective-permute-start(bf16[6,1,32,2048]{3,2,1,0:T(8,128)(2,1)S(1)} %pad_maximum_fusion.1), channel_id=1, source_target_pairs={{0,4},{4,0},{1,5},{5,1},{2,6},{6,2},{3,7},{7,3},{8,12},{12,8},{9,1... | collective-permute-start | bytes 2359304 | tf_op jit(solution)/shard_map/ppermute | solution.py:259
  212.5 61.9 %all-to-all-start.3 = ((bf16[16,6,32,768]{3,2,1,0:T(8,128)(2,1)}), bf16[16,6,32,768]{3,2,1,0:T(8,128)(2,1)}, u32[]{:S(2)}, u32[]{:S(2)}) async-start(bf16[16,6,32,768]{3,2,1,0:T(8,128)(2,1)} %copy-done.1), calls=%async_computation.3 | async-start | bytes 9437184 | tf_op jit(solution)/shard_map/all_to_all | solution.py:263
  224.1 18.9 %collective-permute-start.15 = (bf16[3,1,32,2048]{3,2,1,0:T(8,128)(2,1)}, bf16[3,1,32,2048]{3,2,1,0:T(8,128)(2,1)S(1)}, u32[]{:S(2)}, u32[]{:S(2)}) collective-permute-start(bf16[3,1,32,2048]{3,2,1,0:T(8,128)(2,1)} %get-tuple-element.79), channel_id=1, source_target_pairs={{0,3},{1,0},{2,1},{3,2},{4,7},{5,4},{6,5},{7,6},{8,11},{9,8},{10,9... | collective-permute-start | bytes 1179656 | tf_op jit(solution)/shard_map/ppermute | solution.py:259
  226.6 20.8 %collective-permute-start.23 = (bf16[3,1,32,2048]{3,2,1,0:T(8,128)(2,1)}, bf16[3,1,32,2048]{3,2,1,0:T(8,128)(2,1)S(1)}, u32[]{:S(2)}, u32[]{:S(2)}) collective-permute-start(bf16[3,1,32,2048]{3,2,1,0:T(8,128)(2,1)} %get-tuple-element.102), channel_id=1, source_target_pairs={{0,2},{1,3},{2,0},{3,1},{4,6},{5,7},{6,4},{7,5},{8,10},{9,11},{10,... | collective-permute-start | bytes 1179656 | tf_op jit(solution)/shard_map/ppermute | solution.py:259
  227.2 24.3 %collective-permute-start.24 = (bf16[3,1,32,2048]{3,2,1,0:T(8,128)(2,1)}, bf16[3,1,32,2048]{3,2,1,0:T(8,128)(2,1)S(1)}, u32[]{:S(2)}, u32[]{:S(2)}) collective-permute-start(bf16[3,1,32,2048]{3,2,1,0:T(8,128)(2,1)} %get-tuple-element.103), channel_id=1, source_target_pairs={{0,1},{1,2},{2,3},{3,0},{4,5},{5,6},{6,7},{7,4},{8,9},{9,10},{10,1... | collective-permute-start | bytes 1179656 | tf_op jit(solution)/shard_map/ppermute | solution.py:259
  227.8 32.0 %collective-permute-start.20 = (bf16[3,1,32,2048]{3,2,1,0:T(8,128)(2,1)}, bf16[3,1,32,2048]{3,2,1,0:T(8,128)(2,1)S(1)}, u32[]{:S(2)}, u32[]{:S(2)}) collective-permute-start(bf16[3,1,32,2048]{3,2,1,0:T(8,128)(2,1)} %get-tuple-element.98), channel_id=1, source_target_pairs={{0,3},{1,0},{2,1},{3,2},{4,7},{5,4},{6,5},{7,6},{8,11},{9,8},{10,9... | collective-permute-start | bytes 1179656 | tf_op jit(solution)/shard_map/ppermute | solution.py:259
  229.8 32.6 %collective-permute-start.21 = (bf16[3,1,32,2048]{3,2,1,0:T(8,128)(2,1)}, bf16[3,1,32,2048]{3,2,1,0:T(8,128)(2,1)S(1)}, u32[]{:S(2)}, u32[]{:S(2)}) collective-permute-start(bf16[3,1,32,2048]{3,2,1,0:T(8,128)(2,1)} %get-tuple-element.99), channel_id=1, source_target_pairs={{0,2},{1,3},{2,0},{3,1},{4,6},{5,7},{6,4},{7,5},{8,10},{9,11},{10,... | collective-permute-start | bytes 1179656 | tf_op jit(solution)/shard_map/ppermute | solution.py:259
  243.0 22.4 %collective-permute-start.22 = (bf16[3,1,32,2048]{3,2,1,0:T(8,128)(2,1)}, bf16[3,1,32,2048]{3,2,1,0:T(8,128)(2,1)S(1)}, u32[]{:S(2)}, u32[]{:S(2)}) collective-permute-start(bf16[3,1,32,2048]{3,2,1,0:T(8,128)(2,1)} %get-tuple-element.100), channel_id=1, source_target_pairs={{0,1},{1,2},{2,3},{3,0},{4,5},{5,6},{6,7},{7,4},{8,9},{9,10},{10,1... | collective-permute-start | bytes 1179656 | tf_op jit(solution)/shard_map/ppermute | solution.py:259
  243.0 16.8 %copy-start.8 = (bf16[3,1,32,2048]{3,2,1,0:T(8,128)(2,1)S(1)}, bf16[3,1,32,2048]{3,2,1,0:T(8,128)(2,1)}, u32[]{:S(2)}) copy-start(bf16[3,1,32,2048]{3,2,1,0:T(8,128)(2,1)} %get-tuple-element.101.refs_0_) | copy-start | bytes 1179652
  247.5 31.5 %collective-permute-start.17 = (bf16[3,1,32,2048]{3,2,1,0:T(8,128)(2,1)}, bf16[3,1,32,2048]{3,2,1,0:T(8,128)(2,1)S(1)}, u32[]{:S(2)}, u32[]{:S(2)}) collective-permute-start(bf16[3,1,32,2048]{3,2,1,0:T(8,128)(2,1)} %get-tuple-element.86), channel_id=1, source_target_pairs={{0,3},{1,0},{2,1},{3,2},{4,7},{5,4},{6,5},{7,6},{8,11},{9,8},{10,9... | collective-permute-start | bytes 1179656 | tf_op jit(solution)/shard_map/ppermute | solution.py:259
  251.5 27.6 %collective-permute-start.18 = (bf16[3,1,32,2048]{3,2,1,0:T(8,128)(2,1)}, bf16[3,1,32,2048]{3,2,1,0:T(8,128)(2,1)S(1)}, u32[]{:S(2)}, u32[]{:S(2)}) collective-permute-start(bf16[3,1,32,2048]{3,2,1,0:T(8,128)(2,1)} %get-tuple-element.87), channel_id=1, source_target_pairs={{0,2},{1,3},{2,0},{3,1},{4,6},{5,7},{6,4},{7,5},{8,10},{9,11},{10,... | collective-permute-start | bytes 1179656 | tf_op jit(solution)/shard_map/ppermute | solution.py:259
  259.8 21.6 %collective-permute-start.19 = (bf16[3,1,32,2048]{3,2,1,0:T(8,128)(2,1)}, bf16[3,1,32,2048]{3,2,1,0:T(8,128)(2,1)S(1)}, u32[]{:S(2)}, u32[]{:S(2)}) collective-permute-start(bf16[3,1,32,2048]{3,2,1,0:T(8,128)(2,1)} %get-tuple-element.88), channel_id=1, source_target_pairs={{0,1},{1,2},{2,3},{3,0},{4,5},{5,6},{6,7},{7,4},{8,9},{9,10},{10,1... | collective-permute-start | bytes 1179656 | tf_op jit(solution)/shard_map/ppermute | solution.py:259
  259.8 5.6 %copy-start.7 = (bf16[3,1,32,2048]{3,2,1,0:T(8,128)(2,1)S(1)}, bf16[3,1,32,2048]{3,2,1,0:T(8,128)(2,1)}, u32[]{:S(2)}) copy-start(bf16[3,1,32,2048]{3,2,1,0:T(8,128)(2,1)} %get-tuple-element.97.refs_0_) | copy-start | bytes 1179652
  268.0 13.5 %copy-start.9 = (bf16[3,1,32,2048]{3,2,1,0:T(8,128)(2,1)S(1)}, bf16[3,1,32,2048]{3,2,1,0:T(8,128)(2,1)}, u32[]{:S(2)}) copy-start(bf16[3,1,32,2048]{3,2,1,0:T(8,128)(2,1)} %get-tuple-element.93.refs_0_) | copy-start | bytes 1179652

commit v5 on v4

--- a/solution.py
+++ b/solution.py
@@ -181,30 +181,30 @@
     return jnp.concatenate([ref[0, i] for ref in refs], axis=0)
 
 
-def terms_kernel(*refs, parts):
-    left, keys, values = (refs[i * parts : (i + 1) * parts] for i in range(3))
+def terms_kernel(*refs, count, parts):
+    left, keys, values = refs[:count], refs[count : count + parts], refs[count + parts :][:parts]
     o_ref = refs[-1]
     for i, right in enumerate((keys, values)):
         terms = nt(joined(left, i), joined(right, 0))
         o_ref[:, i, 0, 0] = terms.reshape(o_ref.shape[0], -1, terms.shape[1])
 
 
-def tied_terms(left, keys, values, slices, side, held=()):
-    parts = len(left)
+def tied_terms(left, keys, values, slices, side, first=0, held=()):
+    parts, count = len(keys), len(left)
     heads, _, columns, width = left[0].shape
     wide = parts * columns
-    step = wide // slices
-    return pl.pallas_call(
-        functools.partial(terms_kernel, parts=parts),
+    step, span = wide // slices, slices * count // parts
+    return pl.pallas_call(
+        functools.partial(terms_kernel, count=count, parts=parts),
         grid=(heads,),
-        in_specs=[pl.BlockSpec((1, 2, columns, width), lambda i: (i, 0, 0, 0))] * parts
+        in_specs=[pl.BlockSpec((1, 2, columns, width), lambda i: (i, 0, 0, 0))] * count
         + [pl.BlockSpec((1, 1, columns, width), lambda i: (i, 0, 0, 0))] * (2 * parts)
         + [pl.BlockSpec(memory_space=pl.ANY)] * len(held),
         out_specs=pl.BlockSpec(
-            (slices, 2, 1, 1, step, wide), lambda i: (0, 0, i, side, 0, 0)
+            (span, 2, 1, 1, step, wide), lambda i: (first // count, 0, i, side, 0, 0)
         ),
         out_shape=jax.ShapeDtypeStruct((slices, 2, heads, 2, step, wide), jnp.float32),
-        input_output_aliases={3 * parts: 0} if held else {},
+        input_output_aliases={count + 2 * parts: 0} if held else {},
         compiler_params=params(VMEM_ALL),
         cost_estimate=COST,
         name="tied_terms",
@@ -238,6 +238,12 @@
 def tied_grads(kernel, own, other, tied, factor, name):
     parts = len(own)
     heads, n, columns, width = own[0].shape
+    places = [
+        pl.BlockSpec((1, n, columns, width), lambda i, at=at: (at + i, 0, 0, 0))
+        for x in other
+        for at in range(0, x.shape[0], heads)
+    ]
+    other = [x for x in other for _ in range(0, x.shape[0], heads)]
     wide = parts * columns
     chunk = pl.BlockSpec((1, n, columns, width), lambda i: (i, 0, 0, 0))
     one = pl.BlockSpec((1, 1, columns, width), lambda i: (i, 0, 0, 0))
@@ -245,7 +251,7 @@
     return pl.pallas_call(
         functools.partial(kernel, parts=parts, factor=factor),
         grid=(heads,),
-        in_specs=[chunk] * (2 * parts) + [square],
+        in_specs=[chunk] * parts + places + [square],
         out_specs=[one] * (n * parts),
         out_shape=[jax.ShapeDtypeStruct((heads, 1, columns, width), jnp.bfloat16)] * (n * parts),
         compiler_params=params(VMEM_ALL),
@@ -351,17 +357,12 @@
         return [shift(c, "yl", 1) for c in after(keys, others)]
 
     early = across([jnp.concatenate(keys[:2])], other[-2])[0]
-    left, half = after((other, half), col_done)
-    terms = over_rows(tied_terms(left, keys, values, groups, 1, (half,)))
+    left, half = after((other[:-1], half), col_done)
+    half = tied_terms(left, keys, values, groups, 1, 0, (half,))
+    terms = over_rows(tied_terms(other[-1:], keys, values, groups, 1, parts - 1, (half,)))
     sums = jnp.sum(after(terms, early), axis=0)
     swapped = shift(sums, "yl", 1)
     late = across([jnp.concatenate(keys[2:])], swapped)[0]
-    other_keys = [
-        part[at : at + head_group]
-        for part in (early, late)
-        for at in range(0, part.shape[0], head_group)
-    ]
-
     logits, dprobs = jnp.concatenate([sums, jnp.flip(swapped, 2)], axis=-1)
     probs = jax.nn.softmax(logits * row_factor, axis=-1)
     slopes = probs * (dprobs - jnp.sum(probs * dprobs, axis=-1, keepdims=True))
@@ -385,7 +386,7 @@
     key_chunks, value_chunks = back(pair_grads[:parts]), back(pair_grads[parts:])
     col_grads = column_unpack(over_rows(after(col_done, whole, late)), pieces)
     keys = after(keys, value_chunks[1])
-    query_grads = tied_grads(query_grads_kernel, keys, other_keys, whole, row_factor, "query_grads")
+    query_grads = tied_grads(query_grads_kernel, keys, [early, late], whole, row_factor, "query_grads")
     chunks = (back(query_grads), key_chunks, value_chunks)
     row_grads = [unpack_rows(here, c)[0] for c in chunks[1:]]
     row_grads.insert(0, unpack_rows(here, after(chunks[0], col_grads))[0])

time: 285 us -> 284 us (level)
  Pallas kernels: 72.9 us -> 77.1 us
  waiting for transfers between devices: 130 us -> 126 us
    pallas_call x2 -> x3, Pallas kernels: 9.36 us -> 13.5 us  [tied_terms(): pl.pallas_call(functools.partial(terms_kernel, count=count, parts=parts),...]
    ppermute x25, waiting for transfers between devices: 112 us -> 108 us  [shift(): return lax.ppermute(x, axis, [(i, (i + by) % n) for i in range(n)])]
  transfers between devices with their start and end apart: 28 -> 28, of which waited for: 16 -> 16; matrix products, arithmetic and copies ran while one was open for 1% -> 0% of each run, Pallas kernels for 23% -> 24%
where the time goes in v5:
time: 284 us; the launch traced here: 283 us
  waiting for transfers between devices  126 us (44%)
  Pallas kernels  77.1 us (27%)
  starting transfers between devices  48.6 us (17%)
  blocking collectives  24.3 us (9%)
  local copies, waits for them, and re-layouts  3.96 us (1%)
    ppermute x25, waiting for transfers between devices, shift(): return lax.ppermute(x, axis, [(i, (i + by) % n) for i in range(n)])  108 us
    pallas_call x1, Pallas kernels, column_backward(): pl.pallas_call(functools.partial(column_kernel, chunk=chunk), grid=(piece...  29.5 us
    ppermute x25, starting transfers between devices, shift(): return lax.ppermute(x, axis, [(i, (i + by) % n) for i in range(n)])  25.8 us
    all_to_all x1, blocking collectives, over_rows(): return lax.all_to_all(x, ROWS, split_axis=0, concat_axis=0, tiled=True)  24.3 us
    all_to_all x3, starting transfers between devices, over_rows(): return lax.all_to_all(x, ROWS, split_axis=0, concat_axis=0, tiled=True)  22.8 us
    all_to_all x3, waiting for transfers between devices, over_rows(): return lax.all_to_all(x, ROWS, split_axis=0, concat_axis=0, tiled=True)  18.8 us
    pallas_call x3, Pallas kernels, tied_terms(): pl.pallas_call(functools.partial(terms_kernel, count=count, parts=parts),...  13.5 us
    pallas_call x2, Pallas kernels, tied_grads(): pl.pallas_call(functools.partial(kernel, parts=parts, factor=factor), gri...  10.1 us
  transfers between devices with their start and end apart: 28, of which 16 were waited for; matrix products, arithmetic and copies ran while one was open for 0% of the time, Pallas kernels for 24%

profile of v5, /device:TPU:1, one launch (start us, length us, event | category | flops | bytes accessed | tf_op | source)
XLA Modules:
  0.0 283.2 jit_solution(4535913978499957865)
XLA Ops:
  0.6 5.5 %column_pack.1 = bf16[16,8,32,768]{3,2,1,0:T(8,128)(2,1)} custom-call(bf16[32,32,768]{2,1,0:T(8,128)(2,1)} %refs_0_.1, bf16[32,32,768]{2,1,0:T(8,128)(2,1)} %refs_1_.1, bf16[32,32,768]{2,1,0:T(8,128)(2,1)} %refs_2_.1, bf16[32,32,768]{2,1,0:T(8,128)(2,1)} %refs_3_.1), custom_call_target="tpu_custom_call" | custom-call | flops 1 | bytes 1 | tf_op jit(solution)/shard_map/column_pack/pallas_call | solution.py:296
  6.2 9.6 %all-to-all-start = ((bf16[16,8,32,768]{3,2,1,0:T(8,128)(2,1)}), bf16[16,8,32,768]{3,2,1,0:T(8,128)(2,1)}, u32[]{:S(2)}, u32[]{:S(2)}) async-start(bf16[16,8,32,768]{3,2,1,0:T(8,128)(2,1)} %column_pack.1), calls=%async_computation | async-start | bytes 12582912 | tf_op jit(solution)/shard_map/all_to_all | solution.py:269
  15.8 3.0 %pack_rows.4 = (bf16[3,2,32,2048]{3,2,1,0:T(8,128)(2,1)S(1)}, bf16[3,2,32,2048]{3,2,1,0:T(8,128)(2,1)S(1)}, bf16[3,2,32,2048]{3,2,1,0:T(8,128)(2,1)S(1)}, bf16[3,2,32,2048]{3,2,1,0:T(8,128)(2,1)S(1)}) custom-call(s32[1]{0:T(128)} %bitcast.here_ref, bf16[32,32,768]{2,1,0:T(8,128)(2,1)S(1)} %copy-done.6, bf16[32,32,768]{2,1,0:T(8,128)(2,1)} %refs_1_.2), custom_call_target="tpu_custom_call" | custom-call | flops 1 | bytes 1 | tf_op jit(solution)/shard_map/pack_rows/pallas_call | solution.py:121
  18.8 2.8 collective-permute-start.4
  21.6 1.6 pack_rows.3
  23.6 1.7 collective-permute-start.1
  25.4 0.8 collective-permute-start.2
  26.8 22.0 %collective-permute-done.refs_5_.refs_4_.refs_2_.refs_1_ = bf16[3,1,32,2048]{3,2,1,0:T(8,128)(2,1)S(1)} collective-permute-done((bf16[3,1,32,2048]{3,2,1,0:T(8,128)(2,1)S(1)}, bf16[3,1,32,2048]{3,2,1,0:T(8,128)(2,1)S(1)}, u32[]{:S(2)}, u32[]{:S(2)}) %collective-permute-start) | collective-permute-done | bytes 393248 | tf_op jit(solution)/shard_map/ppermute | solution.py:265
  48.8 1.6 pack_rows.5
  50.5 5.9 %collective-permute-done.1.refs_6_.refs_5_.refs_3_.refs_2_ = bf16[3,1,32,2048]{3,2,1,0:T(8,128)(2,1)S(1)} collective-permute-done((bf16[3,1,32,2048]{3,2,1,0:T(8,128)(2,1)S(1)}, bf16[3,1,32,2048]{3,2,1,0:T(8,128)(2,1)S(1)}, u32[]{:S(2)}, u32[]{:S(2)}) %collective-permute-start.1) | collective-permute-done | bytes 393248 | tf_op jit(solution)/shard_map/ppermute | solution.py:265
  56.8 2.9 %collective-permute-start.11 = (bf16[3,1,32,2048]{3,2,1,0:T(8,128)(2,1)S(1)}, bf16[3,1,32,2048]{3,2,1,0:T(8,128)(2,1)S(1)}, u32[]{:S(2)}, u32[]{:S(2)}) collective-permute-start(bf16[3,1,32,2048]{3,2,1,0:T(8,128)(2,1)S(1)} %get-tuple-element.68), channel_id=1, source_target_pairs={{0,2},{1,3},{2,0},{3,1},{4,6},{5,7},{6,4},{7,5},{8,10},{9,11},{10,... | collective-permute-start | bytes 1179656 | tf_op jit(solution)/shard_map/ppermute | solution.py:265
  59.7 22.8 %collective-permute-done.10.refs_9_.refs_8_.refs_6_ = bf16[3,1,32,2048]{3,2,1,0:T(8,128)(2,1)S(1)} collective-permute-done((bf16[3,1,32,2048]{3,2,1,0:T(8,128)(2,1)S(1)}, bf16[3,1,32,2048]{3,2,1,0:T(8,128)(2,1)S(1)}, u32[]{:S(2)}, u32[]{:S(2)}) %collective-permute-start.10) | collective-permute-done | bytes 393248 | tf_op jit(solution)/shard_map/ppermute | solution.py:265
  82.5 7.6 %collective-permute-done.11.refs_10_.refs_9_.refs_7_ = bf16[3,1,32,2048]{3,2,1,0:T(8,128)(2,1)S(1)} collective-permute-done((bf16[3,1,32,2048]{3,2,1,0:T(8,128)(2,1)S(1)}, bf16[3,1,32,2048]{3,2,1,0:T(8,128)(2,1)S(1)}, u32[]{:S(2)}, u32[]{:S(2)}) %collective-permute-start.11) | collective-permute-done | bytes 393248 | tf_op jit(solution)/shard_map/ppermute | solution.py:265
  90.5 1.1 collective-permute-start.7
  92.1 0.7 collective-permute-done.12.refs_11_.refs_10_.refs_8_
  93.6 4.7 %tied_terms.3.refs_11_ = f32[16,2,3,2,8,128]{5,4,3,2,1,0:T(8,128)} custom-call(bf16[3,2,32,2048]{3,2,1,0:T(8,128)(2,1)} %copy-done.3, bf16[3,2,32,2048]{3,2,1,0:T(8,128)(2,1)} %collective-permute-done.3.refs_1_, bf16[3,2,32,2048]{3,2,1,0:T(8,128)(2,1)} %collective-permute-done.4.refs_2_, bf16[3,2,32,2048]{3,2,1,0:T(8,128)(2,1)} %collective-permute-done.5.refs_3_, ...), custom_call_target="tpu_custom_call" | custom-call | flops 1 | bytes 1 | tf_op jit(solution)/shard_map/tied_terms/pallas_call | solution.py:197
  98.2 4.9 %collective-permute-done.8.refs_2_.refs_6_ = bf16[3,2,32,2048]{3,2,1,0:T(8,128)(2,1)} collective-permute-done((bf16[3,2,32,2048]{3,2,1,0:T(8,128)(2,1)}, bf16[3,2,32,2048]{3,2,1,0:T(8,128)(2,1)}, u32[]{:S(2)}, u32[]{:S(2)}) %collective-permute-start.8) | collective-permute-done | bytes 786464 | tf_op jit(solution)/shard_map/ppermute | solution.py:265
  103.1 1.1 collective-permute-start.13
  104.2 29.5 %column_attention.1 = bf16[16,6,32,768]{3,2,1,0:T(8,128)(2,1)S(1)} custom-call(bf16[16,8,32,768]{3,2,1,0:T(8,128)(2,1)} %all-to-all-done.x_ref), custom_call_target="tpu_custom_call" | custom-call | flops 8053063680 | bytes 11010048 | tf_op jit(solution)/shard_map/column_attention/pallas_call | solution.py:80
  133.7 2.1 copy-done.1
  135.8 1.0 collective-permute-done.7.refs_1_.refs_5_
  136.9 4.6 %tied_terms.4.refs_9_ = f32[16,2,3,2,8,128]{5,4,3,2,1,0:T(8,128)} custom-call(bf16[3,2,32,2048]{3,2,1,0:T(8,128)(2,1)} %collective-permute-done.6.refs_0_.refs_4_, bf16[3,2,32,2048]{3,2,1,0:T(8,128)(2,1)} %collective-permute-done.7.refs_1_.refs_5_, bf16[3,2,32,2048]{3,2,1,0:T(8,128)(2,1)} %collective-permute-done.8.refs_2_.refs_6_, ...), custom_call_target="tpu_custom_call", output_to_operand_aliasing={{}: (11, {})} | custom-call | flops 1 | bytes 1 | tf_op jit(solution)/shard_map/tied_terms/pallas_call | solution.py:197
  141.4 12.3 %collective-permute-done.9.refs_0_.refs_7_ = bf16[3,2,32,2048]{3,2,1,0:T(8,128)(2,1)} collective-permute-done((bf16[3,2,32,2048]{3,2,1,0:T(8,128)(2,1)}, bf16[3,2,32,2048]{3,2,1,0:T(8,128)(2,1)}, u32[]{:S(2)}, u32[]{:S(2)}) %collective-permute-start.9) | collective-permute-done | bytes 786464 | tf_op jit(solution)/shard_map/ppermute | solution.py:265
  153.7 4.3 %tied_terms.5 = f32[16,2,3,2,8,128]{5,4,3,2,1,0:T(8,128)} custom-call(bf16[3,2,32,2048]{3,2,1,0:T(8,128)(2,1)} %collective-permute-done.9.refs_0_.refs_7_, bf16[3,1,32,2048]{3,2,1,0:T(8,128)(2,1)} %copy-done, bf16[3,1,32,2048]{3,2,1,0:T(8,128)(2,1)} %copy-done.10, bf16[3,1,32,2048]{3,2,1,0:T(8,128)(2,1)} %copy-done.11, ...), custom_call_target="tpu_custom_call", output_to_operand_aliasing={{}: (9, {})} | custom-call | flops 1 | bytes 1 | tf_op jit(solution)/shard_map/tied_terms/pallas_call | solution.py:197
  158.0 8.1 %all-to-all-start.1 = ((f32[16,2,3,2,8,128]{5,4,3,2,1,0:T(8,128)}), f32[16,2,3,2,8,128]{5,4,3,2,1,0:T(8,128)S(1)}, u32[]{:S(2)}, u32[]{:S(2)}) async-start(f32[16,2,3,2,8,128]{5,4,3,2,1,0:T(8,128)} %tied_terms.5), calls=%async_computation.1 | async-start | bytes 1572864 | tf_op jit(solution)/shard_map/all_to_all | solution.py:269
  166.0 4.4 %collective-permute-done.13.refs_4_.refs_5_ = bf16[6,1,32,2048]{3,2,1,0:T(8,128)(2,1)S(1)} collective-permute-done((bf16[6,1,32,2048]{3,2,1,0:T(8,128)(2,1)S(1)}, bf16[6,1,32,2048]{3,2,1,0:T(8,128)(2,1)S(1)}, u32[]{:S(2)}, u32[]{:S(2)}) %collective-permute-start.13) | collective-permute-done | bytes 786464 | tf_op jit(solution)/shard_map/ppermute | solution.py:265
  170.5 11.5 %all-to-all-done.1 = f32[16,2,3,2,8,128]{5,4,3,2,1,0:T(8,128)S(1)} async-done(((f32[16,2,3,2,8,128]{5,4,3,2,1,0:T(8,128)}), f32[16,2,3,2,8,128]{5,4,3,2,1,0:T(8,128)S(1)}, u32[]{:S(2)}, u32[]{:S(2)}) %all-to-all-start.1) | async-done | bytes 786464 | tf_op jit(solution)/shard_map/all_to_all | solution.py:269
  182.5 2.5 collective-permute-done.14
  185.1 1.4 fusion.26
  187.3 24.3 %all_to_all.20 = bf16[16,5,3,8,128]{4,3,2,1,0:T(8,128)(2,1)S(1)} all-to-all(bf16[16,5,3,8,128]{4,3,2,1,0:T(8,128)(2,1)S(1)} %broadcast_in_dim.2), channel_id=1, replica_groups=mesh['z'=4,'yh'=2,'core'=2,'yl'=2,'x'=4] {'z','yh','core'}, dimensions={0} | all-to-all | bytes 983040 | tf_op jit(solution)/shard_map/all_to_all | solution.py:269
  211.6 0.9 copy_bitcast_fusion.refs_8_
  212.5 5.1 %all-to-all-start.3 = ((bf16[16,6,32,768]{3,2,1,0:T(8,128)(2,1)}), bf16[16,6,32,768]{3,2,1,0:T(8,128)(2,1)}, u32[]{:S(2)}, u32[]{:S(2)}) async-start(bf16[16,6,32,768]{3,2,1,0:T(8,128)(2,1)} %copy-done.1), calls=%async_computation.3 | async-start | bytes 9437184 | tf_op jit(solution)/shard_map/all_to_all | solution.py:269
  217.6 5.6 %pair_grads.1 = (bf16[3,1,32,2048]{3,2,1,0:T(8,128)(2,1)}, bf16[3,1,32,2048]{3,2,1,0:T(8,128)(2,1)}, bf16[3,1,32,2048]{3,2,1,0:T(8,128)(2,1)}, bf16[3,1,32,2048]...) custom-call(bf16[3,2,32,2048]{3,2,1,0:T(8,128)(2,1)} %copy-done.3, ...), custom_call_target="tpu_custom_call" | custom-call | flops 1 | bytes 1 | tf_op jit(solution)/shard_map/pair_grads/pallas_call | solution.py:251
  223.2 2.5 collective-permute-start.15
  226.9 2.1 collective-permute-start.20
  228.9 1.2 collective-permute-start.21
  230.2 11.9 %collective-permute-done.15.refs_1_ = bf16[3,1,32,2048]{3,2,1,0:T(8,128)(2,1)S(1)} collective-permute-done((bf16[3,1,32,2048]{3,2,1,0:T(8,128)(2,1)}, bf16[3,1,32,2048]{3,2,1,0:T(8,128)(2,1)S(1)}, u32[]{:S(2)}, u32[]{:S(2)}) %collective-permute-start.15) | collective-permute-done | bytes 393248 | tf_op jit(solution)/shard_map/ppermute | solution.py:265
  242.0 4.5 %query_grads.1 = (bf16[3,1,32,2048]{3,2,1,0:T(8,128)(2,1)}, bf16[3,1,32,2048]{3,2,1,0:T(8,128)(2,1)}, bf16[3,1,32,2048]{3,2,1,0:T(8,128)(2,1)}, bf16[3,1,32,2048]{3,2,1,0:T(8,128)(2,1)}) custom-call(bf16[3,1,32,2048]{3,2,1,0:T(8,128)(2,1)} %copy-done, bf16[3,1,32,2048]{3,2,1,0:T(8,128)(2,1)} %copy-done.10, bf16[3,1,32,2048]{3,2,1,0:T(8,128)(2,1)} %copy-done.11, ...), custom_call_target="tpu_custom_call" | custom-call | flops 1 | bytes 1 | tf_op jit(solution)/shard_map/query_grads/pallas_call | solution.py:251
  246.5 4.0 %collective-permute-start.17 = (bf16[3,1,32,2048]{3,2,1,0:T(8,128)(2,1)}, bf16[3,1,32,2048]{3,2,1,0:T(8,128)(2,1)S(1)}, u32[]{:S(2)}, u32[]{:S(2)}) collective-permute-start(bf16[3,1,32,2048]{3,2,1,0:T(8,128)(2,1)} %get-tuple-element.84), channel_id=1, source_target_pairs={{0,3},{1,0},{2,1},{3,2},{4,7},{5,4},{6,5},{7,6},{8,11},{9,8},{10,9... | collective-permute-start | bytes 1179656 | tf_op jit(solution)/shard_map/ppermute | solution.py:265
  250.5 1.2 collective-permute-start.18
  251.8 7.1 %collective-permute-done.20.refs_1_ = bf16[3,1,32,2048]{3,2,1,0:T(8,128)(2,1)S(1)} collective-permute-done((bf16[3,1,32,2048]{3,2,1,0:T(8,128)(2,1)}, bf16[3,1,32,2048]{3,2,1,0:T(8,128)(2,1)S(1)}, u32[]{:S(2)}, u32[]{:S(2)}) %collective-permute-start.20) | collective-permute-done | bytes 393248 | tf_op jit(solution)/shard_map/ppermute | solution.py:265
  258.9 2.6 unpack_rows.5
  261.5 3.0 %collective-permute-done.22.refs_3_ = bf16[3,1,32,2048]{3,2,1,0:T(8,128)(2,1)S(1)} collective-permute-done((bf16[3,1,32,2048]{3,2,1,0:T(8,128)(2,1)}, bf16[3,1,32,2048]{3,2,1,0:T(8,128)(2,1)S(1)}, u32[]{:S(2)}, u32[]{:S(2)}) %collective-permute-start.22) | collective-permute-done | bytes 393248 | tf_op jit(solution)/shard_map/ppermute | solution.py:265
  264.5 2.6 unpack_rows.4
  267.1 7.3 %all-to-all-done.3.x_ref = bf16[16,6,32,768]{3,2,1,0:T(8,128)(2,1)} async-done(((bf16[16,6,32,768]{3,2,1,0:T(8,128)(2,1)}), bf16[16,6,32,768]{3,2,1,0:T(8,128)(2,1)}, u32[]{:S(2)}, u32[]{:S(2)}) %all-to-all-start.3) | async-done | bytes 4718624 | tf_op jit(solution)/shard_map/all_to_all | solution.py:269
  274.4 4.7 %column_unpack.1 = (bf16[32,32,768]{2,1,0:T(8,128)(2,1)}, bf16[32,32,768]{2,1,0:T(8,128)(2,1)}, bf16[32,32,768]{2,1,0:T(8,128)(2,1)}) custom-call(bf16[16,6,32,768]{3,2,1,0:T(8,128)(2,1)} %all-to-all-done.3.x_ref), custom_call_target="tpu_custom_call" | custom-call | flops 1 | bytes 1 | tf_op jit(solution)/shard_map/column_unpack/pallas_call | solution.py:318
  279.1 1.4 collective-permute-done.19.refs_3_
  280.5 2.6 unpack_rows.3
  (77 shorter events, 5.8 us)
Async XLA Ops:
  6.2 9.6 %copy-start.6 = (bf16[32,32,768]{2,1,0:T(8,128)(2,1)S(1)}, bf16[32,32,768]{2,1,0:T(8,128)(2,1)}, u32[]{:S(2)}) copy-start(bf16[32,32,768]{2,1,0:T(8,128)(2,1)} %refs_0_.3) | copy-start | bytes 4718596
  6.2 98.0 %all-to-all-start = ((bf16[16,8,32,768]{3,2,1,0:T(8,128)(2,1)}), bf16[16,8,32,768]{3,2,1,0:T(8,128)(2,1)}, u32[]{:S(2)}, u32[]{:S(2)}) async-start(bf16[16,8,32,768]{3,2,1,0:T(8,128)(2,1)} %column_pack.1), calls=%async_computation | async-start | bytes 12582912 | tf_op jit(solution)/shard_map/all_to_all | solution.py:269
  15.8 5.9 %copy-start.4 = (bf16[32,32,768]{2,1,0:T(8,128)(2,1)S(1)}, bf16[32,32,768]{2,1,0:T(8,128)(2,1)}, u32[]{:S(2)}) copy-start(bf16[32,32,768]{2,1,0:T(8,128)(2,1)} %refs_0_.2) | copy-start | bytes 4718596
  18.8 71.3 %copy-start.3 = (bf16[3,2,32,2048]{3,2,1,0:T(8,128)(2,1)}, bf16[3,2,32,2048]{3,2,1,0:T(8,128)(2,1)S(1)}, u32[]{:S(2)}) copy-start(bf16[3,2,32,2048]{3,2,1,0:T(8,128)(2,1)S(1)} %get-tuple-element.61.refs_0_) | copy-start | bytes 2359300
  18.8 30.0 %copy-start.5 = (bf16[32,32,768]{2,1,0:T(8,128)(2,1)S(1)}, bf16[32,32,768]{2,1,0:T(8,128)(2,1)}, u32[]{:S(2)}) copy-start(bf16[32,32,768]{2,1,0:T(8,128)(2,1)} %refs_0_.4) | copy-start | bytes 4718596
  18.8 37.5 %collective-permute-start.4 = (bf16[3,2,32,2048]{3,2,1,0:T(8,128)(2,1)S(1)}, bf16[3,2,32,2048]{3,2,1,0:T(8,128)(2,1)}, u32[]{:S(2)}, u32[]{:S(2)}) collective-permute-start(bf16[3,2,32,2048]{3,2,1,0:T(8,128)(2,1)S(1)} %get-tuple-element.63), channel_id=1, source_target_pairs={{0,2},{1,3},{2,0},{3,1},{4,6},{5,7},{6,4},{7,5},{8,10},{9,11},{10,... | collective-permute-start | bytes 2359304 | tf_op jit(solution)/shard_map/ppermute | solution.py:265
  23.2 68.9 %copy-start = (bf16[3,1,32,2048]{3,2,1,0:T(8,128)(2,1)}, bf16[3,1,32,2048]{3,2,1,0:T(8,128)(2,1)S(1)}, u32[]{:S(2)}) copy-start(bf16[3,1,32,2048]{3,2,1,0:T(8,128)(2,1)S(1)} %get-tuple-element.78.refs_4_.refs_3_.refs_1_.refs_0_) | copy-start | bytes 1179652
  23.2 25.6 %collective-permute-start = (bf16[3,1,32,2048]{3,2,1,0:T(8,128)(2,1)S(1)}, bf16[3,1,32,2048]{3,2,1,0:T(8,128)(2,1)S(1)}, u32[]{:S(2)}, u32[]{:S(2)}) collective-permute-start(bf16[3,1,32,2048]{3,2,1,0:T(8,128)(2,1)S(1)} %get-tuple-element.56), channel_id=1, source_target_pairs={{0,1},{1,2},{2,3},{3,0},{4,5},{5,6},{6,7},{7,4},{8,9},{9,10},{10,1... | collective-permute-start | bytes 1179656 | tf_op jit(solution)/shard_map/ppermute | solution.py:265
  23.6 32.7 %collective-permute-start.1 = (bf16[3,1,32,2048]{3,2,1,0:T(8,128)(2,1)S(1)}, bf16[3,1,32,2048]{3,2,1,0:T(8,128)(2,1)S(1)}, u32[]{:S(2)}, u32[]{:S(2)}) collective-permute-start(bf16[3,1,32,2048]{3,2,1,0:T(8,128)(2,1)S(1)} %get-tuple-element.57), channel_id=1, source_target_pairs={{0,2},{1,3},{2,0},{3,1},{4,6},{5,7},{6,4},{7,5},{8,10},{9,11},{10,... | collective-permute-start | bytes 1179656 | tf_op jit(solution)/shard_map/ppermute | solution.py:265
  25.4 31.5 %collective-permute-start.2 = (bf16[3,1,32,2048]{3,2,1,0:T(8,128)(2,1)S(1)}, bf16[3,1,32,2048]{3,2,1,0:T(8,128)(2,1)S(1)}, u32[]{:S(2)}, u32[]{:S(2)}) collective-permute-start(bf16[3,1,32,2048]{3,2,1,0:T(8,128)(2,1)S(1)} %get-tuple-element.58), channel_id=1, source_target_pairs={{0,3},{1,0},{2,1},{3,2},{4,7},{5,4},{6,5},{7,6},{8,11},{9,8},{10,9... | collective-permute-start | bytes 1179656 | tf_op jit(solution)/shard_map/ppermute | solution.py:265
  26.1 64.4 %collective-permute-start.3 = (bf16[3,2,32,2048]{3,2,1,0:T(8,128)(2,1)S(1)}, bf16[3,2,32,2048]{3,2,1,0:T(8,128)(2,1)}, u32[]{:S(2)}, u32[]{:S(2)}) collective-permute-start(bf16[3,2,32,2048]{3,2,1,0:T(8,128)(2,1)S(1)} %get-tuple-element.62), channel_id=1, source_target_pairs={{0,1},{1,2},{2,3},{3,0},{4,5},{5,6},{6,7},{7,4},{8,9},{9,10},{10,1... | collective-permute-start | bytes 2359304 | tf_op jit(solution)/shard_map/ppermute | solution.py:265
  48.8 43.3 %copy-start.10 = (bf16[3,1,32,2048]{3,2,1,0:T(8,128)(2,1)}, bf16[3,1,32,2048]{3,2,1,0:T(8,128)(2,1)S(1)}, u32[]{:S(2)}) copy-start(bf16[3,1,32,2048]{3,2,1,0:T(8,128)(2,1)S(1)} %collective-permute-done.refs_5_.refs_4_.refs_2_.refs_1_) | copy-start | bytes 1179652
  48.8 42.8 %collective-permute-start.5 = (bf16[3,2,32,2048]{3,2,1,0:T(8,128)(2,1)S(1)}, bf16[3,2,32,2048]{3,2,1,0:T(8,128)(2,1)}, u32[]{:S(2)}, u32[]{:S(2)}) collective-permute-start(bf16[3,2,32,2048]{3,2,1,0:T(8,128)(2,1)S(1)} %get-tuple-element.64), channel_id=1, source_target_pairs={{0,3},{1,0},{2,1},{3,2},{4,7},{5,4},{6,5},{7,6},{8,11},{9,8},{10,9... | collective-permute-start | bytes 2359304 | tf_op jit(solution)/shard_map/ppermute | solution.py:265
  50.4 42.4 %copy-start.2 = (bf16[3,1,32,2048]{3,2,1,0:T(8,128)(2,1)}, bf16[3,1,32,2048]{3,2,1,0:T(8,128)(2,1)S(1)}, u32[]{:S(2)}) copy-start(bf16[3,1,32,2048]{3,2,1,0:T(8,128)(2,1)S(1)} %get-tuple-element.66.refs_8_.refs_7_.refs_5_) | copy-start | bytes 1179652
  56.3 36.5 %copy-start.11 = (bf16[3,1,32,2048]{3,2,1,0:T(8,128)(2,1)}, bf16[3,1,32,2048]{3,2,1,0:T(8,128)(2,1)S(1)}, u32[]{:S(2)}) copy-start(bf16[3,1,32,2048]{3,2,1,0:T(8,128)(2,1)S(1)} %collective-permute-done.1.refs_6_.refs_5_.refs_3_.refs_2_) | copy-start | bytes 1179652
  56.3 26.2 %collective-permute-start.10 = (bf16[3,1,32,2048]{3,2,1,0:T(8,128)(2,1)S(1)}, bf16[3,1,32,2048]{3,2,1,0:T(8,128)(2,1)S(1)}, u32[]{:S(2)}, u32[]{:S(2)}) collective-permute-start(bf16[3,1,32,2048]{3,2,1,0:T(8,128)(2,1)S(1)} %get-tuple-element.67), channel_id=1, source_target_pairs={{0,1},{1,2},{2,3},{3,0},{4,5},{5,6},{6,7},{7,4},{8,9},{9,10},{10,1... | collective-permute-start | bytes 1179656 | tf_op jit(solution)/shard_map/ppermute | solution.py:265
  56.3 46.8 %collective-permute-start.8 = (bf16[3,2,32,2048]{3,2,1,0:T(8,128)(2,1)}, bf16[3,2,32,2048]{3,2,1,0:T(8,128)(2,1)}, u32[]{:S(2)}, u32[]{:S(2)}) collective-permute-start(bf16[3,2,32,2048]{3,2,1,0:T(8,128)(2,1)} %collective-permute-done.4.refs_2_), channel_id=1, source_target_pairs={{0,4},{4,0},{1,5},{5,1},{2,6},{6,2},{3,7},{7,3},{8,12},{12,8},{9,1... | collective-permute-start | bytes 2359304 | tf_op jit(solution)/shard_map/ppermute | solution.py:265
  56.8 36.0 %copy-start.13 = (bf16[3,1,32,2048]{3,2,1,0:T(8,128)(2,1)}, bf16[3,1,32,2048]{3,2,1,0:T(8,128)(2,1)S(1)}, u32[]{:S(2)}) copy-start(bf16[3,1,32,2048]{3,2,1,0:T(8,128)(2,1)S(1)} %collective-permute-done.2.refs_7_.refs_6_.refs_4_.refs_3_) | copy-start | bytes 1179652
  56.8 33.3 %collective-permute-start.11 = (bf16[3,1,32,2048]{3,2,1,0:T(8,128)(2,1)S(1)}, bf16[3,1,32,2048]{3,2,1,0:T(8,128)(2,1)S(1)}, u32[]{:S(2)}, u32[]{:S(2)}) collective-permute-start(bf16[3,1,32,2048]{3,2,1,0:T(8,128)(2,1)S(1)} %get-tuple-element.68), channel_id=1, source_target_pairs={{0,2},{1,3},{2,0},{3,1},{4,6},{5,7},{6,4},{7,5},{8,10},{9,11},{10,... | collective-permute-start | bytes 1179656 | tf_op jit(solution)/shard_map/ppermute | solution.py:265
  82.5 10.3 %copy-start.15 = (bf16[3,1,32,2048]{3,2,1,0:T(8,128)(2,1)}, bf16[3,1,32,2048]{3,2,1,0:T(8,128)(2,1)S(1)}, u32[]{:S(2)}) copy-start(bf16[3,1,32,2048]{3,2,1,0:T(8,128)(2,1)S(1)} %collective-permute-done.10.refs_9_.refs_8_.refs_6_) | copy-start | bytes 1179652
  82.5 10.3 %collective-permute-start.12 = (bf16[3,1,32,2048]{3,2,1,0:T(8,128)(2,1)S(1)}, bf16[3,1,32,2048]{3,2,1,0:T(8,128)(2,1)S(1)}, u32[]{:S(2)}, u32[]{:S(2)}) collective-permute-start(bf16[3,1,32,2048]{3,2,1,0:T(8,128)(2,1)S(1)} %get-tuple-element.69), channel_id=1, source_target_pairs={{0,3},{1,0},{2,1},{3,2},{4,7},{5,4},{6,5},{7,6},{8,11},{9,8},{10,9... | collective-permute-start | bytes 1179656 | tf_op jit(solution)/shard_map/ppermute | solution.py:265
  90.1 2.7 copy-start.16
  90.1 45.7 %collective-permute-start.6 = (bf16[3,2,32,2048]{3,2,1,0:T(8,128)(2,1)S(1)}, bf16[3,2,32,2048]{3,2,1,0:T(8,128)(2,1)}, u32[]{:S(2)}, u32[]{:S(2)}) collective-permute-start(bf16[3,2,32,2048]{3,2,1,0:T(8,128)(2,1)S(1)} %get-tuple-element.61.refs_0_), channel_id=1, source_target_pairs={{0,4},{4,0},{1,5},{5,1},{2,6},{6,2},{3,7},{7,3},{8,12},{12,8},{9,1... | collective-permute-start | bytes 2359304 | tf_op jit(solution)/shard_map/ppermute | solution.py:265
  90.5 46.3 %collective-permute-start.7 = (bf16[3,2,32,2048]{3,2,1,0:T(8,128)(2,1)}, bf16[3,2,32,2048]{3,2,1,0:T(8,128)(2,1)}, u32[]{:S(2)}, u32[]{:S(2)}) collective-permute-start(bf16[3,2,32,2048]{3,2,1,0:T(8,128)(2,1)} %collective-permute-done.3.refs_1_), channel_id=1, source_target_pairs={{0,4},{4,0},{1,5},{5,1},{2,6},{6,2},{3,7},{7,3},{8,12},{12,8},{9,1... | collective-permute-start | bytes 2359304 | tf_op jit(solution)/shard_map/ppermute | solution.py:265
  91.6 62.1 %collective-permute-start.9 = (bf16[3,2,32,2048]{3,2,1,0:T(8,128)(2,1)}, bf16[3,2,32,2048]{3,2,1,0:T(8,128)(2,1)}, u32[]{:S(2)}, u32[]{:S(2)}) collective-permute-start(bf16[3,2,32,2048]{3,2,1,0:T(8,128)(2,1)} %collective-permute-done.5.refs_3_), channel_id=1, source_target_pairs={{0,4},{4,0},{1,5},{5,1},{2,6},{6,2},{3,7},{7,3},{8,12},{12,8},{9,1... | collective-permute-start | bytes 2359304 | tf_op jit(solution)/shard_map/ppermute | solution.py:265
  92.8 0.7 copy-start.17
  103.1 67.3 %collective-permute-start.13 = (bf16[6,1,32,2048]{3,2,1,0:T(8,128)(2,1)S(1)}, bf16[6,1,32,2048]{3,2,1,0:T(8,128)(2,1)S(1)}, u32[]{:S(2)}, u32[]{:S(2)}) collective-permute-start(bf16[6,1,32,2048]{3,2,1,0:T(8,128)(2,1)S(1)} %pad_maximum_fusion), channel_id=1, source_target_pairs={{0,4},{4,0},{1,5},{5,1},{2,6},{6,2},{3,7},{7,3},{8,12},{12,8},{9,1... | collective-permute-start | bytes 2359304 | tf_op jit(solution)/shard_map/ppermute | solution.py:265
  133.7 2.2 copy-start.1
  158.0 24.5 %copy-start.12 = (bf16[3,1,32,2048]{3,2,1,0:T(8,128)(2,1)S(1)}, bf16[3,1,32,2048]{3,2,1,0:T(8,128)(2,1)}, u32[]{:S(2)}) copy-start(bf16[3,1,32,2048]{3,2,1,0:T(8,128)(2,1)} %copy-done.11) | copy-start | bytes 1179652
  158.0 24.5 %copy-start.14 = (bf16[3,1,32,2048]{3,2,1,0:T(8,128)(2,1)S(1)}, bf16[3,1,32,2048]{3,2,1,0:T(8,128)(2,1)}, u32[]{:S(2)}) copy-start(bf16[3,1,32,2048]{3,2,1,0:T(8,128)(2,1)} %copy-done.13) | copy-start | bytes 1179652
  158.0 23.9 %all-to-all-start.1 = ((f32[16,2,3,2,8,128]{5,4,3,2,1,0:T(8,128)}), f32[16,2,3,2,8,128]{5,4,3,2,1,0:T(8,128)S(1)}, u32[]{:S(2)}, u32[]{:S(2)}) async-start(f32[16,2,3,2,8,128]{5,4,3,2,1,0:T(8,128)} %tied_terms.5), calls=%async_computation.1 | async-start | bytes 1572864 | tf_op jit(solution)/shard_map/all_to_all | solution.py:269
  170.5 16.2 %copy-start.18 = (bf16[6,1,32,2048]{3,2,1,0:T(8,128)(2,1)}, bf16[6,1,32,2048]{3,2,1,0:T(8,128)(2,1)S(1)}, u32[]{:S(2)}) copy-start(bf16[6,1,32,2048]{3,2,1,0:T(8,128)(2,1)S(1)} %collective-permute-done.13.refs_4_.refs_5_) | copy-start | bytes 2359300
  182.0 3.0 %collective-permute-start.14 = (f32[2,3,2,8,128]{4,3,2,1,0:T(8,128)S(1)}, f32[2,3,2,8,128]{4,3,2,1,0:T(8,128)S(1)}, u32[]{:S(2)}, u32[]{:S(2)}) collective-permute-start(f32[2,3,2,8,128]{4,3,2,1,0:T(8,128)S(1)} %reduce_sum.27), channel_id=1, source_target_pairs={{0,4},{4,0},{1,5},{5,1},{2,6},{6,2},{3,7},{7,3},{8,12},{12,8},{9,1... | collective-permute-start | bytes 147464 | tf_op jit(solution)/shard_map/ppermute | solution.py:265
  186.7 25.8 %collective-permute-start.16 = (bf16[6,1,32,2048]{3,2,1,0:T(8,128)(2,1)S(1)}, bf16[6,1,32,2048]{3,2,1,0:T(8,128)(2,1)}, u32[]{:S(2)}, u32[]{:S(2)}) collective-permute-start(bf16[6,1,32,2048]{3,2,1,0:T(8,128)(2,1)S(1)} %pad_maximum_fusion.1), channel_id=1, source_target_pairs={{0,4},{4,0},{1,5},{5,1},{2,6},{6,2},{3,7},{7,3},{8,12},{12,8},{9,1... | collective-permute-start | bytes 2359304 | tf_op jit(solution)/shard_map/ppermute | solution.py:265
  212.5 61.9 %all-to-all-start.3 = ((bf16[16,6,32,768]{3,2,1,0:T(8,128)(2,1)}), bf16[16,6,32,768]{3,2,1,0:T(8,128)(2,1)}, u32[]{:S(2)}, u32[]{:S(2)}) async-start(bf16[16,6,32,768]{3,2,1,0:T(8,128)(2,1)} %copy-done.1), calls=%async_computation.3 | async-start | bytes 9437184 | tf_op jit(solution)/shard_map/all_to_all | solution.py:269
  223.2 18.9 %collective-permute-start.15 = (bf16[3,1,32,2048]{3,2,1,0:T(8,128)(2,1)}, bf16[3,1,32,2048]{3,2,1,0:T(8,128)(2,1)S(1)}, u32[]{:S(2)}, u32[]{:S(2)}) collective-permute-start(bf16[3,1,32,2048]{3,2,1,0:T(8,128)(2,1)} %get-tuple-element.77), channel_id=1, source_target_pairs={{0,3},{1,0},{2,1},{3,2},{4,7},{5,4},{6,5},{7,6},{8,11},{9,8},{10,9... | collective-permute-start | bytes 1179656 | tf_op jit(solution)/shard_map/ppermute | solution.py:265
  225.7 20.8 %collective-permute-start.23 = (bf16[3,1,32,2048]{3,2,1,0:T(8,128)(2,1)}, bf16[3,1,32,2048]{3,2,1,0:T(8,128)(2,1)S(1)}, u32[]{:S(2)}, u32[]{:S(2)}) collective-permute-start(bf16[3,1,32,2048]{3,2,1,0:T(8,128)(2,1)} %get-tuple-element.100), channel_id=1, source_target_pairs={{0,2},{1,3},{2,0},{3,1},{4,6},{5,7},{6,4},{7,5},{8,10},{9,11},{10,... | collective-permute-start | bytes 1179656 | tf_op jit(solution)/shard_map/ppermute | solution.py:265
  226.2 24.3 %collective-permute-start.24 = (bf16[3,1,32,2048]{3,2,1,0:T(8,128)(2,1)}, bf16[3,1,32,2048]{3,2,1,0:T(8,128)(2,1)S(1)}, u32[]{:S(2)}, u32[]{:S(2)}) collective-permute-start(bf16[3,1,32,2048]{3,2,1,0:T(8,128)(2,1)} %get-tuple-element.101), channel_id=1, source_target_pairs={{0,1},{1,2},{2,3},{3,0},{4,5},{5,6},{6,7},{7,4},{8,9},{9,10},{10,1... | collective-permute-start | bytes 1179656 | tf_op jit(solution)/shard_map/ppermute | solution.py:265
  226.9 32.0 %collective-permute-start.20 = (bf16[3,1,32,2048]{3,2,1,0:T(8,128)(2,1)}, bf16[3,1,32,2048]{3,2,1,0:T(8,128)(2,1)S(1)}, u32[]{:S(2)}, u32[]{:S(2)}) collective-permute-start(bf16[3,1,32,2048]{3,2,1,0:T(8,128)(2,1)} %get-tuple-element.96), channel_id=1, source_target_pairs={{0,3},{1,0},{2,1},{3,2},{4,7},{5,4},{6,5},{7,6},{8,11},{9,8},{10,9... | collective-permute-start | bytes 1179656 | tf_op jit(solution)/shard_map/ppermute | solution.py:265
  228.9 32.5 %collective-permute-start.21 = (bf16[3,1,32,2048]{3,2,1,0:T(8,128)(2,1)}, bf16[3,1,32,2048]{3,2,1,0:T(8,128)(2,1)S(1)}, u32[]{:S(2)}, u32[]{:S(2)}) collective-permute-start(bf16[3,1,32,2048]{3,2,1,0:T(8,128)(2,1)} %get-tuple-element.97), channel_id=1, source_target_pairs={{0,2},{1,3},{2,0},{3,1},{4,6},{5,7},{6,4},{7,5},{8,10},{9,11},{10,... | collective-permute-start | bytes 1179656 | tf_op jit(solution)/shard_map/ppermute | solution.py:265
  242.0 16.8 %copy-start.8 = (bf16[3,1,32,2048]{3,2,1,0:T(8,128)(2,1)S(1)}, bf16[3,1,32,2048]{3,2,1,0:T(8,128)(2,1)}, u32[]{:S(2)}) copy-start(bf16[3,1,32,2048]{3,2,1,0:T(8,128)(2,1)} %get-tuple-element.99.refs_0_) | copy-start | bytes 1179652
  242.0 22.4 %collective-permute-start.22 = (bf16[3,1,32,2048]{3,2,1,0:T(8,128)(2,1)}, bf16[3,1,32,2048]{3,2,1,0:T(8,128)(2,1)S(1)}, u32[]{:S(2)}, u32[]{:S(2)}) collective-permute-start(bf16[3,1,32,2048]{3,2,1,0:T(8,128)(2,1)} %get-tuple-element.98), channel_id=1, source_target_pairs={{0,1},{1,2},{2,3},{3,0},{4,5},{5,6},{6,7},{7,4},{8,9},{9,10},{10,1... | collective-permute-start | bytes 1179656 | tf_op jit(solution)/shard_map/ppermute | solution.py:265
  246.5 32.5 %collective-permute-start.17 = (bf16[3,1,32,2048]{3,2,1,0:T(8,128)(2,1)}, bf16[3,1,32,2048]{3,2,1,0:T(8,128)(2,1)S(1)}, u32[]{:S(2)}, u32[]{:S(2)}) collective-permute-start(bf16[3,1,32,2048]{3,2,1,0:T(8,128)(2,1)} %get-tuple-element.84), channel_id=1, source_target_pairs={{0,3},{1,0},{2,1},{3,2},{4,7},{5,4},{6,5},{7,6},{8,11},{9,8},{10,9... | collective-permute-start | bytes 1179656 | tf_op jit(solution)/shard_map/ppermute | solution.py:265
  250.5 28.5 %collective-permute-start.18 = (bf16[3,1,32,2048]{3,2,1,0:T(8,128)(2,1)}, bf16[3,1,32,2048]{3,2,1,0:T(8,128)(2,1)S(1)}, u32[]{:S(2)}, u32[]{:S(2)}) collective-permute-start(bf16[3,1,32,2048]{3,2,1,0:T(8,128)(2,1)} %get-tuple-element.85), channel_id=1, source_target_pairs={{0,2},{1,3},{2,0},{3,1},{4,6},{5,7},{6,4},{7,5},{8,10},{9,11},{10,... | collective-permute-start | bytes 1179656 | tf_op jit(solution)/shard_map/ppermute | solution.py:265
  258.9 21.6 %collective-permute-start.19 = (bf16[3,1,32,2048]{3,2,1,0:T(8,128)(2,1)}, bf16[3,1,32,2048]{3,2,1,0:T(8,128)(2,1)S(1)}, u32[]{:S(2)}, u32[]{:S(2)}) collective-permute-start(bf16[3,1,32,2048]{3,2,1,0:T(8,128)(2,1)} %get-tuple-element.86), channel_id=1, source_target_pairs={{0,1},{1,2},{2,3},{3,0},{4,5},{5,6},{6,7},{7,4},{8,9},{9,10},{10,1... | collective-permute-start | bytes 1179656 | tf_op jit(solution)/shard_map/ppermute | solution.py:265
  258.9 5.6 %copy-start.7 = (bf16[3,1,32,2048]{3,2,1,0:T(8,128)(2,1)S(1)}, bf16[3,1,32,2048]{3,2,1,0:T(8,128)(2,1)}, u32[]{:S(2)}) copy-start(bf16[3,1,32,2048]{3,2,1,0:T(8,128)(2,1)} %get-tuple-element.95.refs_0_) | copy-start | bytes 1179652
  267.1 13.5 %copy-start.9 = (bf16[3,1,32,2048]{3,2,1,0:T(8,128)(2,1)S(1)}, bf16[3,1,32,2048]{3,2,1,0:T(8,128)(2,1)}, u32[]{:S(2)}) copy-start(bf16[3,1,32,2048]{3,2,1,0:T(8,128)(2,1)} %get-tuple-element.91.refs_0_) | copy-start | bytes 1179652

commit v6 on v5

--- a/solution.py
+++ b/solution.py
@@ -205,7 +205,7 @@
         ),
         out_shape=jax.ShapeDtypeStruct((slices, 2, heads, 2, step, wide), jnp.float32),
         input_output_aliases={count + 2 * parts: 0} if held else {},
-        compiler_params=params(VMEM_ALL),
+        compiler_params=params(),
         cost_estimate=COST,
         name="tied_terms",
     )(*left, *keys, *values, *held)

time: 284 us -> 284 us (level)
  transfers between devices with their start and end apart: 28 -> 28, of which waited for: 16 -> 15; matrix products, arithmetic and copies ran while one was open for 0% -> 1% of each run, Pallas kernels for 24% -> 24%
where the time goes in v6:
time: 284 us; the launch traced here: 283 us
  waiting for transfers between devices  128 us (45%)
  Pallas kernels  74.7 us (26%)
  starting transfers between devices  48.7 us (17%)
  blocking collectives  24.3 us (9%)
  local copies, waits for them, and re-layouts  4.09 us (1%)
    ppermute x25, waiting for transfers between devices, shift(): return lax.ppermute(x, axis, [(i, (i + by) % n) for i in range(n)])  109 us
    pallas_call x1, Pallas kernels, column_backward(): pl.pallas_call(functools.partial(column_kernel, chunk=chunk), grid=(piece...  29.5 us
    ppermute x25, starting transfers between devices, shift(): return lax.ppermute(x, axis, [(i, (i + by) % n) for i in range(n)])  26 us
    all_to_all x1, blocking collectives, over_rows(): return lax.all_to_all(x, ROWS, split_axis=0, concat_axis=0, tiled=True)  24.3 us
    all_to_all x3, starting transfers between devices, over_rows(): return lax.all_to_all(x, ROWS, split_axis=0, concat_axis=0, tiled=True)  22.6 us
    all_to_all x3, waiting for transfers between devices, over_rows(): return lax.all_to_all(x, ROWS, split_axis=0, concat_axis=0, tiled=True)  18.8 us
    pallas_call x3, Pallas kernels, tied_terms(): pl.pallas_call(functools.partial(terms_kernel, count=count, parts=parts),...  11.3 us
    pallas_call x2, Pallas kernels, tied_grads(): pl.pallas_call(functools.partial(kernel, parts=parts, factor=factor), gri...  9.99 us
  transfers between devices with their start and end apart: 28, of which 15 were waited for; matrix products, arithmetic and copies ran while one was open for 1% of the time, Pallas kernels for 24%

profile of v6, /device:TPU:1, one launch (start us, length us, event | category | flops | bytes accessed | tf_op | source)
XLA Modules:
  0.0 283.2 jit_solution(2701336934391982353)
XLA Ops:
  0.6 5.6 %column_pack.1 = bf16[16,8,32,768]{3,2,1,0:T(8,128)(2,1)} custom-call(bf16[32,32,768]{2,1,0:T(8,128)(2,1)} %refs_0_.1, bf16[32,32,768]{2,1,0:T(8,128)(2,1)} %refs_1_.1, bf16[32,32,768]{2,1,0:T(8,128)(2,1)} %refs_2_.1, bf16[32,32,768]{2,1,0:T(8,128)(2,1)} %refs_3_.1), custom_call_target="tpu_custom_call" | custom-call | flops 1 | bytes 1 | tf_op jit(solution)/shard_map/column_pack/pallas_call | solution.py:296
  6.2 9.6 %all-to-all-start = ((bf16[16,8,32,768]{3,2,1,0:T(8,128)(2,1)}), bf16[16,8,32,768]{3,2,1,0:T(8,128)(2,1)}, u32[]{:S(2)}, u32[]{:S(2)}) async-start(bf16[16,8,32,768]{3,2,1,0:T(8,128)(2,1)} %column_pack.1), calls=%async_computation | async-start | bytes 12582912 | tf_op jit(solution)/shard_map/all_to_all | solution.py:269
  15.8 2.9 %pack_rows.4 = (bf16[3,2,32,2048]{3,2,1,0:T(8,128)(2,1)}, bf16[3,2,32,2048]{3,2,1,0:T(8,128)(2,1)S(1)}, bf16[3,2,32,2048]{3,2,1,0:T(8,128)(2,1)S(1)}, bf16[3,2,32,2048]{3,2,1,0:T(8,128)(2,1)S(1)}) custom-call(s32[1]{0:T(128)} %bitcast.here_ref, bf16[32,32,768]{2,1,0:T(8,128)(2,1)S(1)} %copy-done.7, bf16[32,32,768]{2,1,0:T(8,128)(2,1)} %refs_1_.2), custom_call_target="tpu_custom_call" | custom-call | flops 1 | bytes 1 | tf_op jit(solution)/shard_map/pack_rows/pallas_call | solution.py:121
  18.7 3.3 %collective-permute-start.4 = (bf16[3,2,32,2048]{3,2,1,0:T(8,128)(2,1)S(1)}, bf16[3,2,32,2048]{3,2,1,0:T(8,128)(2,1)S(1)}, u32[]{:S(2)}, u32[]{:S(2)}) collective-permute-start(bf16[3,2,32,2048]{3,2,1,0:T(8,128)(2,1)S(1)} %get-tuple-element.63), channel_id=1, source_target_pairs={{0,2},{1,3},{2,0},{3,1},{4,6},{5,7},{6,4},{7,5},{8,10},{9,11},{10,... | collective-permute-start | bytes 2359304 | tf_op jit(solution)/shard_map/ppermute | solution.py:265
  22.1 1.6 pack_rows.3
  24.4 1.0 collective-permute-start.1
  25.4 1.4 collective-permute-start.2
  27.0 21.7 %collective-permute-done.refs_5_.refs_4_.refs_2_.refs_1_ = bf16[3,1,32,2048]{3,2,1,0:T(8,128)(2,1)S(1)} collective-permute-done((bf16[3,1,32,2048]{3,2,1,0:T(8,128)(2,1)S(1)}, bf16[3,1,32,2048]{3,2,1,0:T(8,128)(2,1)S(1)}, u32[]{:S(2)}, u32[]{:S(2)}) %collective-permute-start) | collective-permute-done | bytes 393248 | tf_op jit(solution)/shard_map/ppermute | solution.py:265
  48.8 1.6 pack_rows.5
  50.4 6.6 %collective-permute-done.1.refs_6_.refs_5_.refs_3_.refs_2_ = bf16[3,1,32,2048]{3,2,1,0:T(8,128)(2,1)S(1)} collective-permute-done((bf16[3,1,32,2048]{3,2,1,0:T(8,128)(2,1)S(1)}, bf16[3,1,32,2048]{3,2,1,0:T(8,128)(2,1)S(1)}, u32[]{:S(2)}, u32[]{:S(2)}) %collective-permute-start.1) | collective-permute-done | bytes 393248 | tf_op jit(solution)/shard_map/ppermute | solution.py:265
  57.4 2.6 collective-permute-start.11
  60.1 22.3 %collective-permute-done.10.refs_9_.refs_8_.refs_6_ = bf16[3,1,32,2048]{3,2,1,0:T(8,128)(2,1)S(1)} collective-permute-done((bf16[3,1,32,2048]{3,2,1,0:T(8,128)(2,1)S(1)}, bf16[3,1,32,2048]{3,2,1,0:T(8,128)(2,1)S(1)}, u32[]{:S(2)}, u32[]{:S(2)}) %collective-permute-start.10) | collective-permute-done | bytes 393248 | tf_op jit(solution)/shard_map/ppermute | solution.py:265
  82.5 8.0 %collective-permute-done.11.refs_10_.refs_9_.refs_7_ = bf16[3,1,32,2048]{3,2,1,0:T(8,128)(2,1)S(1)} collective-permute-done((bf16[3,1,32,2048]{3,2,1,0:T(8,128)(2,1)S(1)}, bf16[3,1,32,2048]{3,2,1,0:T(8,128)(2,1)S(1)}, u32[]{:S(2)}, u32[]{:S(2)}) %collective-permute-start.11) | collective-permute-done | bytes 393248 | tf_op jit(solution)/shard_map/ppermute | solution.py:265
  90.9 1.1 collective-permute-start.7
  92.4 0.9 pad_maximum_fusion
  93.4 4.0 %tied_terms.3.refs_11_ = f32[16,2,3,2,8,128]{5,4,3,2,1,0:T(8,128)} custom-call(bf16[3,2,32,2048]{3,2,1,0:T(8,128)(2,1)} %get-tuple-element.61.refs_0_, bf16[3,2,32,2048]{3,2,1,0:T(8,128)(2,1)} %collective-permute-done.3.refs_1_, bf16[3,2,32,2048]{3,2,1,0:T(8,128)(2,1)} %copy-done.11, bf16[3,2,32,2048]{3,2,1,0:T(8,128)(2,1)} %collective-permute-done.5.refs_3_, ...), custom_call_target="tpu_custom_call" | custom-call | flops 1 | bytes 1 | tf_op jit(solution)/shard_map/tied_terms/pallas_call | solution.py:197
  97.3 5.7 %collective-permute-done.8.refs_2_.refs_6_ = bf16[3,2,32,2048]{3,2,1,0:T(8,128)(2,1)S(1)} collective-permute-done((bf16[3,2,32,2048]{3,2,1,0:T(8,128)(2,1)S(1)}, bf16[3,2,32,2048]{3,2,1,0:T(8,128)(2,1)S(1)}, u32[]{:S(2)}, u32[]{:S(2)}) %collective-permute-start.8) | collective-permute-done | bytes 786464 | tf_op jit(solution)/shard_map/ppermute | solution.py:265
  103.1 0.9 copy-done.12
  103.9 1.1 collective-permute-start.13
  105.0 29.5 %column_attention.1 = bf16[16,6,32,768]{3,2,1,0:T(8,128)(2,1)S(1)} custom-call(bf16[16,8,32,768]{3,2,1,0:T(8,128)(2,1)} %all-to-all-done.x_ref), custom_call_target="tpu_custom_call" | custom-call | flops 8053063680 | bytes 11010048 | tf_op jit(solution)/shard_map/column_attention/pallas_call | solution.py:80
  134.5 2.1 copy-done.4
  136.9 3.9 %tied_terms.4.refs_9_ = f32[16,2,3,2,8,128]{5,4,3,2,1,0:T(8,128)} custom-call(bf16[3,2,32,2048]{3,2,1,0:T(8,128)(2,1)} %collective-permute-done.6.refs_0_.refs_4_, bf16[3,2,32,2048]{3,2,1,0:T(8,128)(2,1)} %collective-permute-done.7.refs_1_.refs_5_, bf16[3,2,32,2048]{3,2,1,0:T(8,128)(2,1)} %copy-done.12, ...), custom_call_target="tpu_custom_call", output_to_operand_aliasing={{}: (11, {})} | custom-call | flops 1 | bytes 1 | tf_op jit(solution)/shard_map/tied_terms/pallas_call | solution.py:197
  140.7 13.0 %collective-permute-done.9.refs_0_.refs_7_ = bf16[3,2,32,2048]{3,2,1,0:T(8,128)(2,1)} collective-permute-done((bf16[3,2,32,2048]{3,2,1,0:T(8,128)(2,1)}, bf16[3,2,32,2048]{3,2,1,0:T(8,128)(2,1)}, u32[]{:S(2)}, u32[]{:S(2)}) %collective-permute-start.9) | collective-permute-done | bytes 786464 | tf_op jit(solution)/shard_map/ppermute | solution.py:265
  153.7 3.5 %tied_terms.5 = f32[16,2,3,2,8,128]{5,4,3,2,1,0:T(8,128)} custom-call(bf16[3,2,32,2048]{3,2,1,0:T(8,128)(2,1)} %collective-permute-done.9.refs_0_.refs_7_, bf16[3,1,32,2048]{3,2,1,0:T(8,128)(2,1)S(1)} %get-tuple-element.78.refs_4_.refs_3_.refs_1_.refs_0_, ...), custom_call_target="tpu_custom_call", output_to_operand_aliasing={{}: (9, {})} | custom-call | flops 1 | bytes 1 | tf_op jit(solution)/shard_map/tied_terms/pallas_call | solution.py:197
  157.2 7.9 %all-to-all-start.1 = ((f32[16,2,3,2,8,128]{5,4,3,2,1,0:T(8,128)}), f32[16,2,3,2,8,128]{5,4,3,2,1,0:T(8,128)S(1)}, u32[]{:S(2)}, u32[]{:S(2)}) async-start(f32[16,2,3,2,8,128]{5,4,3,2,1,0:T(8,128)} %tied_terms.5), calls=%async_computation.1 | async-start | bytes 1572864 | tf_op jit(solution)/shard_map/all_to_all | solution.py:269
  165.1 5.5 %collective-permute-done.13.refs_4_.refs_5_ = bf16[6,1,32,2048]{3,2,1,0:T(8,128)(2,1)} collective-permute-done((bf16[6,1,32,2048]{3,2,1,0:T(8,128)(2,1)}, bf16[6,1,32,2048]{3,2,1,0:T(8,128)(2,1)}, u32[]{:S(2)}, u32[]{:S(2)}) %collective-permute-start.13) | collective-permute-done | bytes 786464 | tf_op jit(solution)/shard_map/ppermute | solution.py:265
  170.6 11.4 %all-to-all-done.1 = f32[16,2,3,2,8,128]{5,4,3,2,1,0:T(8,128)S(1)} async-done(((f32[16,2,3,2,8,128]{5,4,3,2,1,0:T(8,128)}), f32[16,2,3,2,8,128]{5,4,3,2,1,0:T(8,128)S(1)}, u32[]{:S(2)}, u32[]{:S(2)}) %all-to-all-start.1) | async-done | bytes 786464 | tf_op jit(solution)/shard_map/all_to_all | solution.py:269
  182.6 2.5 collective-permute-done.14
  185.1 1.4 fusion.26
  187.3 24.3 %all_to_all.20 = bf16[16,5,3,8,128]{4,3,2,1,0:T(8,128)(2,1)S(1)} all-to-all(bf16[16,5,3,8,128]{4,3,2,1,0:T(8,128)(2,1)S(1)} %broadcast_in_dim.2), channel_id=1, replica_groups=mesh['z'=4,'yh'=2,'core'=2,'yl'=2,'x'=4] {'z','yh','core'}, dimensions={0} | all-to-all | bytes 983040 | tf_op jit(solution)/shard_map/all_to_all | solution.py:269
  211.6 0.9 copy_bitcast_fusion.refs_8_
  212.5 5.1 %all-to-all-start.3 = ((bf16[16,6,32,768]{3,2,1,0:T(8,128)(2,1)}), bf16[16,6,32,768]{3,2,1,0:T(8,128)(2,1)}, u32[]{:S(2)}, u32[]{:S(2)}) async-start(bf16[16,6,32,768]{3,2,1,0:T(8,128)(2,1)} %copy-done.4), calls=%async_computation.3 | async-start | bytes 9437184 | tf_op jit(solution)/shard_map/all_to_all | solution.py:269
  217.6 5.5 %pair_grads.1 = (bf16[3,1,32,2048]{3,2,1,0:T(8,128)(2,1)}, bf16[3,1,32,2048]{3,2,1,0:T(8,128)(2,1)}, bf16[3,1,32,2048]{3,2,1,0:T(8,128)(2,1)}, bf16[3,1,32,2048]...) custom-call(bf16[3,2,32,2048]{3,2,1,0:T(8,128)(2,1)} %get-tuple-elem, ...), custom_call_target="tpu_custom_call" | custom-call | flops 1 | bytes 1 | tf_op jit(solution)/shard_map/pair_grads/pallas_call | solution.py:251
  223.1 2.5 collective-permute-start.15
  226.8 2.1 collective-permute-start.20
  228.9 1.2 collective-permute-start.21
  230.1 11.9 %collective-permute-done.15.refs_1_ = bf16[3,1,32,2048]{3,2,1,0:T(8,128)(2,1)S(1)} collective-permute-done((bf16[3,1,32,2048]{3,2,1,0:T(8,128)(2,1)}, bf16[3,1,32,2048]{3,2,1,0:T(8,128)(2,1)S(1)}, u32[]{:S(2)}, u32[]{:S(2)}) %collective-permute-start.15) | collective-permute-done | bytes 393248 | tf_op jit(solution)/shard_map/ppermute | solution.py:265
  242.0 4.5 %query_grads.1 = (bf16[3,1,32,2048]{3,2,1,0:T(8,128)(2,1)}, bf16[3,1,32,2048]{3,2,1,0:T(8,128)(2,1)}, bf16[3,1,32,2048]{3,2,1,0:T(8,128)(2,1)}, bf16[3,1,32,2048]{3,2,1,0:T(8,128)(2,1)}) custom-call(bf16[3,1,32,2048]{3,2,1,0:T(8,128)(2,1)} %copy-done, bf16[3,1,32,2048]{3,2,1,0:T(8,128)(2,1)} %copy-done.1, bf16[3,1,32,2048]{3,2,1,0:T(8,128)(2,1)} %copy-done.2, ...), custom_call_target="tpu_custom_call" | custom-call | flops 1 | bytes 1 | tf_op jit(solution)/shard_map/query_grads/pallas_call | solution.py:251
  246.5 4.0 %collective-permute-start.17 = (bf16[3,1,32,2048]{3,2,1,0:T(8,128)(2,1)}, bf16[3,1,32,2048]{3,2,1,0:T(8,128)(2,1)S(1)}, u32[]{:S(2)}, u32[]{:S(2)}) collective-permute-start(bf16[3,1,32,2048]{3,2,1,0:T(8,128)(2,1)} %get-tuple-element.84), channel_id=1, source_target_pairs={{0,3},{1,0},{2,1},{3,2},{4,7},{5,4},{6,5},{7,6},{8,11},{9,8},{10,9... | collective-permute-start | bytes 1179656 | tf_op jit(solution)/shard_map/ppermute | solution.py:265
  250.5 1.2 collective-permute-start.18
  251.7 7.1 %collective-permute-done.20.refs_1_ = bf16[3,1,32,2048]{3,2,1,0:T(8,128)(2,1)S(1)} collective-permute-done((bf16[3,1,32,2048]{3,2,1,0:T(8,128)(2,1)}, bf16[3,1,32,2048]{3,2,1,0:T(8,128)(2,1)S(1)}, u32[]{:S(2)}, u32[]{:S(2)}) %collective-permute-start.20) | collective-permute-done | bytes 393248 | tf_op jit(solution)/shard_map/ppermute | solution.py:265
  258.8 2.6 unpack_rows.5
  261.4 3.0 %collective-permute-done.22.refs_3_ = bf16[3,1,32,2048]{3,2,1,0:T(8,128)(2,1)S(1)} collective-permute-done((bf16[3,1,32,2048]{3,2,1,0:T(8,128)(2,1)}, bf16[3,1,32,2048]{3,2,1,0:T(8,128)(2,1)S(1)}, u32[]{:S(2)}, u32[]{:S(2)}) %collective-permute-start.22) | collective-permute-done | bytes 393248 | tf_op jit(solution)/shard_map/ppermute | solution.py:265
  264.4 2.6 unpack_rows.4
  267.0 7.4 %all-to-all-done.3.x_ref = bf16[16,6,32,768]{3,2,1,0:T(8,128)(2,1)} async-done(((bf16[16,6,32,768]{3,2,1,0:T(8,128)(2,1)}), bf16[16,6,32,768]{3,2,1,0:T(8,128)(2,1)}, u32[]{:S(2)}, u32[]{:S(2)}) %all-to-all-start.3) | async-done | bytes 4718624 | tf_op jit(solution)/shard_map/all_to_all | solution.py:269
  274.4 4.7 %column_unpack.1 = (bf16[32,32,768]{2,1,0:T(8,128)(2,1)}, bf16[32,32,768]{2,1,0:T(8,128)(2,1)}, bf16[32,32,768]{2,1,0:T(8,128)(2,1)}) custom-call(bf16[16,6,32,768]{3,2,1,0:T(8,128)(2,1)} %all-to-all-done.3.x_ref), custom_call_target="tpu_custom_call" | custom-call | flops 1 | bytes 1 | tf_op jit(solution)/shard_map/column_unpack/pallas_call | solution.py:318
  279.1 1.4 collective-permute-done.19.refs_3_
  280.4 2.6 unpack_rows.3
  (65 shorter events, 5.2 us)
Async XLA Ops:
  6.2 9.6 %copy-start.7 = (bf16[32,32,768]{2,1,0:T(8,128)(2,1)S(1)}, bf16[32,32,768]{2,1,0:T(8,128)(2,1)}, u32[]{:S(2)}) copy-start(bf16[32,32,768]{2,1,0:T(8,128)(2,1)} %refs_0_.3) | copy-start | bytes 4718596
  6.2 98.8 %all-to-all-start = ((bf16[16,8,32,768]{3,2,1,0:T(8,128)(2,1)}), bf16[16,8,32,768]{3,2,1,0:T(8,128)(2,1)}, u32[]{:S(2)}, u32[]{:S(2)}) async-start(bf16[16,8,32,768]{3,2,1,0:T(8,128)(2,1)} %column_pack.1), calls=%async_computation | async-start | bytes 12582912 | tf_op jit(solution)/shard_map/all_to_all | solution.py:269
  15.8 6.3 %copy-start.5 = (bf16[32,32,768]{2,1,0:T(8,128)(2,1)S(1)}, bf16[32,32,768]{2,1,0:T(8,128)(2,1)}, u32[]{:S(2)}) copy-start(bf16[32,32,768]{2,1,0:T(8,128)(2,1)} %refs_0_.2) | copy-start | bytes 4718596
  18.7 30.0 %copy-start.6 = (bf16[32,32,768]{2,1,0:T(8,128)(2,1)S(1)}, bf16[32,32,768]{2,1,0:T(8,128)(2,1)}, u32[]{:S(2)}) copy-start(bf16[32,32,768]{2,1,0:T(8,128)(2,1)} %refs_0_.4) | copy-start | bytes 4718596
  18.7 38.2 %collective-permute-start.4 = (bf16[3,2,32,2048]{3,2,1,0:T(8,128)(2,1)S(1)}, bf16[3,2,32,2048]{3,2,1,0:T(8,128)(2,1)S(1)}, u32[]{:S(2)}, u32[]{:S(2)}) collective-permute-start(bf16[3,2,32,2048]{3,2,1,0:T(8,128)(2,1)S(1)} %get-tuple-element.63), channel_id=1, source_target_pairs={{0,2},{1,3},{2,0},{3,1},{4,6},{5,7},{6,4},{7,5},{8,10},{9,11},{10,... | collective-permute-start | bytes 2359304 | tf_op jit(solution)/shard_map/ppermute | solution.py:265
  23.6 130.1 %copy-start = (bf16[3,1,32,2048]{3,2,1,0:T(8,128)(2,1)}, bf16[3,1,32,2048]{3,2,1,0:T(8,128)(2,1)S(1)}, u32[]{:S(2)}) copy-start(bf16[3,1,32,2048]{3,2,1,0:T(8,128)(2,1)S(1)} %get-tuple-element.78.refs_4_.refs_3_.refs_1_.refs_0_) | copy-start | bytes 1179652
  23.7 25.1 %collective-permute-start = (bf16[3,1,32,2048]{3,2,1,0:T(8,128)(2,1)S(1)}, bf16[3,1,32,2048]{3,2,1,0:T(8,128)(2,1)S(1)}, u32[]{:S(2)}, u32[]{:S(2)}) collective-permute-start(bf16[3,1,32,2048]{3,2,1,0:T(8,128)(2,1)S(1)} %get-tuple-element.56), channel_id=1, source_target_pairs={{0,1},{1,2},{2,3},{3,0},{4,5},{5,6},{6,7},{7,4},{8,9},{9,10},{10,1... | collective-permute-start | bytes 1179656 | tf_op jit(solution)/shard_map/ppermute | solution.py:265
  24.4 32.6 %collective-permute-start.1 = (bf16[3,1,32,2048]{3,2,1,0:T(8,128)(2,1)S(1)}, bf16[3,1,32,2048]{3,2,1,0:T(8,128)(2,1)S(1)}, u32[]{:S(2)}, u32[]{:S(2)}) collective-permute-start(bf16[3,1,32,2048]{3,2,1,0:T(8,128)(2,1)S(1)} %get-tuple-element.57), channel_id=1, source_target_pairs={{0,2},{1,3},{2,0},{3,1},{4,6},{5,7},{6,4},{7,5},{8,10},{9,11},{10,... | collective-permute-start | bytes 1179656 | tf_op jit(solution)/shard_map/ppermute | solution.py:265
  25.4 32.0 %collective-permute-start.2 = (bf16[3,1,32,2048]{3,2,1,0:T(8,128)(2,1)S(1)}, bf16[3,1,32,2048]{3,2,1,0:T(8,128)(2,1)S(1)}, u32[]{:S(2)}, u32[]{:S(2)}) collective-permute-start(bf16[3,1,32,2048]{3,2,1,0:T(8,128)(2,1)S(1)} %get-tuple-element.58), channel_id=1, source_target_pairs={{0,3},{1,0},{2,1},{3,2},{4,7},{5,4},{6,5},{7,6},{8,11},{9,8},{10,9... | collective-permute-start | bytes 1179656 | tf_op jit(solution)/shard_map/ppermute | solution.py:265
  26.9 64.1 %collective-permute-start.3 = (bf16[3,2,32,2048]{3,2,1,0:T(8,128)(2,1)S(1)}, bf16[3,2,32,2048]{3,2,1,0:T(8,128)(2,1)}, u32[]{:S(2)}, u32[]{:S(2)}) collective-permute-start(bf16[3,2,32,2048]{3,2,1,0:T(8,128)(2,1)S(1)} %get-tuple-element.62), channel_id=1, source_target_pairs={{0,1},{1,2},{2,3},{3,0},{4,5},{5,6},{6,7},{7,4},{8,9},{9,10},{10,1... | collective-permute-start | bytes 2359304 | tf_op jit(solution)/shard_map/ppermute | solution.py:265
  48.7 105.0 %copy-start.1 = (bf16[3,1,32,2048]{3,2,1,0:T(8,128)(2,1)}, bf16[3,1,32,2048]{3,2,1,0:T(8,128)(2,1)S(1)}, u32[]{:S(2)}) copy-start(bf16[3,1,32,2048]{3,2,1,0:T(8,128)(2,1)S(1)} %collective-permute-done.refs_5_.refs_4_.refs_2_.refs_1_) | copy-start | bytes 1179652
  48.7 43.3 %collective-permute-start.5 = (bf16[3,2,32,2048]{3,2,1,0:T(8,128)(2,1)S(1)}, bf16[3,2,32,2048]{3,2,1,0:T(8,128)(2,1)}, u32[]{:S(2)}, u32[]{:S(2)}) collective-permute-start(bf16[3,2,32,2048]{3,2,1,0:T(8,128)(2,1)S(1)} %get-tuple-element.64), channel_id=1, source_target_pairs={{0,3},{1,0},{2,1},{3,2},{4,7},{5,4},{6,5},{7,6},{8,11},{9,8},{10,9... | collective-permute-start | bytes 2359304 | tf_op jit(solution)/shard_map/ppermute | solution.py:265
  56.9 125.5 %copy-start.2 = (bf16[3,1,32,2048]{3,2,1,0:T(8,128)(2,1)}, bf16[3,1,32,2048]{3,2,1,0:T(8,128)(2,1)S(1)}, u32[]{:S(2)}) copy-start(bf16[3,1,32,2048]{3,2,1,0:T(8,128)(2,1)S(1)} %collective-permute-done.1.refs_6_.refs_5_.refs_3_.refs_2_) | copy-start | bytes 1179652
  56.9 25.4 %collective-permute-start.10 = (bf16[3,1,32,2048]{3,2,1,0:T(8,128)(2,1)S(1)}, bf16[3,1,32,2048]{3,2,1,0:T(8,128)(2,1)S(1)}, u32[]{:S(2)}, u32[]{:S(2)}) collective-permute-start(bf16[3,1,32,2048]{3,2,1,0:T(8,128)(2,1)S(1)} %get-tuple-element.67), channel_id=1, source_target_pairs={{0,1},{1,2},{2,3},{3,0},{4,5},{5,6},{6,7},{7,4},{8,9},{9,10},{10,1... | collective-permute-start | bytes 1179656 | tf_op jit(solution)/shard_map/ppermute | solution.py:265
  57.0 36.4 %copy-start.11 = (bf16[3,2,32,2048]{3,2,1,0:T(8,128)(2,1)}, bf16[3,2,32,2048]{3,2,1,0:T(8,128)(2,1)S(1)}, u32[]{:S(2)}) copy-start(bf16[3,2,32,2048]{3,2,1,0:T(8,128)(2,1)S(1)} %collective-permute-done.4.refs_2_) | copy-start | bytes 2359300
  57.0 46.1 %collective-permute-start.8 = (bf16[3,2,32,2048]{3,2,1,0:T(8,128)(2,1)S(1)}, bf16[3,2,32,2048]{3,2,1,0:T(8,128)(2,1)S(1)}, u32[]{:S(2)}, u32[]{:S(2)}) collective-permute-start(bf16[3,2,32,2048]{3,2,1,0:T(8,128)(2,1)S(1)} %collective-permute-done.4.refs_2_), channel_id=1, source_target_pairs={{0,4},{4,0},{1,5},{5,1},{2,6},{6,2},{3,7},{7,3},{8,12},{12,8},{9,1... | collective-permute-start | bytes 2359304 | tf_op jit(solution)/shard_map/ppermute | solution.py:265
  57.4 125.0 %copy-start.3 = (bf16[3,1,32,2048]{3,2,1,0:T(8,128)(2,1)}, bf16[3,1,32,2048]{3,2,1,0:T(8,128)(2,1)S(1)}, u32[]{:S(2)}) copy-start(bf16[3,1,32,2048]{3,2,1,0:T(8,128)(2,1)S(1)} %collective-permute-done.2.refs_7_.refs_6_.refs_4_.refs_3_) | copy-start | bytes 1179652
  57.4 33.1 %collective-permute-start.11 = (bf16[3,1,32,2048]{3,2,1,0:T(8,128)(2,1)S(1)}, bf16[3,1,32,2048]{3,2,1,0:T(8,128)(2,1)S(1)}, u32[]{:S(2)}, u32[]{:S(2)}) collective-permute-start(bf16[3,1,32,2048]{3,2,1,0:T(8,128)(2,1)S(1)} %get-tuple-element.68), channel_id=1, source_target_pairs={{0,2},{1,3},{2,0},{3,1},{4,6},{5,7},{6,4},{7,5},{8,10},{9,11},{10,... | collective-permute-start | bytes 1179656 | tf_op jit(solution)/shard_map/ppermute | solution.py:265
  82.4 11.0 %collective-permute-start.12 = (bf16[3,1,32,2048]{3,2,1,0:T(8,128)(2,1)S(1)}, bf16[3,1,32,2048]{3,2,1,0:T(8,128)(2,1)S(1)}, u32[]{:S(2)}, u32[]{:S(2)}) collective-permute-start(bf16[3,1,32,2048]{3,2,1,0:T(8,128)(2,1)S(1)} %get-tuple-element.69), channel_id=1, source_target_pairs={{0,3},{1,0},{2,1},{3,2},{4,7},{5,4},{6,5},{7,6},{8,11},{9,8},{10,9... | collective-permute-start | bytes 1179656 | tf_op jit(solution)/shard_map/ppermute | solution.py:265
  90.5 46.1 %collective-permute-start.6 = (bf16[3,2,32,2048]{3,2,1,0:T(8,128)(2,1)}, bf16[3,2,32,2048]{3,2,1,0:T(8,128)(2,1)}, u32[]{:S(2)}, u32[]{:S(2)}) collective-permute-start(bf16[3,2,32,2048]{3,2,1,0:T(8,128)(2,1)} %get-tuple-element.61.refs_0_), channel_id=1, source_target_pairs={{0,4},{4,0},{1,5},{5,1},{2,6},{6,2},{3,7},{7,3},{8,12},{12,8},{9,1... | collective-permute-start | bytes 2359304 | tf_op jit(solution)/shard_map/ppermute | solution.py:265
  90.9 45.9 %collective-permute-start.7 = (bf16[3,2,32,2048]{3,2,1,0:T(8,128)(2,1)}, bf16[3,2,32,2048]{3,2,1,0:T(8,128)(2,1)}, u32[]{:S(2)}, u32[]{:S(2)}) collective-permute-start(bf16[3,2,32,2048]{3,2,1,0:T(8,128)(2,1)} %collective-permute-done.3.refs_1_), channel_id=1, source_target_pairs={{0,4},{4,0},{1,5},{5,1},{2,6},{6,2},{3,7},{7,3},{8,12},{12,8},{9,1... | collective-permute-start | bytes 2359304 | tf_op jit(solution)/shard_map/ppermute | solution.py:265
  92.0 61.7 %collective-permute-start.9 = (bf16[3,2,32,2048]{3,2,1,0:T(8,128)(2,1)}, bf16[3,2,32,2048]{3,2,1,0:T(8,128)(2,1)}, u32[]{:S(2)}, u32[]{:S(2)}) collective-permute-start(bf16[3,2,32,2048]{3,2,1,0:T(8,128)(2,1)} %collective-permute-done.5.refs_3_), channel_id=1, source_target_pairs={{0,4},{4,0},{1,5},{5,1},{2,6},{6,2},{3,7},{7,3},{8,12},{12,8},{9,1... | collective-permute-start | bytes 2359304 | tf_op jit(solution)/shard_map/ppermute | solution.py:265
  103.1 0.9 copy-start.12
  103.9 66.6 %collective-permute-start.13 = (bf16[6,1,32,2048]{3,2,1,0:T(8,128)(2,1)}, bf16[6,1,32,2048]{3,2,1,0:T(8,128)(2,1)}, u32[]{:S(2)}, u32[]{:S(2)}) collective-permute-start(bf16[6,1,32,2048]{3,2,1,0:T(8,128)(2,1)} %pad_maximum_fusion), channel_id=1, source_target_pairs={{0,4},{4,0},{1,5},{5,1},{2,6},{6,2},{3,7},{7,3},{8,12},{12,8},{9,1... | collective-permute-start | bytes 2359304 | tf_op jit(solution)/shard_map/ppermute | solution.py:265
  134.5 2.1 copy-start.4
  157.2 24.8 %all-to-all-start.1 = ((f32[16,2,3,2,8,128]{5,4,3,2,1,0:T(8,128)}), f32[16,2,3,2,8,128]{5,4,3,2,1,0:T(8,128)S(1)}, u32[]{:S(2)}, u32[]{:S(2)}) async-start(f32[16,2,3,2,8,128]{5,4,3,2,1,0:T(8,128)} %tied_terms.5), calls=%async_computation.1 | async-start | bytes 1572864 | tf_op jit(solution)/shard_map/all_to_all | solution.py:269
  182.0 3.0 %collective-permute-start.14 = (f32[2,3,2,8,128]{4,3,2,1,0:T(8,128)S(1)}, f32[2,3,2,8,128]{4,3,2,1,0:T(8,128)S(1)}, u32[]{:S(2)}, u32[]{:S(2)}) collective-permute-start(f32[2,3,2,8,128]{4,3,2,1,0:T(8,128)S(1)} %reduce_sum.27), channel_id=1, source_target_pairs={{0,4},{4,0},{1,5},{5,1},{2,6},{6,2},{3,7},{7,3},{8,12},{12,8},{9,1... | collective-permute-start | bytes 147464 | tf_op jit(solution)/shard_map/ppermute | solution.py:265
  186.7 25.8 %collective-permute-start.16 = (bf16[6,1,32,2048]{3,2,1,0:T(8,128)(2,1)S(1)}, bf16[6,1,32,2048]{3,2,1,0:T(8,128)(2,1)}, u32[]{:S(2)}, u32[]{:S(2)}) collective-permute-start(bf16[6,1,32,2048]{3,2,1,0:T(8,128)(2,1)S(1)} %pad_maximum_fusion.1), channel_id=1, source_target_pairs={{0,4},{4,0},{1,5},{5,1},{2,6},{6,2},{3,7},{7,3},{8,12},{12,8},{9,1... | collective-permute-start | bytes 2359304 | tf_op jit(solution)/shard_map/ppermute | solution.py:265
  212.5 61.9 %all-to-all-start.3 = ((bf16[16,6,32,768]{3,2,1,0:T(8,128)(2,1)}), bf16[16,6,32,768]{3,2,1,0:T(8,128)(2,1)}, u32[]{:S(2)}, u32[]{:S(2)}) async-start(bf16[16,6,32,768]{3,2,1,0:T(8,128)(2,1)} %copy-done.4), calls=%async_computation.3 | async-start | bytes 9437184 | tf_op jit(solution)/shard_map/all_to_all | solution.py:269
  223.1 18.9 %collective-permute-start.15 = (bf16[3,1,32,2048]{3,2,1,0:T(8,128)(2,1)}, bf16[3,1,32,2048]{3,2,1,0:T(8,128)(2,1)S(1)}, u32[]{:S(2)}, u32[]{:S(2)}) collective-permute-start(bf16[3,1,32,2048]{3,2,1,0:T(8,128)(2,1)} %get-tuple-element.77), channel_id=1, source_target_pairs={{0,3},{1,0},{2,1},{3,2},{4,7},{5,4},{6,5},{7,6},{8,11},{9,8},{10,9... | collective-permute-start | bytes 1179656 | tf_op jit(solution)/shard_map/ppermute | solution.py:265
  225.7 20.8 %collective-permute-start.23 = (bf16[3,1,32,2048]{3,2,1,0:T(8,128)(2,1)}, bf16[3,1,32,2048]{3,2,1,0:T(8,128)(2,1)S(1)}, u32[]{:S(2)}, u32[]{:S(2)}) collective-permute-start(bf16[3,1,32,2048]{3,2,1,0:T(8,128)(2,1)} %get-tuple-element.100), channel_id=1, source_target_pairs={{0,2},{1,3},{2,0},{3,1},{4,6},{5,7},{6,4},{7,5},{8,10},{9,11},{10,... | collective-permute-start | bytes 1179656 | tf_op jit(solution)/shard_map/ppermute | solution.py:265
  226.2 24.3 %collective-permute-start.24 = (bf16[3,1,32,2048]{3,2,1,0:T(8,128)(2,1)}, bf16[3,1,32,2048]{3,2,1,0:T(8,128)(2,1)S(1)}, u32[]{:S(2)}, u32[]{:S(2)}) collective-permute-start(bf16[3,1,32,2048]{3,2,1,0:T(8,128)(2,1)} %get-tuple-element.101), channel_id=1, source_target_pairs={{0,1},{1,2},{2,3},{3,0},{4,5},{5,6},{6,7},{7,4},{8,9},{9,10},{10,1... | collective-permute-start | bytes 1179656 | tf_op jit(solution)/shard_map/ppermute | solution.py:265
  226.8 32.0 %collective-permute-start.20 = (bf16[3,1,32,2048]{3,2,1,0:T(8,128)(2,1)}, bf16[3,1,32,2048]{3,2,1,0:T(8,128)(2,1)S(1)}, u32[]{:S(2)}, u32[]{:S(2)}) collective-permute-start(bf16[3,1,32,2048]{3,2,1,0:T(8,128)(2,1)} %get-tuple-element.96), channel_id=1, source_target_pairs={{0,3},{1,0},{2,1},{3,2},{4,7},{5,4},{6,5},{7,6},{8,11},{9,8},{10,9... | collective-permute-start | bytes 1179656 | tf_op jit(solution)/shard_map/ppermute | solution.py:265
  228.9 32.5 %collective-permute-start.21 = (bf16[3,1,32,2048]{3,2,1,0:T(8,128)(2,1)}, bf16[3,1,32,2048]{3,2,1,0:T(8,128)(2,1)S(1)}, u32[]{:S(2)}, u32[]{:S(2)}) collective-permute-start(bf16[3,1,32,2048]{3,2,1,0:T(8,128)(2,1)} %get-tuple-element.97), channel_id=1, source_target_pairs={{0,2},{1,3},{2,0},{3,1},{4,6},{5,7},{6,4},{7,5},{8,10},{9,11},{10,... | collective-permute-start | bytes 1179656 | tf_op jit(solution)/shard_map/ppermute | solution.py:265
  242.0 16.8 %copy-start.9 = (bf16[3,1,32,2048]{3,2,1,0:T(8,128)(2,1)S(1)}, bf16[3,1,32,2048]{3,2,1,0:T(8,128)(2,1)}, u32[]{:S(2)}) copy-start(bf16[3,1,32,2048]{3,2,1,0:T(8,128)(2,1)} %get-tuple-element.99.refs_0_) | copy-start | bytes 1179652
  242.0 22.4 %collective-permute-start.22 = (bf16[3,1,32,2048]{3,2,1,0:T(8,128)(2,1)}, bf16[3,1,32,2048]{3,2,1,0:T(8,128)(2,1)S(1)}, u32[]{:S(2)}, u32[]{:S(2)}) collective-permute-start(bf16[3,1,32,2048]{3,2,1,0:T(8,128)(2,1)} %get-tuple-element.98), channel_id=1, source_target_pairs={{0,1},{1,2},{2,3},{3,0},{4,5},{5,6},{6,7},{7,4},{8,9},{9,10},{10,1... | collective-permute-start | bytes 1179656 | tf_op jit(solution)/shard_map/ppermute | solution.py:265
  246.5 32.6 %collective-permute-start.17 = (bf16[3,1,32,2048]{3,2,1,0:T(8,128)(2,1)}, bf16[3,1,32,2048]{3,2,1,0:T(8,128)(2,1)S(1)}, u32[]{:S(2)}, u32[]{:S(2)}) collective-permute-start(bf16[3,1,32,2048]{3,2,1,0:T(8,128)(2,1)} %get-tuple-element.84), channel_id=1, source_target_pairs={{0,3},{1,0},{2,1},{3,2},{4,7},{5,4},{6,5},{7,6},{8,11},{9,8},{10,9... | collective-permute-start | bytes 1179656 | tf_op jit(solution)/shard_map/ppermute | solution.py:265
  250.5 28.6 %collective-permute-start.18 = (bf16[3,1,32,2048]{3,2,1,0:T(8,128)(2,1)}, bf16[3,1,32,2048]{3,2,1,0:T(8,128)(2,1)S(1)}, u32[]{:S(2)}, u32[]{:S(2)}) collective-permute-start(bf16[3,1,32,2048]{3,2,1,0:T(8,128)(2,1)} %get-tuple-element.85), channel_id=1, source_target_pairs={{0,2},{1,3},{2,0},{3,1},{4,6},{5,7},{6,4},{7,5},{8,10},{9,11},{10,... | collective-permute-start | bytes 1179656 | tf_op jit(solution)/shard_map/ppermute | solution.py:265
  258.8 21.6 %collective-permute-start.19 = (bf16[3,1,32,2048]{3,2,1,0:T(8,128)(2,1)}, bf16[3,1,32,2048]{3,2,1,0:T(8,128)(2,1)S(1)}, u32[]{:S(2)}, u32[]{:S(2)}) collective-permute-start(bf16[3,1,32,2048]{3,2,1,0:T(8,128)(2,1)} %get-tuple-element.86), channel_id=1, source_target_pairs={{0,1},{1,2},{2,3},{3,0},{4,5},{5,6},{6,7},{7,4},{8,9},{9,10},{10,1... | collective-permute-start | bytes 1179656 | tf_op jit(solution)/shard_map/ppermute | solution.py:265
  258.8 5.6 %copy-start.8 = (bf16[3,1,32,2048]{3,2,1,0:T(8,128)(2,1)S(1)}, bf16[3,1,32,2048]{3,2,1,0:T(8,128)(2,1)}, u32[]{:S(2)}) copy-start(bf16[3,1,32,2048]{3,2,1,0:T(8,128)(2,1)} %get-tuple-element.95.refs_0_) | copy-start | bytes 1179652
  267.0 13.5 %copy-start.10 = (bf16[3,1,32,2048]{3,2,1,0:T(8,128)(2,1)S(1)}, bf16[3,1,32,2048]{3,2,1,0:T(8,128)(2,1)}, u32[]{:S(2)}) copy-start(bf16[3,1,32,2048]{3,2,1,0:T(8,128)(2,1)} %get-tuple-element.91.refs_0_) | copy-start | bytes 1179652
